TPU v7x, 32 devices: a whole 2x2x4 slice. The times are simulated.
32 devices in a mesh: dom: 8 (over z, core), grp: 4 (over y, x).
Axes of the slice: x: 2, y: 2, z: 4, core: 2. Of those that a mesh axis runs over, the one named last changes fastest.
Arguments:
- node_latent: bfloat16 [32768, 128], P(('dom', 'grp')), may hold values from -6 to 6
- node_tangent: bfloat16 [32768, 128], P(('dom', 'grp')), may hold values from -6 to 6
- edge_latent: bfloat16 [131072, 128], P(('dom', 'grp')), may hold values from -6 to 6
- node_counts: int32 [32], P(('dom', 'grp')), may hold values from 512 to 1024, as said below
- edge_counts: int32 [32], P(('dom', 'grp')), may hold values from 2048 to 4096, as said below
- send_lists: int32 [32, 4, 128], P(('dom', 'grp')), may hold values from 0 to 1023, as said below
- edge_source: int32 [32, 4096], P(('dom', 'grp')), may hold values from 0 to 1535, as said below
- edge_target: int32 [32, 4096], P(('dom', 'grp')), may hold values from 0 to 1023, as said below
- coarse_owner: int32 [32, 1024], P(('dom', 'grp')), may hold values from 0 to 127
- coarse_source: int32 [1024, 8], P(('dom', 'grp')), may hold values from 0 to 383, as said below
- edge_first: bfloat16 [384, 128], replicated, may hold values from -0.3125 to 0.3125
- edge_second: bfloat16 [128, 128], replicated, may hold values from -0.5 to 0.5
- node_first: bfloat16 [256, 128], replicated, may hold values from -0.375 to 0.375
- node_second: bfloat16 [128, 128], replicated, may hold values from -0.5 to 0.5
- message_first: bfloat16 [256, 128], replicated, may hold values from -0.375 to 0.375
- message_second: bfloat16 [128, 128], replicated, may hold values from -0.5 to 0.5
- coarse_first: bfloat16 [256, 128], replicated, may hold values from -0.375 to 0.375
- coarse_second: bfloat16 [128, 128], replicated, may hold values from -0.5 to 0.5
- prolong_first: bfloat16 [256, 128], replicated, may hold values from -0.375 to 0.375
- prolong_second: bfloat16 [128, 128], replicated, may hold values from -0.5 to 0.5
Outputs:
- node_output: bfloat16 [32768, 128], P(('dom', 'grp'))
- tangent_output: bfloat16 [32768, 128], P(('dom', 'grp'))
Inputs may be any that keep to these rules, and one draw needn't show every extreme that they name: node_counts[p] is at least half of 1024; some partition has all 1024 slots valid. edge_counts[p] is at least half of 4096; some partition has all 4096 slots valid. `send_lists`: every entry is a valid node row of its own partition (below node_counts[p]). `edge_source`: every entry is either a valid node row of the partition (below node_counts[p]) or a halo row 1024 + r with r < 512. `edge_target`: every entry is a valid node row of the partition. `coarse_source`: entries below 32 * 4 name nodes of row d-1, entries from 2 * 32 * 4 on name nodes of row d+1, the others nodes of row d itself.
All inputs are finite; a program needn't handle non-finite values.
Results may differ from a plain program's by a relative error of at most 0.012.
Values may be sent and summed in bfloat16 or wider, within the bound.
No kernel may reach another device: no remote copies, remote signals or barrier semaphores. Data moves between devices by JAX's collectives and lax.ppermute only.
A program may use at most 64 MiB of HBM per device.

v0:
```python
import math

import jax
import jax.numpy as jnp
from jax import lax
from jax.sharding import PartitionSpec as P


def from_behind(x, axis, by):
    size = lax.axis_size(axis)
    pairs = [(i, i + by) for i in range(size) if 0 <= i + by < size]
    return lax.ppermute(x, axis, pairs)


def extended(x, sides, width):
    for axis, dim in sides:
        size, length = (lax.axis_size(axis), x.shape[dim])
        up = [(i, (i + 1) % size) for i in range(size - 1)]
        down = [(j, i) for i, j in up]
        last = lax.slice_in_dim(x, length - width, length, axis=dim)
        first = lax.slice_in_dim(x, 0, width, axis=dim)
        before = lax.ppermute(last, axis, up)
        after = lax.ppermute(first, axis, down)
        x = jnp.concatenate([before, x, after], axis=dim)
    return x


def layer_norm(value):
    centred = value - jnp.mean(value, axis=-1, keepdims=True)
    spread = jnp.mean(centred * centred, axis=-1, keepdims=True)
    return centred * lax.rsqrt(spread + 1e-05)


def perceptron(inputs, first, second):
    hidden = jax.nn.silu(jnp.dot(inputs, first, preferred_element_type=jnp.float32)).astype(
        jnp.bfloat16
    )
    return jnp.dot(hidden, second, preferred_element_type=jnp.float32)


def edge_update(edges, source, target, first, second):
    joined = jnp.concatenate([edges, source, target], axis=-1)
    return (edges.astype(jnp.float32) + layer_norm(perceptron(joined, first, second))).astype(
        jnp.bfloat16
    )


def node_update(nodes, other, first, second):
    joined = jnp.concatenate([nodes, other], axis=-1)
    return (nodes.astype(jnp.float32) + layer_norm(perceptron(joined, first, second))).astype(
        jnp.bfloat16
    )


def coarse_update(table, sources, mine, weights):
    message_first, message_second, coarse_first, coarse_second = weights
    senders = table[sources]
    receivers = jnp.broadcast_to(mine[:, None, :], senders.shape)
    joined = jnp.concatenate([senders, receivers], axis=-1).reshape(-1, 2 * senders.shape[-1])
    terms = perceptron(joined, message_first, message_second).reshape(senders.shape)
    message = jnp.sum(terms, axis=1).astype(jnp.bfloat16)
    joined = jnp.concatenate([mine, message], axis=-1)
    return layer_norm(perceptron(joined, coarse_first, coarse_second)).astype(jnp.bfloat16)


def select_rows(indices, count, values):
    selector = (indices[:, None] == jnp.arange(count)[None, :]).astype(jnp.bfloat16)
    return jnp.dot(selector, values, preferred_element_type=jnp.float32).astype(jnp.bfloat16)


def per_device(
    node_latent,
    node_tangent,
    edge_latent,
    node_counts,
    edge_counts,
    send_lists,
    edge_source,
    edge_target,
    coarse_owner,
    coarse_source,
    edge_first,
    edge_second,
    node_first,
    node_second,
    message_first,
    message_second,
    coarse_first,
    coarse_second,
    prolong_first,
    prolong_second,
):
    width = node_latent.shape[1]
    slots = node_latent.shape[0]
    paired = jnp.concatenate([node_latent, node_tangent], axis=1)
    rim_rows = send_lists.shape[2]
    sent = select_rows(send_lists[0].reshape(-1), slots, paired).reshape(4, rim_rows, 2 * width)
    received = []
    for block, offset in ((0, 1), (1, -1)):
        received.append(from_behind(sent[block], "dom", offset))
    for block, offset in ((2, 1), (3, -1)):
        received.append(from_behind(sent[block], "grp", offset))
    table = jnp.concatenate([paired] + received, axis=0)
    table_rows = table.shape[0]
    edge_slots = edge_latent.shape[0]
    block_rows = math.gcd(edge_slots, 512)
    block_count = edge_slots // block_rows
    edge_blocks = edge_latent.reshape(block_count, block_rows, width)
    source_blocks = edge_source[0].reshape(block_count, block_rows)
    target_blocks = edge_target[0].reshape(block_count, block_rows)
    edge_total = edge_counts[0]

    def edge_block(carry, items):
        edges, source, target, number = items
        sender = select_rows(source, table_rows, table)
        target_pick = (target[:, None] == jnp.arange(slots)[None, :]).astype(jnp.bfloat16)
        receiver = jnp.dot(target_pick, paired, preferred_element_type=jnp.float32).astype(
            jnp.bfloat16
        )
        edge_new, edge_tan = jax.jvp(
            lambda a, b, c: edge_update(a, b, c, edge_first, edge_second),
            (edges, sender[:, :width], receiver[:, :width]),
            (jnp.zeros_like(edges), sender[:, width:], receiver[:, width:]),
        )
        live = (number * block_rows + jnp.arange(block_rows) < edge_total)[:, None]
        pair = jnp.concatenate([edge_new, edge_tan], axis=1)
        pair = jnp.where(live, pair, jnp.zeros_like(pair))
        added = jnp.einsum("es,ef->sf", target_pick, pair, preferred_element_type=jnp.float32)
        return (carry + added, None)

    start_sum = jnp.zeros((slots, 2 * width), jnp.float32)
    agg_pair, _ = lax.scan(
        edge_block,
        start_sum,
        (edge_blocks, source_blocks, target_blocks, jnp.arange(block_count, dtype=jnp.int32)),
    )
    agg_pair = agg_pair.astype(jnp.bfloat16)
    agg = agg_pair[:, :width]
    agg_tan = agg_pair[:, width:]
    first, first_tan = jax.jvp(
        lambda a, b: node_update(a, b, node_first, node_second),
        (node_latent, agg),
        (node_tangent, agg_tan),
    )
    first_pair = jnp.concatenate([first, first_tan], axis=1)
    valid = (jnp.arange(slots) < node_counts[0])[:, None]
    masked = jnp.where(valid, first_pair, jnp.zeros_like(first_pair))
    owner = coarse_owner[0]
    weights = (message_first, message_second, coarse_first, coarse_second)
    owned = coarse_source.shape[0]
    rows = jnp.arange(lax.axis_size("grp") * owned)
    selector = (owner[None, :] == rows[:, None]).astype(jnp.bfloat16)
    own_sum = lax.psum_scatter(
        jnp.dot(selector, masked, preferred_element_type=jnp.float32).astype(jnp.bfloat16),
        "grp",
        scatter_dimension=0,
        tiled=True,
    )
    coarse = lax.all_gather(own_sum, "grp", axis=0, tiled=True)
    row_nodes = coarse.shape[0]
    three_rows = extended(coarse[None], (("dom", 0),), 1).reshape(3 * row_nodes, 2 * width)
    updated, updated_tan = jax.jvp(
        lambda a, b: coarse_update(a, coarse_source, b, weights),
        (three_rows[:, :width], own_sum[:, :width]),
        (three_rows[:, width:], own_sum[:, width:]),
    )
    updated_pair = jnp.concatenate([updated, updated_tan], axis=1)
    piece = lax.all_gather(updated_pair, "grp", axis=0, tiled=True)
    rows = jnp.arange(piece.shape[0])
    selector = (owner[:, None] == rows[None, :]).astype(jnp.bfloat16)
    brought = jnp.dot(selector, piece, preferred_element_type=jnp.float32).astype(jnp.bfloat16)
    final, final_tan = jax.jvp(
        lambda a, b: node_update(a, b, prolong_first, prolong_second),
        (first, brought[:, :width]),
        (first_tan, brought[:, width:]),
    )
    node_output = jnp.where(valid, final, jnp.zeros_like(final))
    tangent_output = jnp.where(valid, final_tan, jnp.zeros_like(final_tan))
    return (node_output, tangent_output)


def solution(mesh):
    in_specs = (
        P(("dom", "grp"), None),
        P(("dom", "grp"), None),
        P(("dom", "grp"), None),
        P(("dom", "grp")),
        P(("dom", "grp")),
        P(("dom", "grp"), None, None),
        P(("dom", "grp"), None),
        P(("dom", "grp"), None),
        P(("dom", "grp"), None),
        P(("dom", "grp"), None),
        P(),
        P(),
        P(),
        P(),
        P(),
        P(),
        P(),
        P(),
        P(),
        P(),
    )
    out_specs = (P(("dom", "grp"), None), P(("dom", "grp"), None))
    return jax.shard_map(
        per_device, mesh=mesh, in_specs=in_specs, out_specs=out_specs, check_vma=False
    )
```

profile of v0, /device:TPU:1, one launch (start us, length us, event | category | flops | bytes accessed | tf_op | source)
XLA Modules:
  0.0 189.5 jit_solution(17610818794056265365)
XLA Ops:
  7.2 1.7 constant_dynamic-update-slice_fusion.1
  9.0 1.8 constant_dynamic-update-slice_fusion
  11.3 4.6 %collective-permute-start = (bf16[128,256]{1,0:T(8,128)(2,1)S(1)}, bf16[128,256]{1,0:T(8,128)(2,1)S(1)}, u32[]{:S(2)}, u32[]{:S(2)}) collective-permute-start(bf16[128,256]{1,0:T(8,128)(2,1)S(1)} %get-tuple-element.166), channel_id=1, source_target_pairs={{0,4},{4,8},{8,12},{12,16},{16,20},{20,24},{24,28},{1,5},{5,9},{9,... | collective-permute-start | bytes 196616 | tf_op jit(solution)/shard_map/ppermute | solution.py:12
  15.9 1.9 %collective-permute-start.1 = (bf16[128,256]{1,0:T(8,128)(2,1)S(1)}, bf16[128,256]{1,0:T(8,128)(2,1)S(1)}, u32[]{:S(2)}, u32[]{:S(2)}) collective-permute-start(bf16[128,256]{1,0:T(8,128)(2,1)S(1)} %get-tuple-element.165), channel_id=1, source_target_pairs={{4,0},{8,4},{12,8},{16,12},{20,16},{24,20},{28,24},{5,1},{9,5},{13... | collective-permute-start | bytes 196616 | tf_op jit(solution)/shard_map/ppermute | solution.py:12
  17.9 3.1 %collective-permute-start.2 = (bf16[128,256]{1,0:T(8,128)(2,1)S(1)}, bf16[128,256]{1,0:T(8,128)(2,1)S(1)}, u32[]{:S(2)}, u32[]{:S(2)}) collective-permute-start(bf16[128,256]{1,0:T(8,128)(2,1)S(1)} %get-tuple-element.164), channel_id=1, source_target_pairs={{0,1},{1,2},{2,3},{4,5},{5,6},{6,7},{8,9},{9,10},{10,11},{12,13},{... | collective-permute-start | bytes 196616 | tf_op jit(solution)/shard_map/ppermute | solution.py:12
  21.0 1.3 collective-permute-start.3
  27.7 94.1 %while.11 = (s32[]{:T(128)}, f32[1024,256]{1,0:T(8,128)S(1)}, s32[8,512]{1,0:T(8,128)S(1)}, s32[8]{0:T(128)S(1)}, s32[]{:T(128)}, /*index=5*/bf16[8,512,128]{2,1...) while((s32[]{:T(128)}, f32[1024,256]{1,0:T(8,128)S(1)}, ...), condition=%wide.region_5.6_spmd.clone, body=%wide.region_0.5_spmd.clone.sunk | while | flops 1082133504 | bytes 9884903 | solution.py:132
  28.5 2.1 %fusion.226 = bf16[512,256]{0,1:T(8,128)(2,1)S(1)} fusion(bf16[1536,256]{1,0:T(8,128)(2,1)} %get-tuple-element.335, s32[512]{0:T(512)S(1)} %bitcast.89), kind=kOutput, calls=%fused_computation.10.clone.1 | convolution fusion | flops 403570688 | bytes 1050624 | tf_op jit(solution)/shard_map/while/body/eval_jaxpr/dot_general | solution.py:68
  31.6 2.0 %fusion.228 = f32[512,128]{1,0:T(8,128)} fusion(bf16[384,128]{1,0:T(8,128)(2,1)} %get-tuple-element.337, bf16[512,128]{0,1:T(8,128)(2,1)S(1)} %get-tuple-element.281, bf16[512,128]{0,1:T(8,128)(2,1)S(1)} %get-tuple-element.283, bf16[512,128]{0,1:T(8,128)(2,1)S(1)} %bitcast.79), kind=kOutput, calls=%fused_computation.13.clone.1 | convolution fusion | flops 51511296 | bytes 753664 | tf_op jit(solution)/shard_map/while/body/eval_jaxpr/jvp()/dot_general | solution.py:35
  33.6 1.5 fusion.230
  35.2 1.2 fusion.229
  38.5 1.0 convolution_add_fusion.2
  40.2 2.1 %fusion.226 = bf16[512,256]{0,1:T(8,128)(2,1)S(1)} fusion(bf16[1536,256]{1,0:T(8,128)(2,1)} %get-tuple-element.335, s32[512]{0:T(512)S(1)} %bitcast.89), kind=kOutput, calls=%fused_computation.10.clone.1 | convolution fusion | flops 403570688 | bytes 1050624 | tf_op jit(solution)/shard_map/while/body/eval_jaxpr/dot_general | solution.py:68
  43.4 2.0 %fusion.228 = f32[512,128]{1,0:T(8,128)} fusion(bf16[384,128]{1,0:T(8,128)(2,1)} %get-tuple-element.337, bf16[512,128]{0,1:T(8,128)(2,1)S(1)} %get-tuple-element.281, bf16[512,128]{0,1:T(8,128)(2,1)S(1)} %get-tuple-element.283, bf16[512,128]{0,1:T(8,128)(2,1)S(1)} %bitcast.79), kind=kOutput, calls=%fused_computation.13.clone.1 | convolution fusion | flops 51511296 | bytes 753664 | tf_op jit(solution)/shard_map/while/body/eval_jaxpr/jvp()/dot_general | solution.py:35
  45.4 1.5 fusion.230
  46.9 1.2 fusion.229
  52.0 2.1 %fusion.226 = bf16[512,256]{0,1:T(8,128)(2,1)S(1)} fusion(bf16[1536,256]{1,0:T(8,128)(2,1)} %get-tuple-element.335, s32[512]{0:T(512)S(1)} %bitcast.89), kind=kOutput, calls=%fused_computation.10.clone.1 | convolution fusion | flops 403570688 | bytes 1050624 | tf_op jit(solution)/shard_map/while/body/eval_jaxpr/dot_general | solution.py:68
  55.1 2.0 %fusion.228 = f32[512,128]{1,0:T(8,128)} fusion(bf16[384,128]{1,0:T(8,128)(2,1)} %get-tuple-element.337, bf16[512,128]{0,1:T(8,128)(2,1)S(1)} %get-tuple-element.281, bf16[512,128]{0,1:T(8,128)(2,1)S(1)} %get-tuple-element.283, bf16[512,128]{0,1:T(8,128)(2,1)S(1)} %bitcast.79), kind=kOutput, calls=%fused_computation.13.clone.1 | convolution fusion | flops 51511296 | bytes 753664 | tf_op jit(solution)/shard_map/while/body/eval_jaxpr/jvp()/dot_general | solution.py:35
  57.1 1.5 fusion.230
  58.7 1.2 fusion.229
  62.0 1.0 convolution_add_fusion.2
  63.8 2.1 %fusion.226 = bf16[512,256]{0,1:T(8,128)(2,1)S(1)} fusion(bf16[1536,256]{1,0:T(8,128)(2,1)} %get-tuple-element.335, s32[512]{0:T(512)S(1)} %bitcast.89), kind=kOutput, calls=%fused_computation.10.clone.1 | convolution fusion | flops 403570688 | bytes 1050624 | tf_op jit(solution)/shard_map/while/body/eval_jaxpr/dot_general | solution.py:68
  66.9 2.0 %fusion.228 = f32[512,128]{1,0:T(8,128)} fusion(bf16[384,128]{1,0:T(8,128)(2,1)} %get-tuple-element.337, bf16[512,128]{0,1:T(8,128)(2,1)S(1)} %get-tuple-element.281, bf16[512,128]{0,1:T(8,128)(2,1)S(1)} %get-tuple-element.283, bf16[512,128]{0,1:T(8,128)(2,1)S(1)} %bitcast.79), kind=kOutput, calls=%fused_computation.13.clone.1 | convolution fusion | flops 51511296 | bytes 753664 | tf_op jit(solution)/shard_map/while/body/eval_jaxpr/jvp()/dot_general | solution.py:35
  68.9 1.5 fusion.230
  70.4 1.2 fusion.229
  73.8 1.0 convolution_add_fusion.2
  75.5 2.1 %fusion.226 = bf16[512,256]{0,1:T(8,128)(2,1)S(1)} fusion(bf16[1536,256]{1,0:T(8,128)(2,1)} %get-tuple-element.335, s32[512]{0:T(512)S(1)} %bitcast.89), kind=kOutput, calls=%fused_computation.10.clone.1 | convolution fusion | flops 403570688 | bytes 1050624 | tf_op jit(solution)/shard_map/while/body/eval_jaxpr/dot_general | solution.py:68
  78.7 2.0 %fusion.228 = f32[512,128]{1,0:T(8,128)} fusion(bf16[384,128]{1,0:T(8,128)(2,1)} %get-tuple-element.337, bf16[512,128]{0,1:T(8,128)(2,1)S(1)} %get-tuple-element.281, bf16[512,128]{0,1:T(8,128)(2,1)S(1)} %get-tuple-element.283, bf16[512,128]{0,1:T(8,128)(2,1)S(1)} %bitcast.79), kind=kOutput, calls=%fused_computation.13.clone.1 | convolution fusion | flops 51511296 | bytes 753664 | tf_op jit(solution)/shard_map/while/body/eval_jaxpr/jvp()/dot_general | solution.py:35
  80.7 1.5 fusion.230
  82.2 1.2 fusion.229
  87.3 2.1 %fusion.226 = bf16[512,256]{0,1:T(8,128)(2,1)S(1)} fusion(bf16[1536,256]{1,0:T(8,128)(2,1)} %get-tuple-element.335, s32[512]{0:T(512)S(1)} %bitcast.89), kind=kOutput, calls=%fused_computation.10.clone.1 | convolution fusion | flops 403570688 | bytes 1050624 | tf_op jit(solution)/shard_map/while/body/eval_jaxpr/dot_general | solution.py:68
  90.4 2.0 %fusion.228 = f32[512,128]{1,0:T(8,128)} fusion(bf16[384,128]{1,0:T(8,128)(2,1)} %get-tuple-element.337, bf16[512,128]{0,1:T(8,128)(2,1)S(1)} %get-tuple-element.281, bf16[512,128]{0,1:T(8,128)(2,1)S(1)} %get-tuple-element.283, bf16[512,128]{0,1:T(8,128)(2,1)S(1)} %bitcast.79), kind=kOutput, calls=%fused_computation.13.clone.1 | convolution fusion | flops 51511296 | bytes 753664 | tf_op jit(solution)/shard_map/while/body/eval_jaxpr/jvp()/dot_general | solution.py:35
  92.4 1.5 fusion.230
  94.0 1.2 fusion.229
  99.1 2.1 %fusion.226 = bf16[512,256]{0,1:T(8,128)(2,1)S(1)} fusion(bf16[1536,256]{1,0:T(8,128)(2,1)} %get-tuple-element.335, s32[512]{0:T(512)S(1)} %bitcast.89), kind=kOutput, calls=%fused_computation.10.clone.1 | convolution fusion | flops 403570688 | bytes 1050624 | tf_op jit(solution)/shard_map/while/body/eval_jaxpr/dot_general | solution.py:68
  102.2 2.0 %fusion.228 = f32[512,128]{1,0:T(8,128)} fusion(bf16[384,128]{1,0:T(8,128)(2,1)} %get-tuple-element.337, bf16[512,128]{0,1:T(8,128)(2,1)S(1)} %get-tuple-element.281, bf16[512,128]{0,1:T(8,128)(2,1)S(1)} %get-tuple-element.283, bf16[512,128]{0,1:T(8,128)(2,1)S(1)} %bitcast.79), kind=kOutput, calls=%fused_computation.13.clone.1 | convolution fusion | flops 51511296 | bytes 753664 | tf_op jit(solution)/shard_map/while/body/eval_jaxpr/jvp()/dot_general | solution.py:35
  104.2 1.5 fusion.230
  105.7 1.2 fusion.229
  110.8 2.1 %fusion.226 = bf16[512,256]{0,1:T(8,128)(2,1)S(1)} fusion(bf16[1536,256]{1,0:T(8,128)(2,1)} %get-tuple-element.335, s32[512]{0:T(512)S(1)} %bitcast.89), kind=kOutput, calls=%fused_computation.10.clone.1 | convolution fusion | flops 403570688 | bytes 1050624 | tf_op jit(solution)/shard_map/while/body/eval_jaxpr/dot_general | solution.py:68
  114.0 2.0 %fusion.228 = f32[512,128]{1,0:T(8,128)} fusion(bf16[384,128]{1,0:T(8,128)(2,1)} %get-tuple-element.337, bf16[512,128]{0,1:T(8,128)(2,1)S(1)} %get-tuple-element.281, bf16[512,128]{0,1:T(8,128)(2,1)S(1)} %get-tuple-element.283, bf16[512,128]{0,1:T(8,128)(2,1)S(1)} %bitcast.79), kind=kOutput, calls=%fused_computation.13.clone.1 | convolution fusion | flops 51511296 | bytes 753664 | tf_op jit(solution)/shard_map/while/body/eval_jaxpr/jvp()/dot_general | solution.py:35
  116.0 1.5 fusion.230
  117.5 1.2 fusion.229
  125.6 25.7 %reduce-scatter.2.cloned.1.call-done = bf16[32,256]{1,0:T(8,128)(2,1)} async-done(((bf16[128,256]{1,0:T(8,128)(2,1)}), bf16[32,256]{1,0:T(8,128)(2,1)}) %reduce-scatter.2.cloned.1.call-update) | async-done | bytes 16400 | tf_op jit(solution)/shard_map/reduce_scatter | solution.py:153
  151.3 6.2 %all_gather.6 = bf16[128,256]{1,0:T(8,128)(2,1)S(1)} all-gather(bf16[32,256]{1,0:T(8,128)(2,1)} %reduce-scatter.2.cloned.1.call-done), channel_id=1, replica_groups=mesh['dom'=8,'grp'=4] {'grp'}, dimensions={0}, use_global_device_ids=true | all-gather | bytes 81920 | tf_op jit(solution)/shard_map/all_gather | solution.py:159
  157.5 6.2 %collective-permute-start.4 = (bf16[1,128,256]{2,1,0:T(8,128)(2,1)S(1)}, bf16[1,128,256]{2,1,0:T(8,128)(2,1)S(1)}, u32[]{:S(2)}, u32[]{:S(2)}) collective-permute-start(bf16[1,128,256]{2,1,0:T(8,128)(2,1)S(1)} %bitcast.83), channel_id=1, source_target_pairs={{0,4},{4,8},{8,12},{12,16},{16,20},{20,24},{24,28},{1,5},{5,9},{9,... | collective-permute-start | bytes 196616 | tf_op jit(solution)/shard_map/ppermute | solution.py:22
  163.7 1.9 %collective-permute-start.5 = (bf16[1,128,256]{2,1,0:T(8,128)(2,1)S(1)}, bf16[1,128,256]{2,1,0:T(8,128)(2,1)S(1)}, u32[]{:S(2)}, u32[]{:S(2)}) collective-permute-start(bf16[1,128,256]{2,1,0:T(8,128)(2,1)S(1)} %bitcast.84), channel_id=1, source_target_pairs={{4,0},{8,4},{12,8},{16,12},{20,16},{24,20},{28,24},{5,1},{9,5},{13... | collective-permute-start | bytes 196616 | tf_op jit(solution)/shard_map/ppermute | solution.py:23
  166.3 2.9 %collective-permute-done.5 = bf16[1,128,256]{2,1,0:T(8,128)(2,1)S(1)} collective-permute-done((bf16[1,128,256]{2,1,0:T(8,128)(2,1)S(1)}, bf16[1,128,256]{2,1,0:T(8,128)(2,1)S(1)}, u32[]{:S(2)}, u32[]{:S(2)}) %collective-permute-start.5) | collective-permute-done | bytes 65568 | tf_op jit(solution)/shard_map/ppermute | solution.py:23
  173.0 5.4 %all_gather.7 = bf16[128,256]{1,0:T(8,128)(2,1)S(1)} all-gather(bf16[32,256]{1,0:T(8,128)(2,1)S(1)} %pad_maximum_fusion.4), channel_id=1, replica_groups=mesh['dom'=8,'grp'=4] {'grp'}, dimensions={0}, use_global_device_ids=true | all-gather | bytes 81920 | tf_op jit(solution)/shard_map/all_gather | solution.py:168
  (241 shorter events, 48.2 us)
Async XLA Ops:
  7.2 114.8 %copy-start = (bf16[256,128]{1,0:T(8,128)(2,1)S(1)}, bf16[256,128]{1,0:T(8,128)(2,1)}, u32[]{:S(2)}) copy-start(bf16[256,128]{1,0:T(8,128)(2,1)} %param.34) | copy-start | bytes 196612
  7.2 3.6 %copy-start.16 = (s32[1,4,128]{2,1,0:T(4,128)S(1)}, s32[1,4,128]{2,1,0:T(4,128)}, u32[]{:S(2)}) copy-start(s32[1,4,128]{2,1,0:T(4,128)} %param.27) | copy-start | bytes 6148
  7.2 144.1 %reduce-scatter.2.cloned.1.call-start = ((), (), s32[]{:S(2)}) async-start(), calls=%async_computation.1 | async-start | bytes 81920 | tf_op jit(solution)/shard_map/reduce_scatter | solution.py:153
  10.7 11.6 %copy-start.1 = (bf16[1024,128]{1,0:T(8,128)(2,1)S(1)}, bf16[1024,128]{1,0:T(8,128)(2,1)}, u32[]{:S(2)}) copy-start(bf16[1024,128]{1,0:T(8,128)(2,1)} %param.22) | copy-start | bytes 786436
  10.7 11.7 %copy-start.2 = (bf16[1024,128]{1,0:T(8,128)(2,1)S(1)}, bf16[1024,128]{1,0:T(8,128)(2,1)}, u32[]{:S(2)}) copy-start(bf16[1024,128]{1,0:T(8,128)(2,1)} %param.23) | copy-start | bytes 786436
  11.3 11.9 %copy-start.6 = (s32[1,4096]{1,0:T(1,128)S(1)}, s32[1,4096]{1,0:T(1,128)}, u32[]{:S(2)}) copy-start(s32[1,4096]{1,0:T(1,128)} %param.29) | copy-start | bytes 49156
  11.3 12.6 %copy-start.7 = (s32[1,4096]{1,0:T(1,128)S(1)}, s32[1,4096]{1,0:T(1,128)}, u32[]{:S(2)}) copy-start(s32[1,4096]{1,0:T(1,128)} %param.28) | copy-start | bytes 49156
  11.3 16.5 %copy-start.11 = (bf16[128,128]{1,0:T(8,128)(2,1)S(1)}, bf16[128,128]{1,0:T(8,128)(2,1)}, u32[]{:S(2)}) copy-start(bf16[128,128]{1,0:T(8,128)(2,1)} %param.33) | copy-start | bytes 98308
  11.3 13.9 %collective-permute-start = (bf16[128,256]{1,0:T(8,128)(2,1)S(1)}, bf16[128,256]{1,0:T(8,128)(2,1)S(1)}, u32[]{:S(2)}, u32[]{:S(2)}) collective-permute-start(bf16[128,256]{1,0:T(8,128)(2,1)S(1)} %get-tuple-element.166), channel_id=1, source_target_pairs={{0,4},{4,8},{8,12},{12,16},{16,20},{20,24},{24,28},{1,5},{5,9},{9,... | collective-permute-start | bytes 196616 | tf_op jit(solution)/shard_map/ppermute | solution.py:12
  15.9 9.9 %collective-permute-start.1 = (bf16[128,256]{1,0:T(8,128)(2,1)S(1)}, bf16[128,256]{1,0:T(8,128)(2,1)S(1)}, u32[]{:S(2)}, u32[]{:S(2)}) collective-permute-start(bf16[128,256]{1,0:T(8,128)(2,1)S(1)} %get-tuple-element.165), channel_id=1, source_target_pairs={{4,0},{8,4},{12,8},{16,12},{20,16},{24,20},{28,24},{5,1},{9,5},{13... | collective-permute-start | bytes 196616 | tf_op jit(solution)/shard_map/ppermute | solution.py:12
  17.9 8.6 %collective-permute-start.2 = (bf16[128,256]{1,0:T(8,128)(2,1)S(1)}, bf16[128,256]{1,0:T(8,128)(2,1)S(1)}, u32[]{:S(2)}, u32[]{:S(2)}) collective-permute-start(bf16[128,256]{1,0:T(8,128)(2,1)S(1)} %get-tuple-element.164), channel_id=1, source_target_pairs={{0,1},{1,2},{2,3},{4,5},{5,6},{6,7},{8,9},{9,10},{10,11},{12,13},{... | collective-permute-start | bytes 196616 | tf_op jit(solution)/shard_map/ppermute | solution.py:12
  21.0 6.1 %collective-permute-start.3 = (bf16[128,256]{1,0:T(8,128)(2,1)S(1)}, bf16[128,256]{1,0:T(8,128)(2,1)S(1)}, u32[]{:S(2)}, u32[]{:S(2)}) collective-permute-start(bf16[128,256]{1,0:T(8,128)(2,1)S(1)} %get-tuple-element.163), channel_id=1, source_target_pairs={{1,0},{2,1},{3,2},{5,4},{6,5},{7,6},{9,8},{10,9},{11,10},{13,12},{... | collective-permute-start | bytes 196616 | tf_op jit(solution)/shard_map/ppermute | solution.py:12
  31.6 2.0 %copy-start.10 = (bf16[384,128]{1,0:T(8,128)(2,1)S(1)}, bf16[384,128]{1,0:T(8,128)(2,1)}, u32[]{:S(2)}) copy-start(bf16[384,128]{1,0:T(8,128)(2,1)} %get-tuple-element.337) | copy-start | bytes 294916 | tf_op jit(solution)/shard_map/while
  43.4 2.0 %copy-start.10 = (bf16[384,128]{1,0:T(8,128)(2,1)S(1)}, bf16[384,128]{1,0:T(8,128)(2,1)}, u32[]{:S(2)}) copy-start(bf16[384,128]{1,0:T(8,128)(2,1)} %get-tuple-element.337) | copy-start | bytes 294916 | tf_op jit(solution)/shard_map/while
  55.1 2.0 %copy-start.10 = (bf16[384,128]{1,0:T(8,128)(2,1)S(1)}, bf16[384,128]{1,0:T(8,128)(2,1)}, u32[]{:S(2)}) copy-start(bf16[384,128]{1,0:T(8,128)(2,1)} %get-tuple-element.337) | copy-start | bytes 294916 | tf_op jit(solution)/shard_map/while
  66.9 2.0 %copy-start.10 = (bf16[384,128]{1,0:T(8,128)(2,1)S(1)}, bf16[384,128]{1,0:T(8,128)(2,1)}, u32[]{:S(2)}) copy-start(bf16[384,128]{1,0:T(8,128)(2,1)} %get-tuple-element.337) | copy-start | bytes 294916 | tf_op jit(solution)/shard_map/while
  78.7 2.0 %copy-start.10 = (bf16[384,128]{1,0:T(8,128)(2,1)S(1)}, bf16[384,128]{1,0:T(8,128)(2,1)}, u32[]{:S(2)}) copy-start(bf16[384,128]{1,0:T(8,128)(2,1)} %get-tuple-element.337) | copy-start | bytes 294916 | tf_op jit(solution)/shard_map/while
  90.4 2.0 %copy-start.10 = (bf16[384,128]{1,0:T(8,128)(2,1)S(1)}, bf16[384,128]{1,0:T(8,128)(2,1)}, u32[]{:S(2)}) copy-start(bf16[384,128]{1,0:T(8,128)(2,1)} %get-tuple-element.337) | copy-start | bytes 294916 | tf_op jit(solution)/shard_map/while
  102.2 2.0 %copy-start.10 = (bf16[384,128]{1,0:T(8,128)(2,1)S(1)}, bf16[384,128]{1,0:T(8,128)(2,1)}, u32[]{:S(2)}) copy-start(bf16[384,128]{1,0:T(8,128)(2,1)} %get-tuple-element.337) | copy-start | bytes 294916 | tf_op jit(solution)/shard_map/while
  114.0 2.0 %copy-start.10 = (bf16[384,128]{1,0:T(8,128)(2,1)S(1)}, bf16[384,128]{1,0:T(8,128)(2,1)}, u32[]{:S(2)}) copy-start(bf16[384,128]{1,0:T(8,128)(2,1)} %get-tuple-element.337) | copy-start | bytes 294916 | tf_op jit(solution)/shard_map/while
  121.9 0.8 copy-start.12
  123.8 0.7 copy-start.8
  124.0 1.4 copy-start.9
  157.5 8.8 %collective-permute-start.4 = (bf16[1,128,256]{2,1,0:T(8,128)(2,1)S(1)}, bf16[1,128,256]{2,1,0:T(8,128)(2,1)S(1)}, u32[]{:S(2)}, u32[]{:S(2)}) collective-permute-start(bf16[1,128,256]{2,1,0:T(8,128)(2,1)S(1)} %bitcast.83), channel_id=1, source_target_pairs={{0,4},{4,8},{8,12},{12,16},{16,20},{20,24},{24,28},{1,5},{5,9},{9,... | collective-permute-start | bytes 196616 | tf_op jit(solution)/shard_map/ppermute | solution.py:22
  163.7 5.6 %collective-permute-start.5 = (bf16[1,128,256]{2,1,0:T(8,128)(2,1)S(1)}, bf16[1,128,256]{2,1,0:T(8,128)(2,1)S(1)}, u32[]{:S(2)}, u32[]{:S(2)}) collective-permute-start(bf16[1,128,256]{2,1,0:T(8,128)(2,1)S(1)} %bitcast.84), channel_id=1, source_target_pairs={{4,0},{8,4},{12,8},{16,12},{20,16},{24,20},{28,24},{5,1},{9,5},{13... | collective-permute-start | bytes 196616 | tf_op jit(solution)/shard_map/ppermute | solution.py:23
  166.3 4.7 %copy-start.3 = (bf16[256,128]{1,0:T(8,128)(2,1)S(1)}, bf16[256,128]{1,0:T(8,128)(2,1)}, u32[]{:S(2)}) copy-start(bf16[256,128]{1,0:T(8,128)(2,1)} %param.36) | copy-start | bytes 196612
  169.3 2.0 %copy-start.13 = (bf16[128,128]{1,0:T(8,128)(2,1)S(1)}, bf16[128,128]{1,0:T(8,128)(2,1)}, u32[]{:S(2)}) copy-start(bf16[128,128]{1,0:T(8,128)(2,1)} %param.37) | copy-start | bytes 98308
  171.1 0.8 copy-start.5
  171.1 1.0 copy-start.14
  172.0 6.9 %copy-start.4 = (bf16[256,128]{1,0:T(8,128)(2,1)S(1)}, bf16[256,128]{1,0:T(8,128)(2,1)}, u32[]{:S(2)}) copy-start(bf16[256,128]{1,0:T(8,128)(2,1)} %param.40) | copy-start | bytes 196612
  178.9 0.8 copy-start.15
Sparse Core Ops, SparseCore 0:
  125.5 25.7 reduce-scatter.1
where the time goes:
time: 192 us; the launch traced here: 190 us
  matrix products  73.4 us (38%)
  waiting for transfers between devices  28.7 us (15%)
  local copies, waits for them, and re-layouts  26.1 us (14%)
  starting transfers between devices  19 us (10%)
  between operations  15.2 us (8%)
  blocking collectives  11.6 us (6%)
  other arithmetic  9.31 us (5%)
  loops' own time  6.23 us (3%)
    reduce_scatter x1, waiting for transfers between devices, per_device(): lax.psum_scatter(jnp.dot(selector, masked, preferred_element_type=jnp.flo...  25.7 us
    dot_general x24, matrix products, perceptron(): return jnp.dot(hidden, second, preferred_element_type=jnp.float32)  24.8 us
    dot_general x9, matrix products, select_rows(): jnp.dot(selector, values, preferred_element_type=jnp.float32)  17 us
    dot_general x12, matrix products, perceptron(): jnp.dot(inputs, first, preferred_element_type=jnp.float32)  16.7 us
    dynamic_slice x32, local copies, waits for them, and re-layouts, per_device(): lax.scan(edge_block, start_sum, (edge_blocks, source_blocks, target_block...  13.1 us
    ppermute x4, starting transfers between devices, from_behind(): return lax.ppermute(x, axis, pairs)  10.9 us
    dot_general x8, matrix products, edge_block(): jnp.einsum('es,ef->sf', target_pick, pair, preferred_element_type=jnp.flo...  8.05 us
    unnamed x41, local copies, waits for them, and re-layouts  7.48 us
  transfers between devices with their start and end apart: 7, of which 2 were waited for; matrix products, arithmetic and copies ran while one was open for 3% of the time, Pallas kernels for 0%

commit v1 on v0

v1 whole, which is shorter than its diff:
```python
import functools

import jax
import jax.numpy as jnp
from jax import lax
from jax.experimental import pallas as pl
from jax.experimental.pallas import tpu as pltpu
from jax.sharding import PartitionSpec as P

BF = jnp.bfloat16
F32 = jnp.float32
I16 = jnp.int16
I32 = jnp.int32
ANY = pl.BlockSpec(memory_space=pl.ANY)
SMEM = pl.BlockSpec(memory_space=pltpu.SMEM)
VMEM = pl.BlockSpec(memory_space=pltpu.VMEM)
LANES = 128


def mm(a, b):
    return jnp.dot(a, b, preferred_element_type=F32)


def twice(weight):
    zero = jnp.zeros_like(weight)
    return jnp.concatenate(
        [jnp.concatenate([weight, zero], 1), jnp.concatenate([zero, weight], 1)], 0
    )


def centred(weight):
    weight = weight.astype(F32)
    return (weight - jnp.mean(weight, axis=1, keepdims=True)).astype(BF)


def averaging(width):
    return twice(jnp.full((width, width), 1.0 / width, BF))


def column(row):
    count = row.shape[1]
    parts = [
        jnp.broadcast_to(row[:, k : k + LANES], (LANES, LANES)).T for k in range(0, count, LANES)
    ]
    return jnp.concatenate(parts, 0).astype(I16)


def picks(col, count):
    lane = lax.broadcasted_iota(I32, (1, LANES), 1).astype(I16)
    one, zero = jnp.ones((), BF), jnp.zeros((), BF)
    return [
        jnp.where(col == jnp.broadcast_to(lane + jnp.asarray(k, I16), col.shape), one, zero)
        for k in range(0, count, LANES)
    ]


def row_picks(row, count):
    shape = (count, row.shape[1])
    return jnp.where(
        jnp.broadcast_to(row, shape).astype(I16) == lax.broadcasted_iota(I32, shape, 0).astype(I16),
        jnp.ones((), BF),
        jnp.zeros((), BF),
    )


def activated(pre):
    width = pre.shape[1] // 2
    value, tangent = pre[:, :width], pre[:, width:]
    gate = 1.0 / (1.0 + jnp.exp(-value))
    hidden = value * gate
    slope = gate + hidden * (1.0 - gate)
    return jnp.concatenate([hidden, tangent * slope], 1)


def normed(pre, second, ones):
    width = pre.shape[1] // 2
    both = mm(activated(pre).astype(BF), second)
    value, tangent = both[:, :width], both[:, width:]
    stats = mm(jnp.concatenate([value * value, value * tangent], 1).astype(BF), ones)
    scale = lax.rsqrt(stats[:, :width] + 1e-05)
    return value * scale, scale * (tangent - value * (scale * scale * stats[:, width:]))


def fetch(pairs, sems):
    copies = [pltpu.make_async_copy(src, dst, sems.at[k]) for k, (src, dst) in enumerate(pairs)]
    for copy in copies:
        copy.start()
    return copies


def halo_kernel(nl, nt, lists, o0, o1, o2, o3, nl_v, nt_v, lists_v, sems):
    for copy in fetch([(nl, nl_v), (nt, nt_v), (lists, lists_v)], sems):
        copy.wait()
    slots = nl.shape[0]
    paired = jnp.concatenate([nl_v[...], nt_v[...]], 1)
    even = (lax.rem(lax.axis_index("dom"), 2) == 0, lax.rem(lax.axis_index("grp"), 2) == 0)
    for k, out in enumerate((o0, o1, o2, o3)):
        base = k // 2 * 2
        up = even[k // 2] if k % 2 == 0 else jnp.logical_not(even[k // 2])
        row = jnp.where(up, lists_v[0, base : base + 1, :], lists_v[0, base + 1 : base + 2, :])
        selector = jnp.concatenate(picks(column(row), slots), 1)
        out[...] = mm(selector, paired).astype(BF)


def edge_kernel(nl, nt, ed, src, tgt, own, cs, nc, ec, h0, h1, h2, h3, ef, es, nf, ns,
                first_o, part_o,
                nl_v, nt_v, ed_v, src_v, tgt_v, own_v, cs_v, h0_v, h1_v, h2_v, h3_v, ef_v, es_v, nf_v, ns_v,
                table, total, second, ones, sems, *, block):
    copies = fetch(
        list(zip(
            (nl, nt, ef, h0, h1, h2, h3, src, tgt, es, ed, nf, ns, own, cs),
            (nl_v, nt_v, ef_v, h0_v, h1_v, h2_v, h3_v, src_v, tgt_v, es_v, ed_v, nf_v, ns_v, own_v, cs_v),
        )),
        sems,
    )
    for copy in copies:
        copy.wait()
    slots, width = nl.shape
    edges = ed.shape[0]
    rim = h0.shape[0]
    reach = slots + 4 * rim
    paired = jnp.concatenate([nl_v[...], nt_v[...]], 1)
    weight = twice(ef_v[width : 2 * width, :])
    table[0:slots, :] = mm(paired, weight).astype(BF)
    odd = (lax.rem(lax.axis_index("dom"), 2), lax.rem(lax.axis_index("grp"), 2))
    for k, got in enumerate((h0_v, h1_v, h2_v, h3_v)):
        place = k // 2 * 2 + (odd[k // 2] if k % 2 else 1 - odd[k // 2])
        at = pl.ds(pl.multiple_of(slots + place * rim, rim), rim)
        table[at, :] = mm(got[...], weight).astype(BF)
    table[reach:, :] = mm(paired, twice(ef_v[2 * width :, :])).astype(BF)
    second[...] = twice(centred(es_v[...]))
    ones[...] = averaging(width)
    total[...] = jnp.zeros_like(total)
    own_weight = ef_v[0:width, :]
    live = ec[0]

    def step(number, carry):
        at = pl.ds(pl.multiple_of(number * block, block), block)
        target = tgt_v[0:1, at]
        selector = jnp.concatenate(
            picks(column(src_v[0:1, at]), reach) + picks(column(target), slots), 1
        )
        pre = mm(selector, table[...])
        mine = ed_v[at, :]
        pre = jnp.concatenate([pre[:, :width] + mm(mine, own_weight), pre[:, width:]], 1)
        value, tangent = normed(pre, second[...], ones[...])
        pair = jnp.concatenate([mine.astype(F32) + value, tangent], 1).astype(BF)
        slot = lax.broadcasted_iota(I32, (1, block), 1) + number * block
        total[...] += mm(row_picks(jnp.where(slot < live, target, -1), slots), pair)
        return carry

    lax.fori_loop(0, edges // block, step, 0)
    pre = mm(paired, twice(nf_v[0:width, :])) + mm(total[...].astype(BF), twice(nf_v[width:, :]))
    value, tangent = normed(pre, twice(centred(ns_v[...])), ones[...])
    first = (paired.astype(F32) + jnp.concatenate([value, tangent], 1)).astype(BF)
    first_o[...] = first
    owner = own_v[...]
    owner = jnp.where(lax.broadcasted_iota(I32, owner.shape, 1) < nc[0], owner, -1)
    owned, fan = cs.shape
    row_nodes = owned * lax.axis_size("grp")
    part_o[0:row_nodes, :] = mm(row_picks(owner, row_nodes), first).astype(BF)
    high = (cs_v[...] // 256).astype(BF)
    low = lax.rem(cs_v[...], 256).astype(BF)
    lane = lax.broadcasted_iota(I32, (owned, 2 * width), 1)
    spot = lax.broadcasted_iota(I32, (owned, 2 * width), 0) + lax.axis_index("grp") * owned
    for k in range((part_o.shape[0] - row_nodes) // (2 * fan)):
        place = jnp.where(lane + k * 2 * width == spot, jnp.ones((), F32), jnp.zeros((), F32)).astype(BF)
        rows = [
            lax.dot_general(part, place, (((0,), (0,)), ((), ())), preferred_element_type=F32)
            for part in (high, low)
        ]
        base = row_nodes + k * 2 * fan
        part_o[base : base + 2 * fan, :] = jnp.concatenate(rows, 0).astype(BF)


def coarse_kernel(summed, v0, v1, first, own, nc, mf, ms, cf, cs, pf, ps,
                  node_o, tangent_o,
                  summed_v, v0_v, v1_v, first_v, own_v, mf_v, ms_v, cf_v, cs_v, pf_v, ps_v,
                  table, sems, *, row_nodes, fan):
    copies = fetch(
        list(zip(
            (mf, summed, v0, v1, ms, cf, cs, pf, ps, own, first),
            (mf_v, summed_v, v0_v, v1_v, ms_v, cf_v, cs_v, pf_v, ps_v, own_v, first_v),
        )),
        sems,
    )
    for copy in copies:
        copy.wait()
    slots, width = node_o.shape
    ones = averaging(width)
    mine = summed_v[0:row_nodes, :]
    weight = twice(mf_v[0:width, :])
    table[row_nodes : 2 * row_nodes, :] = mm(mine, weight).astype(BF)
    odd = lax.rem(lax.axis_index("dom"), 2)
    for k, got in enumerate((v0_v, v1_v)):
        place = 2 * odd if k else 2 - 2 * odd
        at = pl.ds(pl.multiple_of(place * row_nodes, row_nodes), row_nodes)
        table[at, :] = mm(got[0:row_nodes, :], weight).astype(BF)
    received = mm(mine, twice(mf_v[width:, :]))
    sums = []
    for begin in range(0, row_nodes, LANES):
        chunk, lanes = divmod(begin, 2 * width)
        base = row_nodes + chunk * 2 * fan
        spots = summed_v[base : base + 2 * fan, lanes : lanes + LANES].astype(F32)
        spots = (spots[0:fan, :] * 256.0 + spots[fan:, :]).astype(I32)
        got = received[begin : begin + LANES, :]
        selector = jnp.concatenate([column(spots[j : j + 1, :]) for j in range(fan)], 0)
        pre = mm(jnp.concatenate(picks(selector, 3 * row_nodes), 1), table[...])
        hidden = activated(pre + jnp.concatenate([got] * fan, 0))
        sums.append(sum(hidden[j * LANES : (j + 1) * LANES, :] for j in range(fan)))
    hidden = jnp.concatenate(sums, 0)
    weight = twice(ms_v[...])
    large = hidden.astype(BF)
    message = (mm(large, weight) + mm((hidden - large.astype(F32)).astype(BF), weight)).astype(BF)
    pre = mm(mine, twice(cf_v[0:width, :])) + mm(message, twice(cf_v[width:, :]))
    value, tangent = normed(pre, twice(centred(cs_v[...])), ones)
    updated = jnp.concatenate([value, tangent], 1).astype(BF)
    brought = mm(updated, twice(pf_v[width:, :])).astype(BF)
    owner = jnp.concatenate(picks(column(own_v[...]), row_nodes), 1)
    first_all = first_v[...]
    pre = mm(first_all, twice(pf_v[0:width, :])) + mm(owner, brought)
    value, tangent = normed(pre, twice(centred(ps_v[...])), ones)
    valid = lax.broadcasted_iota(I32, (slots, 1), 0) < nc[0]
    node_o[...] = jnp.where(valid, first_all[:, :width].astype(F32) + value, 0.0).astype(BF)
    tangent_o[...] = jnp.where(valid, first_all[:, width:].astype(F32) + tangent, 0.0).astype(BF)


def like(*arrays):
    return [pltpu.VMEM(a.shape, a.dtype) for a in arrays]


def params():
    return pltpu.CompilerParams(vmem_limit_bytes=48 * 2**20)


def swap(x, axis, first):
    pairs = []
    for i in range(first, lax.axis_size(axis) - 1, 2):
        pairs += [(i, i + 1), (i + 1, i)]
    return lax.ppermute(x, axis, pairs)


def row_sum(x):
    size = lax.axis_size("grp")
    total = x.astype(F32)
    for by in range(1, size):
        if size & (size - 1) == 0:
            pairs = [(i, i ^ by) for i in range(size)]
        else:
            pairs = [(i, (i + by) % size) for i in range(size)]
        total = total + lax.ppermute(x, "grp", pairs).astype(F32)
    return total.astype(BF)


def per_device(nl, nt, ed, nc, ec, lists, src, tgt, own, sources, ef, es, nf, ns, mf, ms, cf, cs, pf, ps):
    slots, width = nl.shape
    edges = ed.shape[0]
    rim = lists.shape[2]
    owned, fan = sources.shape
    row_nodes = owned * lax.axis_size("grp")
    extra = 2 * fan * (-(-row_nodes // (2 * width)))
    shape = jax.ShapeDtypeStruct
    sent = pl.pallas_call(
        halo_kernel,
        out_shape=[shape((rim, 2 * width), BF)] * 4,
        in_specs=[ANY] * 3,
        out_specs=[VMEM] * 4,
        scratch_shapes=like(nl, nt, lists) + [pltpu.SemaphoreType.DMA((3,))],
        compiler_params=params(),
        name="halo_rows",
    )(nl, nt, lists)
    got = [swap(sent[k], ("dom", "grp")[k // 2], k % 2) for k in range(4)]
    first, part = pl.pallas_call(
        functools.partial(edge_kernel, block=min(edges, 1024)),
        out_shape=[shape((slots, 2 * width), BF), shape((row_nodes + extra, 2 * width), BF)],
        in_specs=[ANY] * 7 + [SMEM] * 2 + [ANY] * 8,
        out_specs=[VMEM] * 2,
        scratch_shapes=like(nl, nt, ed, src, tgt, own, sources, *got, ef, es, nf, ns)
        + [
            pltpu.VMEM((2 * slots + 4 * rim, 2 * width), BF),
            pltpu.VMEM((slots, 2 * width), F32),
            pltpu.VMEM((2 * width, 2 * width), BF),
            pltpu.VMEM((2 * width, 2 * width), BF),
            pltpu.SemaphoreType.DMA((15,)),
        ],
        compiler_params=params(),
        name="edges",
    )(nl, nt, ed, src, tgt, own, sources, nc, ec, *got, ef, es, nf, ns)
    summed = row_sum(part)
    v0, v1 = swap(summed, "dom", 0), swap(summed, "dom", 1)
    return pl.pallas_call(
        functools.partial(coarse_kernel, row_nodes=row_nodes, fan=fan),
        out_shape=[shape((slots, width), BF)] * 2,
        in_specs=[ANY] * 5 + [SMEM] + [ANY] * 6,
        out_specs=[VMEM] * 2,
        scratch_shapes=like(summed, v0, v1, first, own, mf, ms, cf, cs, pf, ps)
        + [pltpu.VMEM((3 * row_nodes, 2 * width), BF), pltpu.SemaphoreType.DMA((11,))],
        compiler_params=params(),
        name="coarse",
    )(summed, v0, v1, first, own, nc, mf, ms, cf, cs, pf, ps)


def solution(mesh):
    parts = ("dom", "grp")
    rows = P(parts, None)
    in_specs = (rows,) * 3 + (P(parts),) * 2 + (P(parts, None, None),) + (rows,) * 4 + (P(),) * 10
    return jax.shard_map(
        per_device, mesh=mesh, in_specs=in_specs, out_specs=(rows, rows), check_vma=False
    )
```

time: 192 us -> 58.3 us (0.30)
  matrix products: 73.4 us -> 0 us
  Pallas kernels: 0 us -> 23.2 us
  waiting for transfers between devices: 28.7 us -> 5.57 us
  local copies, waits for them, and re-layouts: 26.1 us -> 9.22 us
  between operations: 15.2 us -> 2.13 us
  blocking collectives: 11.6 us -> 0 us
  other arithmetic: 9.31 us -> 0.04 us
  loops' own time: 6.23 us -> 0 us
    dot_general x63 -> x0, matrix products: 73.4 us -> none  [the longest x24 24.8 us: perceptron(): return jnp.dot(hidden, second, preferred_element_type=jnp.float32)]
    reduce_scatter x1 -> x0, waiting for transfers between devices: 25.7 us -> none  [per_device(): lax.psum_scatter(jnp.dot(selector, masked, preferred_element_type=jnp.flo...]
    pallas_call x0 -> x3, Pallas kernels: none -> 23.2 us  [the longest x1 18.5 us: per_device(): pl.pallas_call(functools.partial(edge_kernel, block=min(edges, 1024)), ou...]
    dynamic_slice x32 -> x0, local copies, waits for them, and re-layouts: 13.1 us -> none  [per_device(): lax.scan(edge_block, start_sum, (edge_blocks, source_blocks, target_block...]
    all_gather x2 -> x0, blocking collectives: 11.6 us -> none  [the longest x1 6.19 us: per_device(): coarse = lax.all_gather(own_sum, 'grp', axis=0, tiled=True)]
    another operation x1 -> x0, loops' own time: 6.23 us -> none  [per_device(): lax.scan(edge_block, start_sum, (edge_blocks, source_blocks, target_block...]
    lt x9 -> x0, other arithmetic: 5.24 us -> none  [the longest x8 5.23 us: edge_block(): live = (number * block_rows + jnp.arange(block_rows) < edge_total)[:, None]]
    ppermute x6 -> x9, waiting for transfers between devices: 2.95 us -> 5.57 us  [the longest x3 3.62 us: row_sum(): total = total + lax.ppermute(x, 'grp', pairs).astype(F32)]
  transfers between devices with their start and end apart: 7 -> 9, of which waited for: 2 -> 3; matrix products, arithmetic and copies ran while one was open for 3% -> 1% of each run, Pallas kernels for 0% -> 0%
where the time goes in v1:
time: 58.3 us; the launch traced here: 57.6 us
  Pallas kernels  23.2 us (40%)
  starting transfers between devices  17.4 us (30%)
  local copies, waits for them, and re-layouts  9.22 us (16%)
  waiting for transfers between devices  5.57 us (10%)
  between operations  2.13 us (4%)
    pallas_call x1, Pallas kernels, per_device(): pl.pallas_call(functools.partial(edge_kernel, block=min(edges, 1024)), ou...  18.5 us
    ppermute x6, starting transfers between devices, swap(): return lax.ppermute(x, axis, pairs)  11.8 us
    unnamed x39, local copies, waits for them, and re-layouts  9.22 us
    ppermute x3, starting transfers between devices, row_sum(): total = total + lax.ppermute(x, 'grp', pairs).astype(F32)  5.62 us
    pallas_call x1, Pallas kernels, per_device(): pl.pallas_call(functools.partial(coarse_kernel, row_nodes=row_nodes, fan=...  4.15 us
    ppermute x3, waiting for transfers between devices, row_sum(): total = total + lax.ppermute(x, 'grp', pairs).astype(F32)  3.62 us
    ppermute x6, waiting for transfers between devices, swap(): return lax.ppermute(x, axis, pairs)  1.96 us
  transfers between devices with their start and end apart: 9, of which 3 were waited for; matrix products, arithmetic and copies ran while one was open for 1% of the time, Pallas kernels for 0%

profile of v1, /device:TPU:1, one launch (start us, length us, event | category | flops | bytes accessed | tf_op | source)
XLA Modules:
  0.0 57.6 jit_solution(2956065842567280056)
XLA Ops:
  0.6 0.0 copy-start.1
  0.6 0.9 %copy-done.1 = bf16[1024,128]{1,0:T(8,128)(2,1)S(1)} copy-done((bf16[1024,128]{1,0:T(8,128)(2,1)S(1)}, bf16[1024,128]{1,0:T(8,128)(2,1)}, u32[]{:S(2)}) %copy-start.1) | copy-done | bytes 262168
  1.6 0.9 %copy-done.3 = bf16[1024,128]{1,0:T(8,128)(2,1)S(1)} copy-done((bf16[1024,128]{1,0:T(8,128)(2,1)S(1)}, bf16[1024,128]{1,0:T(8,128)(2,1)}, u32[]{:S(2)}) %copy-start.3) | copy-done | bytes 262168
  2.5 0.7 %copy-done.18 = s32[1,4,128]{2,1,0:T(4,128)S(1)} copy-done((s32[1,4,128]{2,1,0:T(4,128)S(1)}, s32[1,4,128]{2,1,0:T(4,128)}, u32[]{:S(2)}) %copy-start.18) | copy-done | bytes 2072
  3.2 0.6 halo_rows.1
  3.8 0.1 collective-permute-start
  3.9 4.6 %collective-permute-start.1 = (bf16[128,256]{1,0:T(8,128)(2,1)S(1)}, bf16[128,256]{1,0:T(8,128)(2,1)S(1)}, u32[]{:S(2)}, u32[]{:S(2)}) collective-permute-start(bf16[128,256]{1,0:T(8,128)(2,1)S(1)} %get-tuple-element.9), channel_id=1, source_target_pairs={{4,8},{8,4},{12,16},{16,12},{20,24},{24,20},{5,9},{9,5},{13,17},{1... | collective-permute-start | bytes 196616 | tf_op jit(solution)/shard_map/ppermute | solution.py:240
  8.5 1.3 %collective-permute-start.2 = (bf16[128,256]{1,0:T(8,128)(2,1)S(1)}, bf16[128,256]{1,0:T(8,128)(2,1)S(1)}, u32[]{:S(2)}, u32[]{:S(2)}) collective-permute-start(bf16[128,256]{1,0:T(8,128)(2,1)S(1)} %get-tuple-element.10), channel_id=1, source_target_pairs={{0,1},{1,0},{2,3},{3,2},{4,5},{5,4},{6,7},{7,6},{8,9},{9,8},{10,11... | collective-permute-start | bytes 196616 | tf_op jit(solution)/shard_map/ppermute | solution.py:240
  9.8 0.7 %collective-permute-start.3 = (bf16[128,256]{1,0:T(8,128)(2,1)S(1)}, bf16[128,256]{1,0:T(8,128)(2,1)S(1)}, u32[]{:S(2)}, u32[]{:S(2)}) collective-permute-start(bf16[128,256]{1,0:T(8,128)(2,1)S(1)} %get-tuple-element.11), channel_id=1, source_target_pairs={{1,2},{2,1},{5,6},{6,5},{9,10},{10,9},{13,14},{14,13},{17,18},{18,... | collective-permute-start | bytes 196616 | tf_op jit(solution)/shard_map/ppermute | solution.py:240
  11.7 0.8 %copy.22.cs = s32[32,8]{1,0:T(8,128)S(1)} copy(s32[32,8]{0,1:T(8,128)} %param.29) | data formatting | bytes 2048 | tf_op args[9]
  12.5 0.0 collective-permute-done.h0
  12.5 0.0 collective-permute-done.1.h1
  12.5 0.0 collective-permute-done.2.h2
  12.5 0.0 collective-permute-done.3.h3
  12.5 0.0 copy-done.2
  12.5 0.0 copy-done.4
  12.5 0.0 copy-done.10
  12.5 0.0 copy-start
  12.5 1.2 %copy-done = bf16[4096,128]{1,0:T(8,128)(2,1)S(1)} copy-done((bf16[4096,128]{1,0:T(8,128)(2,1)S(1)}, bf16[4096,128]{1,0:T(8,128)(2,1)}, u32[]{:S(2)}) %copy-start) | copy-done | bytes 1048600
  13.8 0.9 %copy-done.5 = bf16[384,128]{1,0:T(8,128)(2,1)S(1)} copy-done((bf16[384,128]{1,0:T(8,128)(2,1)S(1)}, bf16[384,128]{1,0:T(8,128)(2,1)}, u32[]{:S(2)}) %copy-start.5) | copy-done | bytes 98328
  14.7 0.8 %copy-done.9 = bf16[256,128]{1,0:T(8,128)(2,1)S(1)} copy-done((bf16[256,128]{1,0:T(8,128)(2,1)S(1)}, bf16[256,128]{1,0:T(8,128)(2,1)}, u32[]{:S(2)}) %copy-start.9) | copy-done | bytes 65560
  15.5 0.8 %copy-done.11 = bf16[128,128]{1,0:T(8,128)(2,1)S(1)} copy-done((bf16[128,128]{1,0:T(8,128)(2,1)S(1)}, bf16[128,128]{1,0:T(8,128)(2,1)}, u32[]{:S(2)}) %copy-start.11) | copy-done | bytes 32792
  16.3 0.7 %copy-done.15 = s32[1,4096]{1,0:T(1,128)S(1)} copy-done((s32[1,4096]{1,0:T(1,128)S(1)}, s32[1,4096]{1,0:T(1,128)}, u32[]{:S(2)}) %copy-start.15) | copy-done | bytes 16408
  17.0 0.7 %copy-done.16 = s32[1,4096]{1,0:T(1,128)S(1)} copy-done((s32[1,4096]{1,0:T(1,128)S(1)}, s32[1,4096]{1,0:T(1,128)}, u32[]{:S(2)}) %copy-start.16) | copy-done | bytes 16408
  17.7 0.7 %copy-done.17 = s32[1,1024]{1,0:T(1,128)S(1)} copy-done((s32[1,1024]{1,0:T(1,128)S(1)}, s32[1,1024]{1,0:T(1,128)}, u32[]{:S(2)}) %copy-start.17) | copy-done | bytes 4120
  18.4 18.5 %edges.1 = (bf16[1024,256]{1,0:T(8,128)(2,1)S(1)}, bf16[144,256]{1,0:T(8,128)(2,1)S(1)}) custom-call(bf16[1024,128]{1,0:T(8,128)(2,1)S(1)} %copy-done.2, bf16[1024,128]{1,0:T(8,128)(2,1)S(1)} %copy-done.4, bf16[4096,128]{1,0:T(8,128)(2,1)S(1)} %copy-done, s32[1,4096]{1,0:T(1,128)S(1)} %copy-done.15, s32[1,4096]{1,0:T(1,128)S(1)} %copy-done.16, ...), custom_call_target="tpu_custom_call" | custom-call | tf_op jit(solution)/shard_map/edges/pallas_call | solution.py:273
  36.9 0.0 copy-start.6
  36.9 0.0 copy-start.7
  36.9 0.0 copy-start.8
  36.9 0.0 copy-start.12
  37.0 0.0 copy-start.13
  37.0 0.0 copy-start.14
  37.0 2.0 %collective-permute-start.6 = (bf16[144,256]{1,0:T(8,128)(2,1)S(1)}, bf16[144,256]{1,0:T(8,128)(2,1)S(1)}, u32[]{:S(2)}, u32[]{:S(2)}) collective-permute-start(bf16[144,256]{1,0:T(8,128)(2,1)S(1)} %get-tuple-element.12), channel_id=1, source_target_pairs={{0,3},{1,2},{2,1},{3,0},{4,7},{5,6},{6,5},{7,4},{8,11},{9,10},{10,... | collective-permute-start | bytes 221192 | tf_op jit(solution)/shard_map/ppermute | solution.py:251
  39.0 2.9 %collective-permute-start.5 = (bf16[144,256]{1,0:T(8,128)(2,1)S(1)}, bf16[144,256]{1,0:T(8,128)(2,1)S(1)}, u32[]{:S(2)}, u32[]{:S(2)}) collective-permute-start(bf16[144,256]{1,0:T(8,128)(2,1)S(1)} %get-tuple-element.12), channel_id=1, source_target_pairs={{0,2},{1,3},{2,0},{3,1},{4,6},{5,7},{6,4},{7,5},{8,10},{9,11},{10,... | collective-permute-start | bytes 221192 | tf_op jit(solution)/shard_map/ppermute | solution.py:251
  41.9 0.7 %collective-permute-start.4 = (bf16[144,256]{1,0:T(8,128)(2,1)S(1)}, bf16[144,256]{1,0:T(8,128)(2,1)S(1)}, u32[]{:S(2)}, u32[]{:S(2)}) collective-permute-start(bf16[144,256]{1,0:T(8,128)(2,1)S(1)} %get-tuple-element.12), channel_id=1, source_target_pairs={{0,1},{1,0},{2,3},{3,2},{4,5},{5,4},{6,7},{7,6},{8,9},{9,8},{10,11... | collective-permute-start | bytes 221192 | tf_op jit(solution)/shard_map/ppermute | solution.py:251
  42.6 0.0 collective-permute-done.6
  42.6 2.6 %collective-permute-done.5 = bf16[144,256]{1,0:T(8,128)(2,1)S(1)} collective-permute-done((bf16[144,256]{1,0:T(8,128)(2,1)S(1)}, bf16[144,256]{1,0:T(8,128)(2,1)S(1)}, u32[]{:S(2)}, u32[]{:S(2)}) %collective-permute-start.5) | collective-permute-done | bytes 73760 | tf_op jit(solution)/shard_map/ppermute | solution.py:251
  45.2 1.0 %collective-permute-done.4 = bf16[144,256]{1,0:T(8,128)(2,1)S(1)} collective-permute-done((bf16[144,256]{1,0:T(8,128)(2,1)S(1)}, bf16[144,256]{1,0:T(8,128)(2,1)S(1)}, u32[]{:S(2)}, u32[]{:S(2)}) %collective-permute-start.4) | collective-permute-done | bytes 73760 | tf_op jit(solution)/shard_map/ppermute | solution.py:251
  46.3 5.2 %collective-permute-start.8 = (bf16[144,256]{1,0:T(8,128)(2,1)S(1)}, bf16[144,256]{1,0:T(8,128)(2,1)S(1)}, u32[]{:S(2)}, u32[]{:S(2)}) collective-permute-start(bf16[144,256]{1,0:T(8,128)(2,1)S(1)} %add_convert_fusion.summed), channel_id=1, source_target_pairs={{4,8},{8,4},{12,16},{16,12},{20,24},{24,20},{5,9},{9,5},{13,17},{1... | collective-permute-start | bytes 221192 | tf_op jit(solution)/shard_map/ppermute | solution.py:240
  51.4 0.1 collective-permute-start.7
  51.5 1.9 %collective-permute-done.8.v1 = bf16[144,256]{1,0:T(8,128)(2,1)S(1)} collective-permute-done((bf16[144,256]{1,0:T(8,128)(2,1)S(1)}, bf16[144,256]{1,0:T(8,128)(2,1)S(1)}, u32[]{:S(2)}, u32[]{:S(2)}) %collective-permute-start.8) | collective-permute-done | bytes 73760 | tf_op jit(solution)/shard_map/ppermute | solution.py:240
  53.4 0.0 collective-permute-done.7.v0
  53.5 0.0 copy-done.6
  53.5 0.0 copy-done.7
  53.5 0.0 copy-done.8
  53.5 0.0 copy-done.12
  53.5 0.0 copy-done.13
  53.5 4.1 %coarse.1 = (bf16[1024,128]{1,0:T(8,128)(2,1)}, bf16[1024,128]{1,0:T(8,128)(2,1)}) custom-call(bf16[144,256]{1,0:T(8,128)(2,1)S(1)} %add_convert_fusion.summed, bf16[144,256]{1,0:T(8,128)(2,1)S(1)} %collective-permute-done.7.v0, bf16[144,256]{1,0:T(8,128)(2,1)S(1)} %collective-permute-done.8.v1, bf16[1024,256]{1,0:T(8,128)(2,1)S(1)} %get-tuple-element.13.first, ...), custom_call_target="tpu_custom_call" | custom-call | tf_op jit(solution)/shard_map/coarse/pallas_call | solution.py:291
  (13 shorter events, 0.1 us)
Async XLA Ops:
  0.6 1.0 %copy-start.1 = (bf16[1024,128]{1,0:T(8,128)(2,1)S(1)}, bf16[1024,128]{1,0:T(8,128)(2,1)}, u32[]{:S(2)}) copy-start(bf16[1024,128]{1,0:T(8,128)(2,1)} %nl.3) | copy-start | bytes 786436
  1.6 0.9 %copy-start.3 = (bf16[1024,128]{1,0:T(8,128)(2,1)S(1)}, bf16[1024,128]{1,0:T(8,128)(2,1)}, u32[]{:S(2)}) copy-start(bf16[1024,128]{1,0:T(8,128)(2,1)} %nt.3) | copy-start | bytes 786436
  2.5 0.7 %copy-start.18 = (s32[1,4,128]{2,1,0:T(4,128)S(1)}, s32[1,4,128]{2,1,0:T(4,128)}, u32[]{:S(2)}) copy-start(s32[1,4,128]{2,1,0:T(4,128)} %lists.1) | copy-start | bytes 6148
  3.2 9.3 %copy-start.2 = (bf16[1024,128]{1,0:T(8,128)(2,1)S(1)}, bf16[1024,128]{1,0:T(8,128)(2,1)}, u32[]{:S(2)}) copy-start(bf16[1024,128]{1,0:T(8,128)(2,1)} %nl.3) | copy-start | bytes 786436
  3.2 9.3 %copy-start.4 = (bf16[1024,128]{1,0:T(8,128)(2,1)S(1)}, bf16[1024,128]{1,0:T(8,128)(2,1)}, u32[]{:S(2)}) copy-start(bf16[1024,128]{1,0:T(8,128)(2,1)} %nt.3) | copy-start | bytes 786436
  3.2 9.3 %copy-start.10 = (bf16[128,128]{1,0:T(8,128)(2,1)S(1)}, bf16[128,128]{1,0:T(8,128)(2,1)}, u32[]{:S(2)}) copy-start(bf16[128,128]{1,0:T(8,128)(2,1)} %es.1) | copy-start | bytes 98308
  3.8 8.7 %collective-permute-start = (bf16[128,256]{1,0:T(8,128)(2,1)S(1)}, bf16[128,256]{1,0:T(8,128)(2,1)S(1)}, u32[]{:S(2)}, u32[]{:S(2)}) collective-permute-start(bf16[128,256]{1,0:T(8,128)(2,1)S(1)} %get-tuple-element.8), channel_id=1, source_target_pairs={{0,4},{4,0},{8,12},{12,8},{16,20},{20,16},{24,28},{28,24},{1,5},{5... | collective-permute-start | bytes 196616 | tf_op jit(solution)/shard_map/ppermute | solution.py:240
  3.9 8.6 %collective-permute-start.1 = (bf16[128,256]{1,0:T(8,128)(2,1)S(1)}, bf16[128,256]{1,0:T(8,128)(2,1)S(1)}, u32[]{:S(2)}, u32[]{:S(2)}) collective-permute-start(bf16[128,256]{1,0:T(8,128)(2,1)S(1)} %get-tuple-element.9), channel_id=1, source_target_pairs={{4,8},{8,4},{12,16},{16,12},{20,24},{24,20},{5,9},{9,5},{13,17},{1... | collective-permute-start | bytes 196616 | tf_op jit(solution)/shard_map/ppermute | solution.py:240
  8.5 4.0 %collective-permute-start.2 = (bf16[128,256]{1,0:T(8,128)(2,1)S(1)}, bf16[128,256]{1,0:T(8,128)(2,1)S(1)}, u32[]{:S(2)}, u32[]{:S(2)}) collective-permute-start(bf16[128,256]{1,0:T(8,128)(2,1)S(1)} %get-tuple-element.10), channel_id=1, source_target_pairs={{0,1},{1,0},{2,3},{3,2},{4,5},{5,4},{6,7},{7,6},{8,9},{9,8},{10,11... | collective-permute-start | bytes 196616 | tf_op jit(solution)/shard_map/ppermute | solution.py:240
  9.8 2.7 %collective-permute-start.3 = (bf16[128,256]{1,0:T(8,128)(2,1)S(1)}, bf16[128,256]{1,0:T(8,128)(2,1)S(1)}, u32[]{:S(2)}, u32[]{:S(2)}) collective-permute-start(bf16[128,256]{1,0:T(8,128)(2,1)S(1)} %get-tuple-element.11), channel_id=1, source_target_pairs={{1,2},{2,1},{5,6},{6,5},{9,10},{10,9},{13,14},{14,13},{17,18},{18,... | collective-permute-start | bytes 196616 | tf_op jit(solution)/shard_map/ppermute | solution.py:240
  12.5 1.2 %copy-start = (bf16[4096,128]{1,0:T(8,128)(2,1)S(1)}, bf16[4096,128]{1,0:T(8,128)(2,1)}, u32[]{:S(2)}) copy-start(bf16[4096,128]{1,0:T(8,128)(2,1)} %ed.1) | copy-start | bytes 3145732
  13.8 0.9 %copy-start.5 = (bf16[384,128]{1,0:T(8,128)(2,1)S(1)}, bf16[384,128]{1,0:T(8,128)(2,1)}, u32[]{:S(2)}) copy-start(bf16[384,128]{1,0:T(8,128)(2,1)} %ef.1) | copy-start | bytes 294916
  14.7 0.8 %copy-start.9 = (bf16[256,128]{1,0:T(8,128)(2,1)S(1)}, bf16[256,128]{1,0:T(8,128)(2,1)}, u32[]{:S(2)}) copy-start(bf16[256,128]{1,0:T(8,128)(2,1)} %nf.1) | copy-start | bytes 196612
  15.5 0.8 %copy-start.11 = (bf16[128,128]{1,0:T(8,128)(2,1)S(1)}, bf16[128,128]{1,0:T(8,128)(2,1)}, u32[]{:S(2)}) copy-start(bf16[128,128]{1,0:T(8,128)(2,1)} %ns.1) | copy-start | bytes 98308
  16.3 0.7 %copy-start.15 = (s32[1,4096]{1,0:T(1,128)S(1)}, s32[1,4096]{1,0:T(1,128)}, u32[]{:S(2)}) copy-start(s32[1,4096]{1,0:T(1,128)} %src.1) | copy-start | bytes 49156
  17.0 0.7 %copy-start.16 = (s32[1,4096]{1,0:T(1,128)S(1)}, s32[1,4096]{1,0:T(1,128)}, u32[]{:S(2)}) copy-start(s32[1,4096]{1,0:T(1,128)} %tgt.1) | copy-start | bytes 49156
  17.7 0.7 %copy-start.17 = (s32[1,1024]{1,0:T(1,128)S(1)}, s32[1,1024]{1,0:T(1,128)}, u32[]{:S(2)}) copy-start(s32[1,1024]{1,0:T(1,128)} %own.3) | copy-start | bytes 12292
  36.9 16.5 %copy-start.6 = (bf16[256,128]{1,0:T(8,128)(2,1)S(1)}, bf16[256,128]{1,0:T(8,128)(2,1)}, u32[]{:S(2)}) copy-start(bf16[256,128]{1,0:T(8,128)(2,1)} %mf.1) | copy-start | bytes 196612
  36.9 16.5 %copy-start.7 = (bf16[256,128]{1,0:T(8,128)(2,1)S(1)}, bf16[256,128]{1,0:T(8,128)(2,1)}, u32[]{:S(2)}) copy-start(bf16[256,128]{1,0:T(8,128)(2,1)} %cf.1) | copy-start | bytes 196612
  36.9 16.5 %copy-start.8 = (bf16[256,128]{1,0:T(8,128)(2,1)S(1)}, bf16[256,128]{1,0:T(8,128)(2,1)}, u32[]{:S(2)}) copy-start(bf16[256,128]{1,0:T(8,128)(2,1)} %pf.1) | copy-start | bytes 196612
  36.9 16.5 %copy-start.12 = (bf16[128,128]{1,0:T(8,128)(2,1)S(1)}, bf16[128,128]{1,0:T(8,128)(2,1)}, u32[]{:S(2)}) copy-start(bf16[128,128]{1,0:T(8,128)(2,1)} %ms.1) | copy-start | bytes 98308
  37.0 16.5 %copy-start.13 = (bf16[128,128]{1,0:T(8,128)(2,1)S(1)}, bf16[128,128]{1,0:T(8,128)(2,1)}, u32[]{:S(2)}) copy-start(bf16[128,128]{1,0:T(8,128)(2,1)} %cs.2) | copy-start | bytes 98308
  37.0 16.5 %copy-start.14 = (bf16[128,128]{1,0:T(8,128)(2,1)S(1)}, bf16[128,128]{1,0:T(8,128)(2,1)}, u32[]{:S(2)}) copy-start(bf16[128,128]{1,0:T(8,128)(2,1)} %ps.1) | copy-start | bytes 98308
  37.0 5.6 %collective-permute-start.6 = (bf16[144,256]{1,0:T(8,128)(2,1)S(1)}, bf16[144,256]{1,0:T(8,128)(2,1)S(1)}, u32[]{:S(2)}, u32[]{:S(2)}) collective-permute-start(bf16[144,256]{1,0:T(8,128)(2,1)S(1)} %get-tuple-element.12), channel_id=1, source_target_pairs={{0,3},{1,2},{2,1},{3,0},{4,7},{5,6},{6,5},{7,4},{8,11},{9,10},{10,... | collective-permute-start | bytes 221192 | tf_op jit(solution)/shard_map/ppermute | solution.py:251
  39.0 6.2 %collective-permute-start.5 = (bf16[144,256]{1,0:T(8,128)(2,1)S(1)}, bf16[144,256]{1,0:T(8,128)(2,1)S(1)}, u32[]{:S(2)}, u32[]{:S(2)}) collective-permute-start(bf16[144,256]{1,0:T(8,128)(2,1)S(1)} %get-tuple-element.12), channel_id=1, source_target_pairs={{0,2},{1,3},{2,0},{3,1},{4,6},{5,7},{6,4},{7,5},{8,10},{9,11},{10,... | collective-permute-start | bytes 221192 | tf_op jit(solution)/shard_map/ppermute | solution.py:251
  41.9 4.3 %collective-permute-start.4 = (bf16[144,256]{1,0:T(8,128)(2,1)S(1)}, bf16[144,256]{1,0:T(8,128)(2,1)S(1)}, u32[]{:S(2)}, u32[]{:S(2)}) collective-permute-start(bf16[144,256]{1,0:T(8,128)(2,1)S(1)} %get-tuple-element.12), channel_id=1, source_target_pairs={{0,1},{1,0},{2,3},{3,2},{4,5},{5,4},{6,7},{7,6},{8,9},{9,8},{10,11... | collective-permute-start | bytes 221192 | tf_op jit(solution)/shard_map/ppermute | solution.py:251
  46.3 7.2 %collective-permute-start.8 = (bf16[144,256]{1,0:T(8,128)(2,1)S(1)}, bf16[144,256]{1,0:T(8,128)(2,1)S(1)}, u32[]{:S(2)}, u32[]{:S(2)}) collective-permute-start(bf16[144,256]{1,0:T(8,128)(2,1)S(1)} %add_convert_fusion.summed), channel_id=1, source_target_pairs={{4,8},{8,4},{12,16},{16,12},{20,24},{24,20},{5,9},{9,5},{13,17},{1... | collective-permute-start | bytes 221192 | tf_op jit(solution)/shard_map/ppermute | solution.py:240
  51.4 2.0 %collective-permute-start.7 = (bf16[144,256]{1,0:T(8,128)(2,1)S(1)}, bf16[144,256]{1,0:T(8,128)(2,1)S(1)}, u32[]{:S(2)}, u32[]{:S(2)}) collective-permute-start(bf16[144,256]{1,0:T(8,128)(2,1)S(1)} %add_convert_fusion.summed), channel_id=1, source_target_pairs={{0,4},{4,0},{8,12},{12,8},{16,20},{20,16},{24,28},{28,24},{1,5},{5... | collective-permute-start | bytes 221192 | tf_op jit(solution)/shard_map/ppermute | solution.py:240

commit v2 on v1

v2 whole, which is shorter than its diff:
```python
import functools

import jax
import jax.numpy as jnp
from jax import lax
from jax.experimental import pallas as pl
from jax.experimental.pallas import tpu as pltpu
from jax.sharding import PartitionSpec as P

BF = jnp.bfloat16
F32 = jnp.float32
I16 = jnp.int16
I32 = jnp.int32
HBM = pl.BlockSpec(memory_space=pltpu.HBM)
SMEM = pl.BlockSpec(memory_space=pltpu.SMEM)
VMEM = pl.BlockSpec(memory_space=pltpu.VMEM)
LANES = 128


def mm(a, b):
    return jnp.dot(a, b, preferred_element_type=F32)


def twice(weight):
    zero = jnp.zeros_like(weight)
    return jnp.concatenate(
        [jnp.concatenate([weight, zero], 1), jnp.concatenate([zero, weight], 1)], 0
    )


def centred(weight):
    weight = weight.astype(F32)
    return (weight - jnp.mean(weight, axis=1, keepdims=True)).astype(BF)


def averaging(width):
    return twice(jnp.full((width, width), 1.0 / width, BF))


def column(row):
    count = row.shape[1]
    parts = [
        jnp.broadcast_to(row[:, k : k + LANES], (LANES, LANES)).T for k in range(0, count, LANES)
    ]
    return jnp.concatenate(parts, 0).astype(I16)


def picks(col, count):
    lane = lax.broadcasted_iota(I32, (1, LANES), 1).astype(I16)
    one, zero = jnp.ones((), BF), jnp.zeros((), BF)
    return [
        jnp.where(col == jnp.broadcast_to(lane + jnp.asarray(k, I16), col.shape), one, zero)
        for k in range(0, count, LANES)
    ]


def row_picks(row, count):
    shape = (count, row.shape[1])
    return jnp.where(
        jnp.broadcast_to(row, shape).astype(I16) == lax.broadcasted_iota(I32, shape, 0).astype(I16),
        jnp.ones((), BF),
        jnp.zeros((), BF),
    )


def activated(pre):
    width = pre.shape[1] // 2
    value, tangent = pre[:, :width], pre[:, width:]
    gate = 1.0 / (1.0 + jnp.exp(-value))
    hidden = value * gate
    slope = gate + hidden * (1.0 - gate)
    return jnp.concatenate([hidden, tangent * slope], 1)


def normed(pre, second, ones):
    width = pre.shape[1] // 2
    both = mm(activated(pre).astype(BF), second)
    value, tangent = both[:, :width], both[:, width:]
    stats = mm(jnp.concatenate([value * value, value * tangent], 1).astype(BF), ones)
    scale = lax.rsqrt(stats[:, :width] + 1e-05)
    return value * scale, scale * (tangent - value * (scale * scale * stats[:, width:]))


def fetch(pairs, sems):
    copies = [pltpu.make_async_copy(src, dst, sems.at[k]) for k, (src, dst) in enumerate(pairs)]
    for copy in copies:
        copy.start()
    return copies


def halo_kernel(nl, nt, lists, o0, o1, o2, o3, nl_v, nt_v, lists_v, sems):
    for copy in fetch([(nl, nl_v), (nt, nt_v), (lists, lists_v)], sems):
        copy.wait()
    slots = nl.shape[0]
    paired = jnp.concatenate([nl_v[...], nt_v[...]], 1)
    even = (lax.rem(lax.axis_index("dom"), 2) == 0, lax.rem(lax.axis_index("grp"), 2) == 0)
    for k, out in enumerate((o0, o1, o2, o3)):
        base = k // 2 * 2
        up = even[k // 2] if k % 2 == 0 else jnp.logical_not(even[k // 2])
        row = jnp.where(up, lists_v[0, base : base + 1, :], lists_v[0, base + 1 : base + 2, :])
        selector = jnp.concatenate(picks(column(row), slots), 1)
        out[...] = mm(selector, paired).astype(BF)


def local_kernel(nl, nt, src, tgt, ef, pre_o, nl_v, nt_v, src_v, tgt_v, ef_v, table, pre_v, sems, out_sems, *, block):
    copies = fetch([(nl, nl_v), (nt, nt_v), (ef, ef_v), (src, src_v), (tgt, tgt_v)], sems)
    for copy in copies:
        copy.wait()
    slots, width = nl.shape
    paired = jnp.concatenate([nl_v[...], nt_v[...]], 1)
    table[0:slots, :] = mm(paired, twice(ef_v[width : 2 * width, :])).astype(BF)
    table[slots:, :] = mm(paired, twice(ef_v[2 * width :, :])).astype(BF)
    stores = []
    for k, begin in enumerate(range(0, pre_o.shape[0], block)):
        at = slice(begin, begin + block)
        selector = jnp.concatenate(
            picks(column(src_v[0:1, at]), slots) + picks(column(tgt_v[0:1, at]), slots), 1
        )
        pre_v[at, :] = mm(selector, table[...])
        copy = pltpu.make_async_copy(pre_v.at[at], pre_o.at[at], out_sems.at[k])
        copy.start()
        stores.append(copy)
    for copy in stores:
        copy.wait()


def edge_kernel(nl, nt, ed, src, tgt, own, sources, ef, es, nf, ns, nc, ec, h0, h1, h2, h3, pre,
                first_o, part_o,
                nl_v, nt_v, ed_v, src_v, tgt_v, own_v, sources_v, ef_v, es_v, nf_v, ns_v,
                table, pairs, pre_v, sems, pre_sems, *, block, rows):
    copies = fetch(
        list(zip(
            (ef, src, es, ed, tgt, nl, nt, nf, ns, own, sources),
            (ef_v, src_v, es_v, ed_v, tgt_v, nl_v, nt_v, nf_v, ns_v, own_v, sources_v),
        )),
        sems,
    )
    slots, width = nl.shape
    edges = ed.shape[0]
    rim = h0.shape[0]
    cuts = [slice(begin, begin + block) for begin in range(0, edges, block)]
    given_copies = fetch([(pre.at[at], pre_v.at[at]) for at in cuts], pre_sems)
    for copy in copies[:3]:
        copy.wait()
    weight = twice(ef_v[width : 2 * width, :])
    odd = (lax.rem(lax.axis_index("dom"), 2), lax.rem(lax.axis_index("grp"), 2))
    for k, got in enumerate((h0, h1, h2, h3)):
        place = k // 2 * 2 + (odd[k // 2] if k % 2 else 1 - odd[k // 2])
        at = pl.ds(pl.multiple_of(place * rim, rim), rim)
        table[at, :] = mm(got[...], weight).astype(BF)
    second = twice(centred(es_v[...]))
    ones = averaging(width)
    own_weight = ef_v[0:width, :]
    for copy in copies[3:]:
        copy.wait()
    for at, copy in zip(cuts, given_copies):
        copy.wait()
        selector = jnp.concatenate(picks(column(src_v[0:1, at] - slots), 4 * rim), 1)
        mine = ed_v[at, :]
        given = pre_v[at, :] + mm(selector, table[...])
        given = jnp.concatenate([given[:, :width] + mm(mine, own_weight), given[:, width:]], 1)
        value, tangent = normed(given, second, ones)
        pairs[at, :] = jnp.concatenate([mine.astype(F32) + value, tangent], 1).astype(BF)
    target = jnp.where(lax.broadcasted_iota(I32, (1, edges), 1) < ec[0], tgt_v[...], -1)
    owner = jnp.where(lax.broadcasted_iota(I32, (1, slots), 1) < nc[0], own_v[...], -1)
    fixed = twice(nf_v[0:width, :])
    added = twice(nf_v[width:, :])
    second = twice(centred(ns_v[...]))
    fan, owned = sources.shape
    row_nodes = owned * lax.axis_size("grp")
    part = jnp.zeros((row_nodes, 2 * width), F32)
    for begin in range(0, slots, rows):
        at = slice(begin, begin + rows)
        agg = mm(row_picks(target - begin, rows), pairs[...]).astype(BF)
        paired = jnp.concatenate([nl_v[at, :], nt_v[at, :]], 1)
        value, tangent = normed(mm(paired, fixed) + mm(agg, added), second, ones)
        first = (paired.astype(F32) + jnp.concatenate([value, tangent], 1)).astype(BF)
        first_o[at, :] = first
        part = part + mm(row_picks(owner[:, at], row_nodes), first)
    part_o[0:row_nodes, :] = part.astype(BF)
    high = (sources_v[...] // 256).astype(F32).astype(BF)
    low = lax.rem(sources_v[...], 256).astype(F32).astype(BF)
    lane = lax.broadcasted_iota(I32, (owned, 2 * width), 1)
    spot = lax.broadcasted_iota(I32, (owned, 2 * width), 0) + lax.axis_index("grp") * owned
    for k in range((part_o.shape[0] - row_nodes) // (2 * fan)):
        place = jnp.where(lane + k * 2 * width == spot, jnp.ones((), F32), jnp.zeros((), F32)).astype(BF)
        base = row_nodes + k * 2 * fan
        part_o[base : base + 2 * fan, :] = jnp.concatenate([mm(high, place), mm(low, place)], 0).astype(BF)


def coarse_kernel(summed, v0, v1, first, nc, own, mf, ms, cf, cs, pf, ps,
                  node_o, tangent_o,
                  own_v, mf_v, ms_v, cf_v, cs_v, pf_v, ps_v,
                  table, node_v, tangent_v, sems, out_sems, *, row_nodes, fan, rows):
    copies = fetch(
        list(zip(
            (mf, ms, cf, cs, pf, ps, own),
            (mf_v, ms_v, cf_v, cs_v, pf_v, ps_v, own_v),
        )),
        sems,
    )
    for copy in copies:
        copy.wait()
    slots, width = node_o.shape
    ones = averaging(width)
    mine = summed[0:row_nodes, :]
    weight = twice(mf_v[0:width, :])
    table[row_nodes : 2 * row_nodes, :] = mm(mine, weight).astype(BF)
    odd = lax.rem(lax.axis_index("dom"), 2)
    for k, got in enumerate((v0, v1)):
        place = 2 * odd if k else 2 - 2 * odd
        at = pl.ds(pl.multiple_of(place * row_nodes, row_nodes), row_nodes)
        table[at, :] = mm(got[0:row_nodes, :], weight).astype(BF)
    received = mm(mine, twice(mf_v[width:, :]))
    sums = []
    for begin in range(0, row_nodes, LANES):
        chunk, lanes = divmod(begin, 2 * width)
        base = row_nodes + chunk * 2 * fan
        spots = summed[base : base + 2 * fan, lanes : lanes + LANES].astype(F32)
        spots = (spots[0:fan, :] * 256.0 + spots[fan:, :]).astype(I32)
        got = received[begin : begin + LANES, :]
        selector = jnp.concatenate([column(spots[j : j + 1, :]) for j in range(fan)], 0)
        pre = mm(jnp.concatenate(picks(selector, 3 * row_nodes), 1), table[...])
        hidden = activated(pre + jnp.concatenate([got] * fan, 0))
        sums.append(sum(hidden[j * LANES : (j + 1) * LANES, :] for j in range(fan)))
    hidden = jnp.concatenate(sums, 0)
    weight = twice(ms_v[...])
    large = hidden.astype(BF)
    message = (mm(large, weight) + mm((hidden - large.astype(F32)).astype(BF), weight)).astype(BF)
    pre = mm(mine, twice(cf_v[0:width, :])) + mm(message, twice(cf_v[width:, :]))
    value, tangent = normed(pre, twice(centred(cs_v[...])), ones)
    updated = jnp.concatenate([value, tangent], 1).astype(BF)
    brought = mm(updated, twice(pf_v[width:, :])).astype(BF)
    fixed = twice(pf_v[0:width, :])
    second = twice(centred(ps_v[...]))
    stores = []
    for k, begin in enumerate(range(0, slots, rows)):
        at = slice(begin, begin + rows)
        selector = jnp.concatenate(picks(column(own_v[:, at]), row_nodes), 1)
        block = first[at, :]
        value, tangent = normed(mm(block, fixed) + mm(selector, brought), second, ones)
        valid = lax.broadcasted_iota(I32, (rows, 1), 0) + begin < nc[0]
        node_v[at, :] = jnp.where(valid, block[:, :width].astype(F32) + value, 0.0).astype(BF)
        tangent_v[at, :] = jnp.where(valid, block[:, width:].astype(F32) + tangent, 0.0).astype(BF)
        for i, (held, out) in enumerate(((node_v, node_o), (tangent_v, tangent_o))):
            copy = pltpu.make_async_copy(held.at[at], out.at[at], out_sems.at[2 * k + i])
            copy.start()
            stores.append(copy)
    for copy in stores:
        copy.wait()


def like(*arrays):
    return [pltpu.VMEM(a.shape, a.dtype) for a in arrays]


def params(mib=40):
    return pltpu.CompilerParams(vmem_limit_bytes=int(mib * 2**20))


def swap(x, axis, first):
    pairs = []
    for i in range(first, lax.axis_size(axis) - 1, 2):
        pairs += [(i, i + 1), (i + 1, i)]
    return lax.ppermute(x, axis, pairs)


def row_sum(x):
    size = lax.axis_size("grp")
    total = x.astype(F32)
    for by in range(1, size):
        if size & (size - 1) == 0:
            pairs = [(i, i ^ by) for i in range(size)]
        else:
            pairs = [(i, (i + by) % size) for i in range(size)]
        total = total + lax.ppermute(x, "grp", pairs).astype(F32)
    return total.astype(BF)


def per_device(nl, nt, ed, nc, ec, lists, src, tgt, own, sources, ef, es, nf, ns, mf, ms, cf, cs, pf, ps):
    slots, width = nl.shape
    edges = ed.shape[0]
    rim = lists.shape[2]
    owned, fan = sources.shape
    sources = sources.T
    row_nodes = owned * lax.axis_size("grp")
    extra = 2 * fan * (-(-row_nodes // (2 * width)))
    rows, block = min(slots, 256), min(edges, 512)
    shape = jax.ShapeDtypeStruct
    dma = pltpu.SemaphoreType.DMA
    sent = pl.pallas_call(
        halo_kernel,
        out_shape=[shape((rim, 2 * width), BF)] * 4,
        in_specs=[HBM] * 3,
        out_specs=[VMEM] * 4,
        scratch_shapes=like(nl, nt, lists) + [dma((3,))],
        compiler_params=params(60),
        name="halo_rows",
    )(nl, nt, lists)
    got = [swap(sent[k], ("dom", "grp")[k // 2], k % 2) for k in range(4)]
    pre = pl.pallas_call(
        functools.partial(local_kernel, block=block),
        out_shape=shape((edges, 2 * width), F32),
        in_specs=[HBM] * 5,
        out_specs=HBM,
        scratch_shapes=like(nl, nt, src, tgt, ef)
        + [
            pltpu.VMEM((2 * slots, 2 * width), BF),
            pltpu.VMEM((edges, 2 * width), F32),
            dma((5,)),
            dma((edges // block,)),
        ],
        compiler_params=params(59),
        cost_estimate=pl.CostEstimate(
            flops=8 * edges * slots * width, bytes_accessed=8 * edges * width, transcendentals=0
        ),
        name="local",
    )(nl, nt, src, tgt, ef)
    first, part = pl.pallas_call(
        functools.partial(edge_kernel, block=block, rows=rows),
        out_shape=[shape((slots, 2 * width), BF), shape((row_nodes + extra, 2 * width), BF)],
        in_specs=[HBM] * 11 + [SMEM] * 2 + [VMEM] * 4 + [HBM],
        out_specs=[VMEM] * 2,
        scratch_shapes=like(nl, nt, ed, src, tgt, own, sources)
        + like(ef, es, nf, ns)
        + [pltpu.VMEM((4 * rim, 2 * width), BF), pltpu.VMEM((edges, 2 * width), BF), pltpu.VMEM((edges, 2 * width), F32)]
        + [dma((11,)), dma((edges // block,))],
        compiler_params=params(51),
        name="edges",
    )(nl, nt, ed, src, tgt, own, sources, ef, es, nf, ns, nc, ec, *got, pre)
    summed = row_sum(part)
    v1, v0 = swap(summed, "dom", 1), swap(summed, "dom", 0)
    return pl.pallas_call(
        functools.partial(coarse_kernel, row_nodes=row_nodes, fan=fan, rows=rows),
        out_shape=[shape((slots, width), BF)] * 2,
        in_specs=[VMEM] * 4 + [SMEM] + [HBM] * 7,
        out_specs=[HBM] * 2,
        scratch_shapes=like(own)
        + like(mf, ms, cf, cs, pf, ps)
        + [
            pltpu.VMEM((3 * row_nodes, 2 * width), BF),
            pltpu.VMEM((slots, width), BF),
            pltpu.VMEM((slots, width), BF),
            dma((7,)),
            dma((2 * slots // rows,)),
        ],
        compiler_params=params(),
        name="coarse",
    )(summed, v0, v1, first, nc, own, mf, ms, cf, cs, pf, ps)


def solution(mesh):
    parts = ("dom", "grp")
    rows = P(parts, None)
    in_specs = (rows,) * 3 + (P(parts),) * 2 + (P(parts, None, None),) + (rows,) * 4 + (P(),) * 10
    return jax.shard_map(
        per_device, mesh=mesh, in_specs=in_specs, out_specs=(rows, rows), check_vma=False
    )
```

time: 58.3 us -> 52 us (0.89)
  local copies, waits for them, and re-layouts: 9.22 us -> 0.1 us
  Pallas kernels: 23.2 us -> 27.6 us
  starting transfers between devices: 17.4 us -> 16.4 us
    unnamed x39 -> x34, local copies, waits for them, and re-layouts: 9.22 us -> 0.1 us
    pallas_call x1 -> x2, Pallas kernels: 18.5 us -> 21.1 us  [the longest x1 14.1 us: per_device(): pl.pallas_call(functools.partial(edge_kernel, block=block, rows=rows), ou...]
    pallas_call x1, Pallas kernels: 0.57 us -> 2.2 us  [per_device(): pl.pallas_call(halo_kernel, out_shape=[shape((rim, 2 * width), BF)] * 4,...]
    ppermute x3, starting transfers between devices: 5.62 us -> 4.92 us  [row_sum(): total = total + lax.ppermute(x, 'grp', pairs).astype(F32)]
  transfers between devices with their start and end apart: 9 -> 9, of which waited for: 3 -> 3; matrix products, arithmetic and copies ran while one was open for 1% -> 0% of each run, Pallas kernels for 0% -> 14%
where the time goes in v2:
time: 52 us; the launch traced here: 51.8 us
  Pallas kernels  27.6 us (53%)
  starting transfers between devices  16.4 us (32%)
  waiting for transfers between devices  5.16 us (10%)
  between operations  2.48 us (5%)
    pallas_call x1, Pallas kernels, per_device(): pl.pallas_call(functools.partial(edge_kernel, block=block, rows=rows), ou...  14.1 us
    ppermute x6, starting transfers between devices, swap(): return lax.ppermute(x, axis, pairs)  11.5 us
    pallas_call x1, Pallas kernels, per_device(): pl.pallas_call(functools.partial(local_kernel, block=block), out_shape=sh...  7.02 us
    ppermute x3, starting transfers between devices, row_sum(): total = total + lax.ppermute(x, 'grp', pairs).astype(F32)  4.92 us
    pallas_call x1, Pallas kernels, per_device(): pl.pallas_call(functools.partial(coarse_kernel, row_nodes=row_nodes, fan=...  4.27 us
    ppermute x3, waiting for transfers between devices, row_sum(): total = total + lax.ppermute(x, 'grp', pairs).astype(F32)  3.2 us
    pallas_call x1, Pallas kernels, per_device(): pl.pallas_call(halo_kernel, out_shape=[shape((rim, 2 * width), BF)] * 4,...  2.2 us
    ppermute x6, waiting for transfers between devices, swap(): return lax.ppermute(x, axis, pairs)  1.96 us
  transfers between devices with their start and end apart: 9, of which 3 were waited for; matrix products, arithmetic and copies ran while one was open for 0% of the time, Pallas kernels for 14%

profile of v2, /device:TPU:1, one launch (start us, length us, event | category | flops | bytes accessed | tf_op | source)
XLA Modules:
  0.0 51.8 jit_solution(9105680556873659295)
XLA Ops:
  0.6 2.2 %halo_rows.1 = (bf16[128,256]{1,0:T(8,128)(2,1)}, bf16[128,256]{1,0:T(8,128)(2,1)}, bf16[128,256]{1,0:T(8,128)(2,1)}, bf16[128,256]{1,0:T(8,128)(2,1)}) custom-call(bf16[1024,128]{1,0:T(8,128)(2,1)} %nl.5, bf16[1024,128]{1,0:T(8,128)(2,1)} %nt.5, s32[1,4,128]{2,1,0:T(4,128)} %lists.1), custom_call_target="tpu_custom_call" | custom-call | tf_op jit(solution)/shard_map/halo_rows/pallas_call | solution.py:291
  2.8 0.1 collective-permute-start
  3.0 4.5 %collective-permute-start.1 = (bf16[128,256]{1,0:T(8,128)(2,1)}, bf16[128,256]{1,0:T(8,128)(2,1)S(1)}, u32[]{:S(2)}, u32[]{:S(2)}) collective-permute-start(bf16[128,256]{1,0:T(8,128)(2,1)} %get-tuple-element.9), channel_id=1, source_target_pairs={{4,8},{8,4},{12,16},{16,12},{20,24},{24,20},{5,9},{9,5},{13,17},{1... | collective-permute-start | bytes 196616 | tf_op jit(solution)/shard_map/ppermute | solution.py:265
  7.5 1.3 %collective-permute-start.2 = (bf16[128,256]{1,0:T(8,128)(2,1)}, bf16[128,256]{1,0:T(8,128)(2,1)S(1)}, u32[]{:S(2)}, u32[]{:S(2)}) collective-permute-start(bf16[128,256]{1,0:T(8,128)(2,1)} %get-tuple-element.10), channel_id=1, source_target_pairs={{0,1},{1,0},{2,3},{3,2},{4,5},{5,4},{6,7},{7,6},{8,9},{9,8},{10,11... | collective-permute-start | bytes 196616 | tf_op jit(solution)/shard_map/ppermute | solution.py:265
  8.8 0.0 copy-start.7
  8.8 0.0 copy-start.8
  8.8 0.0 copy-start.9
  8.8 0.0 copy-start.13
  8.8 0.0 copy-start.14
  8.9 0.0 copy-start.15
  8.9 0.0 copy-start.16
  8.9 0.8 %collective-permute-start.3 = (bf16[128,256]{1,0:T(8,128)(2,1)}, bf16[128,256]{1,0:T(8,128)(2,1)S(1)}, u32[]{:S(2)}, u32[]{:S(2)}) collective-permute-start(bf16[128,256]{1,0:T(8,128)(2,1)} %get-tuple-element.11), channel_id=1, source_target_pairs={{1,2},{2,1},{5,6},{6,5},{9,10},{10,9},{13,14},{14,13},{17,18},{18,... | collective-permute-start | bytes 196616 | tf_op jit(solution)/shard_map/ppermute | solution.py:265
  9.7 7.0 %local.1.pre = f32[4096,256]{1,0:T(8,128)} custom-call(bf16[1024,128]{1,0:T(8,128)(2,1)} %nl.5, bf16[1024,128]{1,0:T(8,128)(2,1)} %nt.5, s32[1,4096]{1,0:T(1,128)} %src.3, s32[1,4096]{1,0:T(1,128)} %tgt.3, bf16[384,128]{1,0:T(8,128)(2,1)} %ef.3), custom_call_target="tpu_custom_call" | custom-call | flops 4294967296 | bytes 4194304 | tf_op jit(solution)/shard_map/local/pallas_call | solution.py:301
  16.7 0.0 copy-start.4
  16.7 0.0 copy-start.5
  16.7 0.0 copy-start.6
  16.8 0.0 copy-start.10
  16.8 0.0 copy-start.11
  16.8 0.0 copy-start.12
  18.2 0.0 collective-permute-done.h0
  18.2 0.0 collective-permute-done.1.h1
  18.2 0.0 collective-permute-done.2.h2
  18.2 0.0 collective-permute-done.3.h3
  18.2 0.0 copy-done
  18.2 0.0 copy-done.1
  18.2 0.0 copy-done.2
  18.2 0.0 copy-done.3
  18.2 0.0 copy-done.7
  18.2 0.0 copy-done.8
  18.3 0.0 copy-done.9
  18.3 0.0 copy-done.13
  18.3 0.0 copy-done.14
  18.3 0.0 copy-done.15
  18.3 0.0 copy-done.16
  18.3 14.1 %edges.1 = (bf16[1024,256]{1,0:T(8,128)(2,1)S(1)}, bf16[144,256]{1,0:T(8,128)(2,1)S(1)}) custom-call(bf16[1024,128]{1,0:T(8,128)(2,1)S(1)} %copy-done.1, bf16[1024,128]{1,0:T(8,128)(2,1)S(1)} %copy-done.2, bf16[4096,128]{1,0:T(8,128)(2,1)S(1)} %copy-done, s32[1,4096]{1,0:T(1,128)S(1)} %copy-done.13, s32[1,4096]{1,0:T(1,128)S(1)} %copy-done.14, ...), custom_call_target="tpu_custom_call" | custom-call | tf_op jit(solution)/shard_map/edges/pallas_call | solution.py:319
  32.4 1.3 %collective-permute-start.6 = (bf16[144,256]{1,0:T(8,128)(2,1)S(1)}, bf16[144,256]{1,0:T(8,128)(2,1)S(1)}, u32[]{:S(2)}, u32[]{:S(2)}) collective-permute-start(bf16[144,256]{1,0:T(8,128)(2,1)S(1)} %get-tuple-element.12), channel_id=1, source_target_pairs={{0,3},{1,2},{2,1},{3,0},{4,7},{5,6},{6,5},{7,4},{8,11},{9,10},{10,... | collective-permute-start | bytes 221192 | tf_op jit(solution)/shard_map/ppermute | solution.py:276
  33.7 3.6 %collective-permute-start.5 = (bf16[144,256]{1,0:T(8,128)(2,1)S(1)}, bf16[144,256]{1,0:T(8,128)(2,1)S(1)}, u32[]{:S(2)}, u32[]{:S(2)}) collective-permute-start(bf16[144,256]{1,0:T(8,128)(2,1)S(1)} %get-tuple-element.12), channel_id=1, source_target_pairs={{0,2},{1,3},{2,0},{3,1},{4,6},{5,7},{6,4},{7,5},{8,10},{9,11},{10,... | collective-permute-start | bytes 221192 | tf_op jit(solution)/shard_map/ppermute | solution.py:276
  37.3 0.0 collective-permute-start.4
  37.3 0.0 collective-permute-done.6
  37.3 2.0 %collective-permute-done.5 = bf16[144,256]{1,0:T(8,128)(2,1)S(1)} collective-permute-done((bf16[144,256]{1,0:T(8,128)(2,1)S(1)}, bf16[144,256]{1,0:T(8,128)(2,1)S(1)}, u32[]{:S(2)}, u32[]{:S(2)}) %collective-permute-start.5) | collective-permute-done | bytes 73760 | tf_op jit(solution)/shard_map/ppermute | solution.py:276
  39.3 1.2 %collective-permute-done.4 = bf16[144,256]{1,0:T(8,128)(2,1)S(1)} collective-permute-done((bf16[144,256]{1,0:T(8,128)(2,1)S(1)}, bf16[144,256]{1,0:T(8,128)(2,1)S(1)}, u32[]{:S(2)}, u32[]{:S(2)}) %collective-permute-start.4) | collective-permute-done | bytes 73760 | tf_op jit(solution)/shard_map/ppermute | solution.py:276
  40.6 4.7 %collective-permute-start.8 = (bf16[144,256]{1,0:T(8,128)(2,1)S(1)}, bf16[144,256]{1,0:T(8,128)(2,1)S(1)}, u32[]{:S(2)}, u32[]{:S(2)}) collective-permute-start(bf16[144,256]{1,0:T(8,128)(2,1)S(1)} %add_convert_fusion.summed), channel_id=1, source_target_pairs={{4,8},{8,4},{12,16},{16,12},{20,24},{24,20},{5,9},{9,5},{13,17},{1... | collective-permute-start | bytes 221192 | tf_op jit(solution)/shard_map/ppermute | solution.py:265
  45.3 0.1 collective-permute-start.7
  45.4 1.9 %collective-permute-done.8.v1 = bf16[144,256]{1,0:T(8,128)(2,1)S(1)} collective-permute-done((bf16[144,256]{1,0:T(8,128)(2,1)S(1)}, bf16[144,256]{1,0:T(8,128)(2,1)S(1)}, u32[]{:S(2)}, u32[]{:S(2)}) %collective-permute-start.8) | collective-permute-done | bytes 73760 | tf_op jit(solution)/shard_map/ppermute | solution.py:265
  47.3 0.0 collective-permute-done.7.v0
  47.3 0.0 copy-done.5
  47.3 0.0 copy-done.6
  47.4 4.3 %coarse.1 = (bf16[1024,128]{1,0:T(8,128)(2,1)}, bf16[1024,128]{1,0:T(8,128)(2,1)}) custom-call(bf16[144,256]{1,0:T(8,128)(2,1)S(1)} %add_convert_fusion.summed, bf16[144,256]{1,0:T(8,128)(2,1)S(1)} %collective-permute-done.7.v0, bf16[144,256]{1,0:T(8,128)(2,1)S(1)} %collective-permute-done.8.v1, bf16[1024,256]{1,0:T(8,128)(2,1)S(1)} %get-tuple-element.13.first, ...), custom_call_target="tpu_custom_call" | custom-call | tf_op jit(solution)/shard_map/coarse/pallas_call | solution.py:333
  (9 shorter events, 0.1 us)
Async XLA Ops:
  2.8 15.3 %collective-permute-start = (bf16[128,256]{1,0:T(8,128)(2,1)}, bf16[128,256]{1,0:T(8,128)(2,1)S(1)}, u32[]{:S(2)}, u32[]{:S(2)}) collective-permute-start(bf16[128,256]{1,0:T(8,128)(2,1)} %get-tuple-element.8), channel_id=1, source_target_pairs={{0,4},{4,0},{8,12},{12,8},{16,20},{20,16},{24,28},{28,24},{1,5},{5... | collective-permute-start | bytes 196616 | tf_op jit(solution)/shard_map/ppermute | solution.py:265
  3.0 15.2 %collective-permute-start.1 = (bf16[128,256]{1,0:T(8,128)(2,1)}, bf16[128,256]{1,0:T(8,128)(2,1)S(1)}, u32[]{:S(2)}, u32[]{:S(2)}) collective-permute-start(bf16[128,256]{1,0:T(8,128)(2,1)} %get-tuple-element.9), channel_id=1, source_target_pairs={{4,8},{8,4},{12,16},{16,12},{20,24},{24,20},{5,9},{9,5},{13,17},{1... | collective-permute-start | bytes 196616 | tf_op jit(solution)/shard_map/ppermute | solution.py:265
  7.5 10.7 %collective-permute-start.2 = (bf16[128,256]{1,0:T(8,128)(2,1)}, bf16[128,256]{1,0:T(8,128)(2,1)S(1)}, u32[]{:S(2)}, u32[]{:S(2)}) collective-permute-start(bf16[128,256]{1,0:T(8,128)(2,1)} %get-tuple-element.10), channel_id=1, source_target_pairs={{0,1},{1,0},{2,3},{3,2},{4,5},{5,4},{6,7},{7,6},{8,9},{9,8},{10,11... | collective-permute-start | bytes 196616 | tf_op jit(solution)/shard_map/ppermute | solution.py:265
  8.8 9.4 %copy-start = (bf16[4096,128]{1,0:T(8,128)(2,1)S(1)}, bf16[4096,128]{1,0:T(8,128)(2,1)}, u32[]{:S(2)}) copy-start(bf16[4096,128]{1,0:T(8,128)(2,1)} %ed.1) | copy-start | bytes 3145732
  8.8 9.4 %copy-start.1 = (bf16[1024,128]{1,0:T(8,128)(2,1)S(1)}, bf16[1024,128]{1,0:T(8,128)(2,1)}, u32[]{:S(2)}) copy-start(bf16[1024,128]{1,0:T(8,128)(2,1)} %nl.5) | copy-start | bytes 786436
  8.8 9.4 %copy-start.2 = (bf16[1024,128]{1,0:T(8,128)(2,1)S(1)}, bf16[1024,128]{1,0:T(8,128)(2,1)}, u32[]{:S(2)}) copy-start(bf16[1024,128]{1,0:T(8,128)(2,1)} %nt.5) | copy-start | bytes 786436
  8.8 9.4 %copy-start.3 = (bf16[384,128]{1,0:T(8,128)(2,1)S(1)}, bf16[384,128]{1,0:T(8,128)(2,1)}, u32[]{:S(2)}) copy-start(bf16[384,128]{1,0:T(8,128)(2,1)} %ef.3) | copy-start | bytes 294916
  8.8 9.4 %copy-start.7 = (bf16[256,128]{1,0:T(8,128)(2,1)S(1)}, bf16[256,128]{1,0:T(8,128)(2,1)}, u32[]{:S(2)}) copy-start(bf16[256,128]{1,0:T(8,128)(2,1)} %nf.1) | copy-start | bytes 196612
  8.8 9.4 %copy-start.8 = (bf16[128,128]{1,0:T(8,128)(2,1)S(1)}, bf16[128,128]{1,0:T(8,128)(2,1)}, u32[]{:S(2)}) copy-start(bf16[128,128]{1,0:T(8,128)(2,1)} %es.1) | copy-start | bytes 98308
  8.8 9.4 %copy-start.9 = (bf16[128,128]{1,0:T(8,128)(2,1)S(1)}, bf16[128,128]{1,0:T(8,128)(2,1)}, u32[]{:S(2)}) copy-start(bf16[128,128]{1,0:T(8,128)(2,1)} %ns.1) | copy-start | bytes 98308
  8.8 9.4 %copy-start.13 = (s32[1,4096]{1,0:T(1,128)S(1)}, s32[1,4096]{1,0:T(1,128)}, u32[]{:S(2)}) copy-start(s32[1,4096]{1,0:T(1,128)} %src.3) | copy-start | bytes 49156
  8.8 9.4 %copy-start.14 = (s32[1,4096]{1,0:T(1,128)S(1)}, s32[1,4096]{1,0:T(1,128)}, u32[]{:S(2)}) copy-start(s32[1,4096]{1,0:T(1,128)} %tgt.3) | copy-start | bytes 49156
  8.9 9.4 %copy-start.15 = (s32[1,1024]{1,0:T(1,128)S(1)}, s32[1,1024]{1,0:T(1,128)}, u32[]{:S(2)}) copy-start(s32[1,1024]{1,0:T(1,128)} %own.3) | copy-start | bytes 12292
  8.9 9.4 %copy-start.16 = (s32[32,8]{0,1:T(8,128)S(1)}, s32[32,8]{0,1:T(8,128)}, u32[]{:S(2)}) copy-start(s32[32,8]{0,1:T(8,128)} %param.29) | copy-start | bytes 3076
  8.9 9.3 %collective-permute-start.3 = (bf16[128,256]{1,0:T(8,128)(2,1)}, bf16[128,256]{1,0:T(8,128)(2,1)S(1)}, u32[]{:S(2)}, u32[]{:S(2)}) collective-permute-start(bf16[128,256]{1,0:T(8,128)(2,1)} %get-tuple-element.11), channel_id=1, source_target_pairs={{1,2},{2,1},{5,6},{6,5},{9,10},{10,9},{13,14},{14,13},{17,18},{18,... | collective-permute-start | bytes 196616 | tf_op jit(solution)/shard_map/ppermute | solution.py:265
  16.7 30.6 %copy-start.4 = (bf16[256,128]{1,0:T(8,128)(2,1)S(1)}, bf16[256,128]{1,0:T(8,128)(2,1)}, u32[]{:S(2)}) copy-start(bf16[256,128]{1,0:T(8,128)(2,1)} %mf.1) | copy-start | bytes 196612
  16.7 30.6 %copy-start.5 = (bf16[256,128]{1,0:T(8,128)(2,1)S(1)}, bf16[256,128]{1,0:T(8,128)(2,1)}, u32[]{:S(2)}) copy-start(bf16[256,128]{1,0:T(8,128)(2,1)} %cf.1) | copy-start | bytes 196612
  16.7 30.6 %copy-start.6 = (bf16[256,128]{1,0:T(8,128)(2,1)S(1)}, bf16[256,128]{1,0:T(8,128)(2,1)}, u32[]{:S(2)}) copy-start(bf16[256,128]{1,0:T(8,128)(2,1)} %pf.1) | copy-start | bytes 196612
  16.8 30.6 %copy-start.10 = (bf16[128,128]{1,0:T(8,128)(2,1)S(1)}, bf16[128,128]{1,0:T(8,128)(2,1)}, u32[]{:S(2)}) copy-start(bf16[128,128]{1,0:T(8,128)(2,1)} %ms.1) | copy-start | bytes 98308
  16.8 30.6 %copy-start.11 = (bf16[128,128]{1,0:T(8,128)(2,1)S(1)}, bf16[128,128]{1,0:T(8,128)(2,1)}, u32[]{:S(2)}) copy-start(bf16[128,128]{1,0:T(8,128)(2,1)} %cs.1) | copy-start | bytes 98308
  16.8 30.6 %copy-start.12 = (bf16[128,128]{1,0:T(8,128)(2,1)S(1)}, bf16[128,128]{1,0:T(8,128)(2,1)}, u32[]{:S(2)}) copy-start(bf16[128,128]{1,0:T(8,128)(2,1)} %ps.1) | copy-start | bytes 98308
  32.4 4.9 %collective-permute-start.6 = (bf16[144,256]{1,0:T(8,128)(2,1)S(1)}, bf16[144,256]{1,0:T(8,128)(2,1)S(1)}, u32[]{:S(2)}, u32[]{:S(2)}) collective-permute-start(bf16[144,256]{1,0:T(8,128)(2,1)S(1)} %get-tuple-element.12), channel_id=1, source_target_pairs={{0,3},{1,2},{2,1},{3,0},{4,7},{5,6},{6,5},{7,4},{8,11},{9,10},{10,... | collective-permute-start | bytes 221192 | tf_op jit(solution)/shard_map/ppermute | solution.py:276
  33.7 5.7 %collective-permute-start.5 = (bf16[144,256]{1,0:T(8,128)(2,1)S(1)}, bf16[144,256]{1,0:T(8,128)(2,1)S(1)}, u32[]{:S(2)}, u32[]{:S(2)}) collective-permute-start(bf16[144,256]{1,0:T(8,128)(2,1)S(1)} %get-tuple-element.12), channel_id=1, source_target_pairs={{0,2},{1,3},{2,0},{3,1},{4,6},{5,7},{6,4},{7,5},{8,10},{9,11},{10,... | collective-permute-start | bytes 221192 | tf_op jit(solution)/shard_map/ppermute | solution.py:276
  37.3 3.2 %collective-permute-start.4 = (bf16[144,256]{1,0:T(8,128)(2,1)S(1)}, bf16[144,256]{1,0:T(8,128)(2,1)S(1)}, u32[]{:S(2)}, u32[]{:S(2)}) collective-permute-start(bf16[144,256]{1,0:T(8,128)(2,1)S(1)} %get-tuple-element.12), channel_id=1, source_target_pairs={{0,1},{1,0},{2,3},{3,2},{4,5},{5,4},{6,7},{7,6},{8,9},{9,8},{10,11... | collective-permute-start | bytes 221192 | tf_op jit(solution)/shard_map/ppermute | solution.py:276
  40.6 6.7 %collective-permute-start.8 = (bf16[144,256]{1,0:T(8,128)(2,1)S(1)}, bf16[144,256]{1,0:T(8,128)(2,1)S(1)}, u32[]{:S(2)}, u32[]{:S(2)}) collective-permute-start(bf16[144,256]{1,0:T(8,128)(2,1)S(1)} %add_convert_fusion.summed), channel_id=1, source_target_pairs={{4,8},{8,4},{12,16},{16,12},{20,24},{24,20},{5,9},{9,5},{13,17},{1... | collective-permute-start | bytes 221192 | tf_op jit(solution)/shard_map/ppermute | solution.py:265
  45.3 2.0 %collective-permute-start.7 = (bf16[144,256]{1,0:T(8,128)(2,1)S(1)}, bf16[144,256]{1,0:T(8,128)(2,1)S(1)}, u32[]{:S(2)}, u32[]{:S(2)}) collective-permute-start(bf16[144,256]{1,0:T(8,128)(2,1)S(1)} %add_convert_fusion.summed), channel_id=1, source_target_pairs={{0,4},{4,0},{8,12},{12,8},{16,20},{20,16},{24,28},{28,24},{1,5},{5... | collective-permute-start | bytes 221192 | tf_op jit(solution)/shard_map/ppermute | solution.py:265

commit v3 on v2

--- a/solution.py
+++ b/solution.py
@@ -54,19 +54,20 @@
     ]
 
 
-def row_picks(row, count):
-    shape = (count, row.shape[1])
-    return jnp.where(
-        jnp.broadcast_to(row, shape).astype(I16) == lax.broadcasted_iota(I32, shape, 0).astype(I16),
-        jnp.ones((), BF),
-        jnp.zeros((), BF),
-    )
+def row_picks(row, count, begin=0):
+    place = (lax.broadcasted_iota(I32, (count, LANES), 0) + begin).astype(I16)
+    one, zero = jnp.ones((), BF), jnp.zeros((), BF)
+    parts = []
+    for k in range(0, row.shape[1], LANES):
+        few = jnp.broadcast_to(row[:, k : k + LANES], (16, LANES)).astype(I16)
+        parts.append(jnp.where(jnp.concatenate([few] * (count // 16), 0) == place, one, zero))
+    return jnp.concatenate(parts, 1)
 
 
 def activated(pre):
     width = pre.shape[1] // 2
     value, tangent = pre[:, :width], pre[:, width:]
-    gate = 1.0 / (1.0 + jnp.exp(-value))
+    gate = 0.5 + 0.5 * jnp.tanh(0.5 * value)
     hidden = value * gate
     slope = gate + hidden * (1.0 - gate)
     return jnp.concatenate([hidden, tangent * slope], 1)
@@ -127,7 +128,7 @@
 def edge_kernel(nl, nt, ed, src, tgt, own, sources, ef, es, nf, ns, nc, ec, h0, h1, h2, h3, pre,
                 first_o, part_o,
                 nl_v, nt_v, ed_v, src_v, tgt_v, own_v, sources_v, ef_v, es_v, nf_v, ns_v,
-                table, pairs, pre_v, sems, pre_sems, *, block, rows):
+                table, pairs, sums, pre_v, sems, pre_sems, *, block, rows):
     copies = fetch(
         list(zip(
             (ef, src, es, ed, tgt, nl, nt, nf, ns, own, sources),
@@ -168,16 +169,13 @@
     second = twice(centred(ns_v[...]))
     fan, owned = sources.shape
     row_nodes = owned * lax.axis_size("grp")
-    part = jnp.zeros((row_nodes, 2 * width), F32)
     for begin in range(0, slots, rows):
-        at = slice(begin, begin + rows)
-        agg = mm(row_picks(target - begin, rows), pairs[...]).astype(BF)
-        paired = jnp.concatenate([nl_v[at, :], nt_v[at, :]], 1)
-        value, tangent = normed(mm(paired, fixed) + mm(agg, added), second, ones)
-        first = (paired.astype(F32) + jnp.concatenate([value, tangent], 1)).astype(BF)
-        first_o[at, :] = first
-        part = part + mm(row_picks(owner[:, at], row_nodes), first)
-    part_o[0:row_nodes, :] = part.astype(BF)
+        sums[begin : begin + rows, :] = mm(row_picks(target, rows, begin), pairs[...]).astype(BF)
+    paired = jnp.concatenate([nl_v[...], nt_v[...]], 1)
+    value, tangent = normed(mm(paired, fixed) + mm(sums[...], added), second, ones)
+    first = (paired.astype(F32) + jnp.concatenate([value, tangent], 1)).astype(BF)
+    first_o[...] = first
+    part_o[0:row_nodes, :] = mm(row_picks(owner, row_nodes), first).astype(BF)
     high = (sources_v[...] // 256).astype(F32).astype(BF)
     low = lax.rem(sources_v[...], 256).astype(F32).astype(BF)
     lane = lax.broadcasted_iota(I32, (owned, 2 * width), 1)
@@ -285,7 +283,7 @@
     sources = sources.T
     row_nodes = owned * lax.axis_size("grp")
     extra = 2 * fan * (-(-row_nodes // (2 * width)))
-    rows, block = min(slots, 256), min(edges, 512)
+    rows, block, cut = min(slots, 512), min(edges, 1024), min(edges, 512)
     shape = jax.ShapeDtypeStruct
     dma = pltpu.SemaphoreType.DMA
     sent = pl.pallas_call(
@@ -299,7 +297,7 @@
     )(nl, nt, lists)
     got = [swap(sent[k], ("dom", "grp")[k // 2], k % 2) for k in range(4)]
     pre = pl.pallas_call(
-        functools.partial(local_kernel, block=block),
+        functools.partial(local_kernel, block=cut),
         out_shape=shape((edges, 2 * width), F32),
         in_specs=[HBM] * 5,
         out_specs=HBM,
@@ -308,7 +306,7 @@
             pltpu.VMEM((2 * slots, 2 * width), BF),
             pltpu.VMEM((edges, 2 * width), F32),
             dma((5,)),
-            dma((edges // block,)),
+            dma((edges // cut,)),
         ],
         compiler_params=params(59),
         cost_estimate=pl.CostEstimate(
@@ -323,15 +321,15 @@
         out_specs=[VMEM] * 2,
         scratch_shapes=like(nl, nt, ed, src, tgt, own, sources)
         + like(ef, es, nf, ns)
-        + [pltpu.VMEM((4 * rim, 2 * width), BF), pltpu.VMEM((edges, 2 * width), BF), pltpu.VMEM((edges, 2 * width), F32)]
-        + [dma((11,)), dma((edges // block,))],
+        + [pltpu.VMEM((4 * rim, 2 * width), BF), pltpu.VMEM((edges, 2 * width), BF), pltpu.VMEM((slots, 2 * width), BF)]
+        + [pltpu.VMEM((edges, 2 * width), F32), dma((11,)), dma((edges // block,))],
         compiler_params=params(51),
         name="edges",
     )(nl, nt, ed, src, tgt, own, sources, ef, es, nf, ns, nc, ec, *got, pre)
     summed = row_sum(part)
     v1, v0 = swap(summed, "dom", 1), swap(summed, "dom", 0)
     return pl.pallas_call(
-        functools.partial(coarse_kernel, row_nodes=row_nodes, fan=fan, rows=rows),
+        functools.partial(coarse_kernel, row_nodes=row_nodes, fan=fan, rows=slots),
         out_shape=[shape((slots, width), BF)] * 2,
         in_specs=[VMEM] * 4 + [SMEM] + [HBM] * 7,
         out_specs=[HBM] * 2,
@@ -342,7 +340,7 @@
             pltpu.VMEM((slots, width), BF),
             pltpu.VMEM((slots, width), BF),
             dma((7,)),
-            dma((2 * slots // rows,)),
+            dma((2,)),
         ],
         compiler_params=params(),
         name="coarse",

time: 52 us -> 46.5 us (0.89)
  Pallas kernels: 27.6 us -> 22.2 us
    pallas_call x1, Pallas kernels: 14.1 us -> 9.18 us  [per_device(): pl.pallas_call(functools.partial(edge_kernel, block=block, rows=rows), ou...]
  transfers between devices with their start and end apart: 9 -> 9, of which waited for: 3 -> 3; matrix products, arithmetic and copies ran while one was open for 0% -> 0% of each run, Pallas kernels for 14% -> 15%
where the time goes in v3:
time: 46.5 us; the launch traced here: 46.2 us
  Pallas kernels  22.2 us (48%)
  starting transfers between devices  16.5 us (35%)
  waiting for transfers between devices  5.16 us (11%)
  between operations  2.32 us (5%)
    ppermute x6, starting transfers between devices, swap(): return lax.ppermute(x, axis, pairs)  11.5 us
    pallas_call x1, Pallas kernels, per_device(): pl.pallas_call(functools.partial(edge_kernel, block=block, rows=rows), ou...  9.18 us
    pallas_call x1, Pallas kernels, per_device(): pl.pallas_call(functools.partial(local_kernel, block=cut), out_shape=shap...  7.02 us
    ppermute x3, starting transfers between devices, row_sum(): total = total + lax.ppermute(x, 'grp', pairs).astype(F32)  4.92 us
    pallas_call x1, Pallas kernels, per_device(): pl.pallas_call(functools.partial(coarse_kernel, row_nodes=row_nodes, fan=...  3.78 us
    ppermute x3, waiting for transfers between devices, row_sum(): total = total + lax.ppermute(x, 'grp', pairs).astype(F32)  3.2 us
    pallas_call x1, Pallas kernels, per_device(): pl.pallas_call(halo_kernel, out_shape=[shape((rim, 2 * width), BF)] * 4,...  2.2 us
    ppermute x6, waiting for transfers between devices, swap(): return lax.ppermute(x, axis, pairs)  1.96 us
  transfers between devices with their start and end apart: 9, of which 3 were waited for; matrix products, arithmetic and copies ran while one was open for 0% of the time, Pallas kernels for 15%

profile of v3, /device:TPU:1, one launch (start us, length us, event | category | flops | bytes accessed | tf_op | source)
XLA Modules:
  0.0 46.2 jit_solution(6660240011380720692)
XLA Ops:
  0.6 2.2 %halo_rows.1 = (bf16[128,256]{1,0:T(8,128)(2,1)}, bf16[128,256]{1,0:T(8,128)(2,1)}, bf16[128,256]{1,0:T(8,128)(2,1)}, bf16[128,256]{1,0:T(8,128)(2,1)}) custom-call(bf16[1024,128]{1,0:T(8,128)(2,1)} %nl.5, bf16[1024,128]{1,0:T(8,128)(2,1)} %nt.5, s32[1,4,128]{2,1,0:T(4,128)} %lists.1), custom_call_target="tpu_custom_call" | custom-call | tf_op jit(solution)/shard_map/halo_rows/pallas_call | solution.py:289
  2.8 0.1 collective-permute-start
  3.0 4.5 %collective-permute-start.1 = (bf16[128,256]{1,0:T(8,128)(2,1)}, bf16[128,256]{1,0:T(8,128)(2,1)S(1)}, u32[]{:S(2)}, u32[]{:S(2)}) collective-permute-start(bf16[128,256]{1,0:T(8,128)(2,1)} %get-tuple-element.9), channel_id=1, source_target_pairs={{4,8},{8,4},{12,16},{16,12},{20,24},{24,20},{5,9},{9,5},{13,17},{1... | collective-permute-start | bytes 196616 | tf_op jit(solution)/shard_map/ppermute | solution.py:263
  7.5 1.3 %collective-permute-start.2 = (bf16[128,256]{1,0:T(8,128)(2,1)}, bf16[128,256]{1,0:T(8,128)(2,1)S(1)}, u32[]{:S(2)}, u32[]{:S(2)}) collective-permute-start(bf16[128,256]{1,0:T(8,128)(2,1)} %get-tuple-element.10), channel_id=1, source_target_pairs={{0,1},{1,0},{2,3},{3,2},{4,5},{5,4},{6,7},{7,6},{8,9},{9,8},{10,11... | collective-permute-start | bytes 196616 | tf_op jit(solution)/shard_map/ppermute | solution.py:263
  8.8 0.0 copy-start.7
  8.8 0.0 copy-start.8
  8.8 0.0 copy-start.9
  8.8 0.0 copy-start.13
  8.8 0.0 copy-start.14
  8.9 0.0 copy-start.15
  8.9 0.0 copy-start.16
  8.9 0.8 %collective-permute-start.3 = (bf16[128,256]{1,0:T(8,128)(2,1)}, bf16[128,256]{1,0:T(8,128)(2,1)S(1)}, u32[]{:S(2)}, u32[]{:S(2)}) collective-permute-start(bf16[128,256]{1,0:T(8,128)(2,1)} %get-tuple-element.11), channel_id=1, source_target_pairs={{1,2},{2,1},{5,6},{6,5},{9,10},{10,9},{13,14},{14,13},{17,18},{18,... | collective-permute-start | bytes 196616 | tf_op jit(solution)/shard_map/ppermute | solution.py:263
  9.7 7.0 %local.1.pre = f32[4096,256]{1,0:T(8,128)} custom-call(bf16[1024,128]{1,0:T(8,128)(2,1)} %nl.5, bf16[1024,128]{1,0:T(8,128)(2,1)} %nt.5, s32[1,4096]{1,0:T(1,128)} %src.3, s32[1,4096]{1,0:T(1,128)} %tgt.3, bf16[384,128]{1,0:T(8,128)(2,1)} %ef.3), custom_call_target="tpu_custom_call" | custom-call | flops 4294967296 | bytes 4194304 | tf_op jit(solution)/shard_map/local/pallas_call | solution.py:299
  16.7 0.0 copy-start.4
  16.7 0.0 copy-start.5
  16.7 0.0 copy-start.6
  16.8 0.0 copy-start.10
  16.8 0.0 copy-start.11
  16.8 0.0 copy-start.12
  18.2 0.0 collective-permute-done.h0
  18.2 0.0 collective-permute-done.1.h1
  18.2 0.0 collective-permute-done.2.h2
  18.2 0.0 collective-permute-done.3.h3
  18.2 0.0 copy-done
  18.2 0.0 copy-done.1
  18.2 0.0 copy-done.2
  18.2 0.0 copy-done.3
  18.2 0.0 copy-done.7
  18.2 0.0 copy-done.8
  18.3 0.0 copy-done.9
  18.3 0.0 copy-done.13
  18.3 0.0 copy-done.14
  18.3 0.0 copy-done.15
  18.3 0.0 copy-done.16
  18.3 9.2 %edges.1 = (bf16[1024,256]{1,0:T(8,128)(2,1)S(1)}, bf16[144,256]{1,0:T(8,128)(2,1)S(1)}) custom-call(bf16[1024,128]{1,0:T(8,128)(2,1)S(1)} %copy-done.1, bf16[1024,128]{1,0:T(8,128)(2,1)S(1)} %copy-done.2, bf16[4096,128]{1,0:T(8,128)(2,1)S(1)} %copy-done, s32[1,4096]{1,0:T(1,128)S(1)} %copy-done.13, s32[1,4096]{1,0:T(1,128)S(1)} %copy-done.14, ...), custom_call_target="tpu_custom_call" | custom-call | tf_op jit(solution)/shard_map/edges/pallas_call | solution.py:317
  27.5 1.3 %collective-permute-start.6 = (bf16[144,256]{1,0:T(8,128)(2,1)S(1)}, bf16[144,256]{1,0:T(8,128)(2,1)S(1)}, u32[]{:S(2)}, u32[]{:S(2)}) collective-permute-start(bf16[144,256]{1,0:T(8,128)(2,1)S(1)} %get-tuple-element.12), channel_id=1, source_target_pairs={{0,3},{1,2},{2,1},{3,0},{4,7},{5,6},{6,5},{7,4},{8,11},{9,10},{10,... | collective-permute-start | bytes 221192 | tf_op jit(solution)/shard_map/ppermute | solution.py:274
  28.8 3.6 %collective-permute-start.5 = (bf16[144,256]{1,0:T(8,128)(2,1)S(1)}, bf16[144,256]{1,0:T(8,128)(2,1)S(1)}, u32[]{:S(2)}, u32[]{:S(2)}) collective-permute-start(bf16[144,256]{1,0:T(8,128)(2,1)S(1)} %get-tuple-element.12), channel_id=1, source_target_pairs={{0,2},{1,3},{2,0},{3,1},{4,6},{5,7},{6,4},{7,5},{8,10},{9,11},{10,... | collective-permute-start | bytes 221192 | tf_op jit(solution)/shard_map/ppermute | solution.py:274
  32.4 0.0 collective-permute-start.4
  32.4 0.0 collective-permute-done.6
  32.4 2.0 %collective-permute-done.5 = bf16[144,256]{1,0:T(8,128)(2,1)S(1)} collective-permute-done((bf16[144,256]{1,0:T(8,128)(2,1)S(1)}, bf16[144,256]{1,0:T(8,128)(2,1)S(1)}, u32[]{:S(2)}, u32[]{:S(2)}) %collective-permute-start.5) | collective-permute-done | bytes 73760 | tf_op jit(solution)/shard_map/ppermute | solution.py:274
  34.4 1.2 %collective-permute-done.4 = bf16[144,256]{1,0:T(8,128)(2,1)S(1)} collective-permute-done((bf16[144,256]{1,0:T(8,128)(2,1)S(1)}, bf16[144,256]{1,0:T(8,128)(2,1)S(1)}, u32[]{:S(2)}, u32[]{:S(2)}) %collective-permute-start.4) | collective-permute-done | bytes 73760 | tf_op jit(solution)/shard_map/ppermute | solution.py:274
  35.7 4.7 %collective-permute-start.8 = (bf16[144,256]{1,0:T(8,128)(2,1)S(1)}, bf16[144,256]{1,0:T(8,128)(2,1)S(1)}, u32[]{:S(2)}, u32[]{:S(2)}) collective-permute-start(bf16[144,256]{1,0:T(8,128)(2,1)S(1)} %add_convert_fusion.summed), channel_id=1, source_target_pairs={{4,8},{8,4},{12,16},{16,12},{20,24},{24,20},{5,9},{9,5},{13,17},{1... | collective-permute-start | bytes 221192 | tf_op jit(solution)/shard_map/ppermute | solution.py:263
  40.4 0.1 collective-permute-start.7
  40.5 1.9 %collective-permute-done.8.v1 = bf16[144,256]{1,0:T(8,128)(2,1)S(1)} collective-permute-done((bf16[144,256]{1,0:T(8,128)(2,1)S(1)}, bf16[144,256]{1,0:T(8,128)(2,1)S(1)}, u32[]{:S(2)}, u32[]{:S(2)}) %collective-permute-start.8) | collective-permute-done | bytes 73760 | tf_op jit(solution)/shard_map/ppermute | solution.py:263
  42.4 0.0 collective-permute-done.7.v0
  42.4 0.0 copy-done.5
  42.4 0.0 copy-done.6
  42.5 3.8 %coarse.1 = (bf16[1024,128]{1,0:T(8,128)(2,1)}, bf16[1024,128]{1,0:T(8,128)(2,1)}) custom-call(bf16[144,256]{1,0:T(8,128)(2,1)S(1)} %add_convert_fusion.summed, bf16[144,256]{1,0:T(8,128)(2,1)S(1)} %collective-permute-done.7.v0, bf16[144,256]{1,0:T(8,128)(2,1)S(1)} %collective-permute-done.8.v1, bf16[1024,256]{1,0:T(8,128)(2,1)S(1)} %get-tuple-element.13.first, ...), custom_call_target="tpu_custom_call" | custom-call | tf_op jit(solution)/shard_map/coarse/pallas_call | solution.py:331
  (9 shorter events, 0.1 us)
Async XLA Ops:
  2.8 15.3 %collective-permute-start = (bf16[128,256]{1,0:T(8,128)(2,1)}, bf16[128,256]{1,0:T(8,128)(2,1)S(1)}, u32[]{:S(2)}, u32[]{:S(2)}) collective-permute-start(bf16[128,256]{1,0:T(8,128)(2,1)} %get-tuple-element.8), channel_id=1, source_target_pairs={{0,4},{4,0},{8,12},{12,8},{16,20},{20,16},{24,28},{28,24},{1,5},{5... | collective-permute-start | bytes 196616 | tf_op jit(solution)/shard_map/ppermute | solution.py:263
  3.0 15.2 %collective-permute-start.1 = (bf16[128,256]{1,0:T(8,128)(2,1)}, bf16[128,256]{1,0:T(8,128)(2,1)S(1)}, u32[]{:S(2)}, u32[]{:S(2)}) collective-permute-start(bf16[128,256]{1,0:T(8,128)(2,1)} %get-tuple-element.9), channel_id=1, source_target_pairs={{4,8},{8,4},{12,16},{16,12},{20,24},{24,20},{5,9},{9,5},{13,17},{1... | collective-permute-start | bytes 196616 | tf_op jit(solution)/shard_map/ppermute | solution.py:263
  7.5 10.7 %collective-permute-start.2 = (bf16[128,256]{1,0:T(8,128)(2,1)}, bf16[128,256]{1,0:T(8,128)(2,1)S(1)}, u32[]{:S(2)}, u32[]{:S(2)}) collective-permute-start(bf16[128,256]{1,0:T(8,128)(2,1)} %get-tuple-element.10), channel_id=1, source_target_pairs={{0,1},{1,0},{2,3},{3,2},{4,5},{5,4},{6,7},{7,6},{8,9},{9,8},{10,11... | collective-permute-start | bytes 196616 | tf_op jit(solution)/shard_map/ppermute | solution.py:263
  8.8 9.4 %copy-start = (bf16[4096,128]{1,0:T(8,128)(2,1)S(1)}, bf16[4096,128]{1,0:T(8,128)(2,1)}, u32[]{:S(2)}) copy-start(bf16[4096,128]{1,0:T(8,128)(2,1)} %ed.1) | copy-start | bytes 3145732
  8.8 9.4 %copy-start.1 = (bf16[1024,128]{1,0:T(8,128)(2,1)S(1)}, bf16[1024,128]{1,0:T(8,128)(2,1)}, u32[]{:S(2)}) copy-start(bf16[1024,128]{1,0:T(8,128)(2,1)} %nl.5) | copy-start | bytes 786436
  8.8 9.4 %copy-start.2 = (bf16[1024,128]{1,0:T(8,128)(2,1)S(1)}, bf16[1024,128]{1,0:T(8,128)(2,1)}, u32[]{:S(2)}) copy-start(bf16[1024,128]{1,0:T(8,128)(2,1)} %nt.5) | copy-start | bytes 786436
  8.8 9.4 %copy-start.3 = (bf16[384,128]{1,0:T(8,128)(2,1)S(1)}, bf16[384,128]{1,0:T(8,128)(2,1)}, u32[]{:S(2)}) copy-start(bf16[384,128]{1,0:T(8,128)(2,1)} %ef.3) | copy-start | bytes 294916
  8.8 9.4 %copy-start.7 = (bf16[256,128]{1,0:T(8,128)(2,1)S(1)}, bf16[256,128]{1,0:T(8,128)(2,1)}, u32[]{:S(2)}) copy-start(bf16[256,128]{1,0:T(8,128)(2,1)} %nf.1) | copy-start | bytes 196612
  8.8 9.4 %copy-start.8 = (bf16[128,128]{1,0:T(8,128)(2,1)S(1)}, bf16[128,128]{1,0:T(8,128)(2,1)}, u32[]{:S(2)}) copy-start(bf16[128,128]{1,0:T(8,128)(2,1)} %es.1) | copy-start | bytes 98308
  8.8 9.4 %copy-start.9 = (bf16[128,128]{1,0:T(8,128)(2,1)S(1)}, bf16[128,128]{1,0:T(8,128)(2,1)}, u32[]{:S(2)}) copy-start(bf16[128,128]{1,0:T(8,128)(2,1)} %ns.1) | copy-start | bytes 98308
  8.8 9.4 %copy-start.13 = (s32[1,4096]{1,0:T(1,128)S(1)}, s32[1,4096]{1,0:T(1,128)}, u32[]{:S(2)}) copy-start(s32[1,4096]{1,0:T(1,128)} %src.3) | copy-start | bytes 49156
  8.8 9.4 %copy-start.14 = (s32[1,4096]{1,0:T(1,128)S(1)}, s32[1,4096]{1,0:T(1,128)}, u32[]{:S(2)}) copy-start(s32[1,4096]{1,0:T(1,128)} %tgt.3) | copy-start | bytes 49156
  8.9 9.4 %copy-start.15 = (s32[1,1024]{1,0:T(1,128)S(1)}, s32[1,1024]{1,0:T(1,128)}, u32[]{:S(2)}) copy-start(s32[1,1024]{1,0:T(1,128)} %own.3) | copy-start | bytes 12292
  8.9 9.4 %copy-start.16 = (s32[32,8]{0,1:T(8,128)S(1)}, s32[32,8]{0,1:T(8,128)}, u32[]{:S(2)}) copy-start(s32[32,8]{0,1:T(8,128)} %param.29) | copy-start | bytes 3076
  8.9 9.3 %collective-permute-start.3 = (bf16[128,256]{1,0:T(8,128)(2,1)}, bf16[128,256]{1,0:T(8,128)(2,1)S(1)}, u32[]{:S(2)}, u32[]{:S(2)}) collective-permute-start(bf16[128,256]{1,0:T(8,128)(2,1)} %get-tuple-element.11), channel_id=1, source_target_pairs={{1,2},{2,1},{5,6},{6,5},{9,10},{10,9},{13,14},{14,13},{17,18},{18,... | collective-permute-start | bytes 196616 | tf_op jit(solution)/shard_map/ppermute | solution.py:263
  16.7 25.7 %copy-start.4 = (bf16[256,128]{1,0:T(8,128)(2,1)S(1)}, bf16[256,128]{1,0:T(8,128)(2,1)}, u32[]{:S(2)}) copy-start(bf16[256,128]{1,0:T(8,128)(2,1)} %mf.1) | copy-start | bytes 196612
  16.7 25.7 %copy-start.5 = (bf16[256,128]{1,0:T(8,128)(2,1)S(1)}, bf16[256,128]{1,0:T(8,128)(2,1)}, u32[]{:S(2)}) copy-start(bf16[256,128]{1,0:T(8,128)(2,1)} %cf.1) | copy-start | bytes 196612
  16.7 25.7 %copy-start.6 = (bf16[256,128]{1,0:T(8,128)(2,1)S(1)}, bf16[256,128]{1,0:T(8,128)(2,1)}, u32[]{:S(2)}) copy-start(bf16[256,128]{1,0:T(8,128)(2,1)} %pf.1) | copy-start | bytes 196612
  16.8 25.7 %copy-start.10 = (bf16[128,128]{1,0:T(8,128)(2,1)S(1)}, bf16[128,128]{1,0:T(8,128)(2,1)}, u32[]{:S(2)}) copy-start(bf16[128,128]{1,0:T(8,128)(2,1)} %ms.1) | copy-start | bytes 98308
  16.8 25.7 %copy-start.11 = (bf16[128,128]{1,0:T(8,128)(2,1)S(1)}, bf16[128,128]{1,0:T(8,128)(2,1)}, u32[]{:S(2)}) copy-start(bf16[128,128]{1,0:T(8,128)(2,1)} %cs.1) | copy-start | bytes 98308
  16.8 25.7 %copy-start.12 = (bf16[128,128]{1,0:T(8,128)(2,1)S(1)}, bf16[128,128]{1,0:T(8,128)(2,1)}, u32[]{:S(2)}) copy-start(bf16[128,128]{1,0:T(8,128)(2,1)} %ps.1) | copy-start | bytes 98308
  27.5 4.9 %collective-permute-start.6 = (bf16[144,256]{1,0:T(8,128)(2,1)S(1)}, bf16[144,256]{1,0:T(8,128)(2,1)S(1)}, u32[]{:S(2)}, u32[]{:S(2)}) collective-permute-start(bf16[144,256]{1,0:T(8,128)(2,1)S(1)} %get-tuple-element.12), channel_id=1, source_target_pairs={{0,3},{1,2},{2,1},{3,0},{4,7},{5,6},{6,5},{7,4},{8,11},{9,10},{10,... | collective-permute-start | bytes 221192 | tf_op jit(solution)/shard_map/ppermute | solution.py:274
  28.8 5.7 %collective-permute-start.5 = (bf16[144,256]{1,0:T(8,128)(2,1)S(1)}, bf16[144,256]{1,0:T(8,128)(2,1)S(1)}, u32[]{:S(2)}, u32[]{:S(2)}) collective-permute-start(bf16[144,256]{1,0:T(8,128)(2,1)S(1)} %get-tuple-element.12), channel_id=1, source_target_pairs={{0,2},{1,3},{2,0},{3,1},{4,6},{5,7},{6,4},{7,5},{8,10},{9,11},{10,... | collective-permute-start | bytes 221192 | tf_op jit(solution)/shard_map/ppermute | solution.py:274
  32.4 3.2 %collective-permute-start.4 = (bf16[144,256]{1,0:T(8,128)(2,1)S(1)}, bf16[144,256]{1,0:T(8,128)(2,1)S(1)}, u32[]{:S(2)}, u32[]{:S(2)}) collective-permute-start(bf16[144,256]{1,0:T(8,128)(2,1)S(1)} %get-tuple-element.12), channel_id=1, source_target_pairs={{0,1},{1,0},{2,3},{3,2},{4,5},{5,4},{6,7},{7,6},{8,9},{9,8},{10,11... | collective-permute-start | bytes 221192 | tf_op jit(solution)/shard_map/ppermute | solution.py:274
  35.7 6.8 %collective-permute-start.8 = (bf16[144,256]{1,0:T(8,128)(2,1)S(1)}, bf16[144,256]{1,0:T(8,128)(2,1)S(1)}, u32[]{:S(2)}, u32[]{:S(2)}) collective-permute-start(bf16[144,256]{1,0:T(8,128)(2,1)S(1)} %add_convert_fusion.summed), channel_id=1, source_target_pairs={{4,8},{8,4},{12,16},{16,12},{20,24},{24,20},{5,9},{9,5},{13,17},{1... | collective-permute-start | bytes 221192 | tf_op jit(solution)/shard_map/ppermute | solution.py:263
  40.4 2.0 %collective-permute-start.7 = (bf16[144,256]{1,0:T(8,128)(2,1)S(1)}, bf16[144,256]{1,0:T(8,128)(2,1)S(1)}, u32[]{:S(2)}, u32[]{:S(2)}) collective-permute-start(bf16[144,256]{1,0:T(8,128)(2,1)S(1)} %add_convert_fusion.summed), channel_id=1, source_target_pairs={{0,4},{4,0},{8,12},{12,8},{16,20},{20,16},{24,28},{28,24},{1,5},{5... | collective-permute-start | bytes 221192 | tf_op jit(solution)/shard_map/ppermute | solution.py:263

commit v4 on v3

v4 whole, which is shorter than its diff:
```python
import functools

import jax
import jax.numpy as jnp
from jax import lax
from jax.experimental import pallas as pl
from jax.experimental.pallas import tpu as pltpu
from jax.sharding import PartitionSpec as P

BF = jnp.bfloat16
F32 = jnp.float32
I16 = jnp.int16
I32 = jnp.int32
HBM = pl.BlockSpec(memory_space=pltpu.HBM)
SMEM = pl.BlockSpec(memory_space=pltpu.SMEM)
VMEM = pl.BlockSpec(memory_space=pltpu.VMEM)
LANES = 128


def mm(a, b):
    return jnp.dot(a, b, preferred_element_type=F32)


def twice(weight):
    zero = jnp.zeros_like(weight)
    return jnp.concatenate(
        [jnp.concatenate([weight, zero], 1), jnp.concatenate([zero, weight], 1)], 0
    )


def centred(weight):
    weight = weight.astype(F32)
    return (weight - jnp.mean(weight, axis=1, keepdims=True)).astype(BF)


def averaging(width):
    return twice(jnp.full((width, width), 1.0 / width, BF))


def column(row):
    count = row.shape[1]
    parts = [
        jnp.broadcast_to(row[:, k : k + LANES], (LANES, LANES)).T for k in range(0, count, LANES)
    ]
    return jnp.concatenate(parts, 0).astype(I16)


def picks(col, count):
    lane = lax.broadcasted_iota(I32, (1, LANES), 1).astype(I16)
    one, zero = jnp.ones((), BF), jnp.zeros((), BF)
    return [
        jnp.where(col == jnp.broadcast_to(lane + jnp.asarray(k, I16), col.shape), one, zero)
        for k in range(0, count, LANES)
    ]


def row_picks(row, count, begin=0):
    place = (lax.broadcasted_iota(I32, (count, LANES), 0) + begin).astype(I16)
    one, zero = jnp.ones((), BF), jnp.zeros((), BF)
    parts = []
    for k in range(0, row.shape[1], LANES):
        few = jnp.broadcast_to(row[:, k : k + LANES], (16, LANES)).astype(I16)
        parts.append(jnp.where(jnp.concatenate([few] * (count // 16), 0) == place, one, zero))
    return jnp.concatenate(parts, 1)


def activated(pre):
    width = pre.shape[1] // 2
    value, tangent = pre[:, :width], pre[:, width:]
    gate = 0.5 + 0.5 * jnp.tanh(0.5 * value)
    hidden = value * gate
    slope = gate + hidden * (1.0 - gate)
    return jnp.concatenate([hidden, tangent * slope], 1)


def normed(pre, second, ones):
    width = pre.shape[1] // 2
    both = mm(activated(pre).astype(BF), second)
    value, tangent = both[:, :width], both[:, width:]
    stats = mm(jnp.concatenate([value * value, value * tangent], 1).astype(BF), ones)
    scale = lax.rsqrt(stats[:, :width] + 1e-05)
    return value * scale, scale * (tangent - value * (scale * scale * stats[:, width:]))


def fetch(pairs, sems):
    copies = [pltpu.make_async_copy(src, dst, sems.at[k]) for k, (src, dst) in enumerate(pairs)]
    for copy in copies:
        copy.start()
    return copies


def halo_kernel(nl, nt, lists, o0, o1, o2, o3, nl_v, nt_v, lists_v, sent_v, sems, out_sems):
    for copy in fetch([(lists, lists_v), (nl, nl_v), (nt, nt_v)], sems):
        copy.wait()
    slots = nl.shape[0]
    rim = o0.shape[0]
    paired = jnp.concatenate([nl_v[...], nt_v[...]], 1)
    even = (lax.rem(lax.axis_index("dom"), 2) == 0, lax.rem(lax.axis_index("grp"), 2) == 0)
    stores = []
    for k, out in enumerate((o0, o1, o2, o3)):
        base = k // 2 * 2
        up = even[k // 2] if k % 2 == 0 else jnp.logical_not(even[k // 2])
        row = jnp.where(up, lists_v[0, base : base + 1, :], lists_v[0, base + 1 : base + 2, :])
        selector = jnp.concatenate(picks(column(row), slots), 1)
        at = slice(k * rim, (k + 1) * rim)
        sent_v[at, :] = mm(selector, paired).astype(BF)
        copy = pltpu.make_async_copy(sent_v.at[at], out, out_sems.at[k])
        copy.start()
        stores.append(copy)
    for copy in stores:
        copy.wait()


def local_kernel(nl, nt, src, tgt, ef, pre_o, table, *, block):
    slots, width = nl.shape
    paired = jnp.concatenate([nl[...], nt[...]], 1)
    table[0:slots, :] = mm(paired, twice(ef[width : 2 * width, :])).astype(BF)
    table[slots:, :] = mm(paired, twice(ef[2 * width :, :])).astype(BF)
    for begin in range(0, pre_o.shape[0], block):
        at = slice(begin, begin + block)
        selector = jnp.concatenate(
            picks(column(src[0:1, at]), slots) + picks(column(tgt[0:1, at]), slots), 1
        )
        pre_o[at, :] = mm(selector, table[...])


def edge_kernel(nl_v, nt_v, ed_v, src_v, tgt_v, own_v, sources_v, ef_v, es_v, nf_v, ns_v, nc, ec,
                h0, h1, h2, h3, pre, first_o, part_o, table, pairs, sums, *, block, rows):
    slots, width = nl_v.shape
    edges = ed_v.shape[0]
    rim = h0.shape[0]
    weight = twice(ef_v[width : 2 * width, :])
    odd = (lax.rem(lax.axis_index("dom"), 2), lax.rem(lax.axis_index("grp"), 2))
    for k, got in enumerate((h0, h1, h2, h3)):
        place = k // 2 * 2 + (odd[k // 2] if k % 2 else 1 - odd[k // 2])
        at = pl.ds(pl.multiple_of(place * rim, rim), rim)
        table[at, :] = mm(got[...], weight).astype(BF)
    second = twice(centred(es_v[...]))
    ones = averaging(width)
    own_weight = ef_v[0:width, :]
    for begin in range(0, edges, block):
        at = slice(begin, begin + block)
        selector = jnp.concatenate(picks(column(src_v[0:1, at] - slots), 4 * rim), 1)
        mine = ed_v[at, :]
        given = pre[at, :] + mm(selector, table[...])
        given = jnp.concatenate([given[:, :width] + mm(mine, own_weight), given[:, width:]], 1)
        value, tangent = normed(given, second, ones)
        pairs[at, :] = jnp.concatenate([mine.astype(F32) + value, tangent], 1).astype(BF)
    target = jnp.where(lax.broadcasted_iota(I32, (1, edges), 1) < ec[0], tgt_v[...], -1)
    owner = jnp.where(lax.broadcasted_iota(I32, (1, slots), 1) < nc[0], own_v[...], -1)
    fixed = twice(nf_v[0:width, :])
    added = twice(nf_v[width:, :])
    second = twice(centred(ns_v[...]))
    fan, owned = sources_v.shape
    row_nodes = owned * lax.axis_size("grp")
    for begin in range(0, slots, rows):
        sums[begin : begin + rows, :] = mm(row_picks(target, rows, begin), pairs[...]).astype(BF)
    paired = jnp.concatenate([nl_v[...], nt_v[...]], 1)
    value, tangent = normed(mm(paired, fixed) + mm(sums[...], added), second, ones)
    first = (paired.astype(F32) + jnp.concatenate([value, tangent], 1)).astype(BF)
    first_o[...] = first
    part_o[0:row_nodes, :] = mm(row_picks(owner, row_nodes), first).astype(BF)
    high = (sources_v[...] // 256).astype(F32).astype(BF)
    low = lax.rem(sources_v[...], 256).astype(F32).astype(BF)
    lane = lax.broadcasted_iota(I32, (owned, 2 * width), 1)
    spot = lax.broadcasted_iota(I32, (owned, 2 * width), 0) + lax.axis_index("grp") * owned
    for k in range((part_o.shape[0] - row_nodes) // (2 * fan)):
        place = jnp.where(lane + k * 2 * width == spot, jnp.ones((), F32), jnp.zeros((), F32)).astype(BF)
        base = row_nodes + k * 2 * fan
        part_o[base : base + 2 * fan, :] = jnp.concatenate([mm(high, place), mm(low, place)], 0).astype(BF)


def prepare_kernel(first, own, mf, ms, cf, cs, pf, ps, weights_o, fixed_o, owner_o):
    width = mf.shape[1]
    size = 2 * width
    stack = (
        twice(mf[0:width, :]),
        twice(mf[width:, :]),
        twice(ms[...]),
        twice(cf[0:width, :]),
        twice(cf[width:, :]),
        twice(centred(cs[...])),
        twice(pf[width:, :]),
        twice(centred(ps[...])),
    )
    for k, weight in enumerate(stack):
        weights_o[k * size : (k + 1) * size, :] = weight
    fixed_o[...] = mm(first[...], twice(pf[0:width, :]))
    owner_o[...] = jnp.concatenate(picks(column(own[...]), owner_o.shape[1]), 1)


def own_row_kernel(summed, weights, given_o, outer_o, mine_o, *, fan):
    row_nodes, size = mine_o.shape
    mine = summed[0:row_nodes, :]
    table = mm(mine, weights[0:size, :]).astype(BF)
    received = mm(mine, weights[size : 2 * size, :])
    for begin in range(0, row_nodes, LANES):
        chunk, lanes = divmod(begin, size)
        base = row_nodes + chunk * 2 * fan
        spots = summed[base : base + 2 * fan, lanes : lanes + LANES].astype(F32)
        spots = (spots[0:fan, :] * 256.0 + spots[fan:, :]).astype(I32)
        spots = jnp.concatenate([column(spots[j : j + 1, :]) for j in range(fan)], 0)
        blocks = picks(spots, 3 * row_nodes)
        few = row_nodes // LANES
        at = slice(begin * fan, (begin + LANES) * fan)
        got = received[begin : begin + LANES, :]
        given_o[at, :] = mm(jnp.concatenate(blocks[few : 2 * few], 1), table) + jnp.concatenate([got] * fan, 0)
        outer_o[at, :] = jnp.concatenate(blocks[:few] + blocks[2 * few :], 1)
    mine_o[...] = mm(mine, weights[3 * size : 4 * size, :])


def coarse_kernel(v0, v1, given, outer, mine, weights, fixed, owner, first, nc,
                  node_o, tangent_o, table, node_v, tangent_v, out_sems, *, fan):
    slots, width = node_o.shape
    row_nodes, size = mine.shape
    held = [weights[k * size : (k + 1) * size, :] for k in range(8)]
    ones = averaging(width)
    odd = lax.rem(lax.axis_index("dom"), 2)
    for k, got in enumerate((v0, v1)):
        place = odd if k else 1 - odd
        at = pl.ds(pl.multiple_of(place * row_nodes, row_nodes), row_nodes)
        table[at, :] = mm(got[0:row_nodes, :], held[0]).astype(BF)
    hidden = activated(given[...] + mm(outer[...], table[...]))
    sums = []
    for begin in range(0, row_nodes, LANES):
        part = [hidden[begin * fan + j * LANES : begin * fan + (j + 1) * LANES, :] for j in range(fan)]
        sums.append(sum(part))
    hidden = jnp.concatenate(sums, 0)
    large = hidden.astype(BF)
    message = mm(large, held[2]) + mm((hidden - large.astype(F32)).astype(BF), held[2])
    value, tangent = normed(mine[...] + mm(message.astype(BF), held[4]), held[5], ones)
    updated = jnp.concatenate([value, tangent], 1).astype(BF)
    brought = mm(updated, held[6]).astype(BF)
    value, tangent = normed(fixed[...] + mm(owner[...], brought), held[7], ones)
    base = first[...].astype(F32)
    valid = lax.broadcasted_iota(I32, (slots, 1), 0) < nc[0]
    node_v[...] = jnp.where(valid, base[:, :width] + value, 0.0).astype(BF)
    tangent_v[...] = jnp.where(valid, base[:, width:] + tangent, 0.0).astype(BF)
    for copy in fetch([(node_v, node_o), (tangent_v, tangent_o)], out_sems):
        copy.wait()


def like(*arrays):
    return [pltpu.VMEM(a.shape, a.dtype) for a in arrays]


def params(mib=40):
    return pltpu.CompilerParams(vmem_limit_bytes=int(mib * 2**20))


def swap(x, axis, first):
    pairs = []
    for i in range(first, lax.axis_size(axis) - 1, 2):
        pairs += [(i, i + 1), (i + 1, i)]
    return lax.ppermute(x, axis, pairs)


def row_sum(x):
    size = lax.axis_size("grp")
    total = x.astype(F32)
    for by in range(1, size):
        if size & (size - 1) == 0:
            pairs = [(i, i ^ by) for i in range(size)]
        else:
            pairs = [(i, (i + by) % size) for i in range(size)]
        total = total + lax.ppermute(x, "grp", pairs).astype(F32)
    return total.astype(BF)


def per_device(nl, nt, ed, nc, ec, lists, src, tgt, own, sources, ef, es, nf, ns, mf, ms, cf, cs, pf, ps):
    slots, width = nl.shape
    edges = ed.shape[0]
    rim = lists.shape[2]
    owned, fan = sources.shape
    sources = sources.T
    row_nodes = owned * lax.axis_size("grp")
    extra = 2 * fan * (-(-row_nodes // (2 * width)))
    rows, block, cut = min(slots, 512), min(edges, 1024), min(edges, 512)
    shape = jax.ShapeDtypeStruct
    dma = pltpu.SemaphoreType.DMA
    sent = pl.pallas_call(
        halo_kernel,
        out_shape=[shape((rim, 2 * width), BF)] * 4,
        in_specs=[HBM] * 3,
        out_specs=[HBM] * 4,
        scratch_shapes=like(nl, nt, lists) + [pltpu.VMEM((4 * rim, 2 * width), BF), dma((3,)), dma((4,))],
        compiler_params=params(60),
        cost_estimate=pl.CostEstimate(flops=8 * edges * slots * width, bytes_accessed=4 * slots * width, transcendentals=0),
        name="halo_rows",
    )(nl, nt, lists)
    got = [swap(sent[k], ("dom", "grp")[k // 2], k % 2) for k in range(4)]
    pre = pl.pallas_call(
        functools.partial(local_kernel, block=cut),
        out_shape=shape((edges, 2 * width), F32),
        in_specs=[VMEM] * 5,
        out_specs=VMEM,
        scratch_shapes=[pltpu.VMEM((2 * slots, 2 * width), BF)],
        compiler_params=params(),
        cost_estimate=pl.CostEstimate(
            flops=8 * edges * slots * width, bytes_accessed=8 * edges * width, transcendentals=0
        ),
        name="local",
    )(nl, nt, src, tgt, ef)
    first, part = pl.pallas_call(
        functools.partial(edge_kernel, block=block, rows=rows),
        out_shape=[shape((slots, 2 * width), BF), shape((row_nodes + extra, 2 * width), BF)],
        in_specs=[VMEM] * 11 + [SMEM] * 2 + [VMEM] * 5,
        out_specs=[VMEM] * 2,
        scratch_shapes=[
            pltpu.VMEM((4 * rim, 2 * width), BF),
            pltpu.VMEM((edges, 2 * width), BF),
            pltpu.VMEM((slots, 2 * width), BF),
        ],
        compiler_params=params(),
        name="edges",
    )(nl, nt, ed, src, tgt, own, sources, ef, es, nf, ns, nc, ec, *got, pre)
    weights, fixed, owner = pl.pallas_call(
        prepare_kernel,
        out_shape=[
            shape((16 * width, 2 * width), BF),
            shape((slots, 2 * width), F32),
            shape((slots, row_nodes), BF),
        ],
        in_specs=[VMEM] * 8,
        out_specs=[VMEM] * 3,
        compiler_params=params(),
        cost_estimate=pl.CostEstimate(
            flops=8 * slots * width * width, bytes_accessed=slots * width * 32, transcendentals=0
        ),
        name="prepare",
    )(first, own, mf, ms, cf, cs, pf, ps)
    summed = row_sum(part)
    v1, v0 = swap(summed, "dom", 1), swap(summed, "dom", 0)
    given, outer, mine = pl.pallas_call(
        functools.partial(own_row_kernel, fan=fan),
        out_shape=[
            shape((fan * row_nodes, 2 * width), F32),
            shape((fan * row_nodes, 2 * row_nodes), BF),
            shape((row_nodes, 2 * width), F32),
        ],
        in_specs=[VMEM] * 2,
        out_specs=[VMEM] * 3,
        compiler_params=params(),
        cost_estimate=pl.CostEstimate(
            flops=4 * fan * row_nodes * row_nodes * width,
            bytes_accessed=slots * width * 32,
            transcendentals=0,
        ),
        name="own_row",
    )(summed, weights)
    return pl.pallas_call(
        functools.partial(coarse_kernel, fan=fan),
        out_shape=[shape((slots, width), BF)] * 2,
        in_specs=[VMEM] * 9 + [SMEM],
        out_specs=[HBM] * 2,
        scratch_shapes=[
            pltpu.VMEM((2 * row_nodes, 2 * width), BF),
            pltpu.VMEM((slots, width), BF),
            pltpu.VMEM((slots, width), BF),
            dma((2,)),
        ],
        compiler_params=params(),
        name="coarse",
    )(v0, v1, given, outer, mine, weights, fixed, owner, first, nc)


def solution(mesh):
    parts = ("dom", "grp")
    rows = P(parts, None)
    in_specs = (rows,) * 3 + (P(parts),) * 2 + (P(parts, None, None),) + (rows,) * 4 + (P(),) * 10
    return jax.shard_map(
        per_device, mesh=mesh, in_specs=in_specs, out_specs=(rows, rows), check_vma=False
    )
```

time: 46.5 us -> 40.6 us (0.87)
  Pallas kernels: 22.2 us -> 17.2 us
  waiting for transfers between devices: 5.16 us -> 4.26 us
    pallas_call x1, Pallas kernels: 9.18 us -> 6.52 us  [per_device(): pl.pallas_call(functools.partial(edge_kernel, block=block, rows=rows), ou...]
    pallas_call x1, Pallas kernels: 7.02 us -> 4.76 us  [per_device(): pl.pallas_call(functools.partial(local_kernel, block=cut), out_shape=shap...]
    ppermute x6, waiting for transfers between devices: 1.96 us -> 1.06 us  [swap(): return lax.ppermute(x, axis, pairs)]
    pallas_call x1 -> x3, Pallas kernels: 3.78 us -> 3.65 us  [the longest x1 2.83 us: per_device(): pl.pallas_call(functools.partial(coarse_kernel, fan=fan), out_shape=[shap...]
  transfers between devices with their start and end apart: 9 -> 9, of which waited for: 3 -> 3; matrix products, arithmetic and copies ran while one was open for 0% -> 0% of each run, Pallas kernels for 15% -> 14%
where the time goes in v4:
time: 40.6 us; the launch traced here: 40.4 us
  Pallas kernels  17.2 us (42%)
  starting transfers between devices  16.4 us (40%)
  waiting for transfers between devices  4.26 us (10%)
  between operations  2.34 us (6%)
    ppermute x6, starting transfers between devices, swap(): return lax.ppermute(x, axis, pairs)  11.5 us
    pallas_call x1, Pallas kernels, per_device(): pl.pallas_call(functools.partial(edge_kernel, block=block, rows=rows), ou...  6.52 us
    ppermute x3, starting transfers between devices, row_sum(): total = total + lax.ppermute(x, 'grp', pairs).astype(F32)  4.92 us
    pallas_call x1, Pallas kernels, per_device(): pl.pallas_call(functools.partial(local_kernel, block=cut), out_shape=shap...  4.76 us
    ppermute x3, waiting for transfers between devices, row_sum(): total = total + lax.ppermute(x, 'grp', pairs).astype(F32)  3.2 us
    pallas_call x1, Pallas kernels, per_device(): pl.pallas_call(functools.partial(coarse_kernel, fan=fan), out_shape=[shap...  2.83 us
    pallas_call x1, Pallas kernels, per_device(): pl.pallas_call(halo_kernel, out_shape=[shape((rim, 2 * width), BF)] * 4,...  2.3 us
    ppermute x6, waiting for transfers between devices, swap(): return lax.ppermute(x, axis, pairs)  1.06 us
  transfers between devices with their start and end apart: 9, of which 3 were waited for; matrix products, arithmetic and copies ran while one was open for 0% of the time, Pallas kernels for 14%

profile of v4, /device:TPU:1, one launch (start us, length us, event | category | flops | bytes accessed | tf_op | source)
XLA Modules:
  0.0 40.4 jit_solution(8835636250593063256)
XLA Ops:
  0.6 0.0 copy-start.2
  0.6 0.0 copy-start.1
  0.7 0.0 copy-start.3
  0.7 0.0 copy-start.14
  0.7 0.0 copy-start.13
  0.7 2.3 %halo_rows.1 = (bf16[128,256]{1,0:T(8,128)(2,1)}, bf16[128,256]{1,0:T(8,128)(2,1)}, bf16[128,256]{1,0:T(8,128)(2,1)}, bf16[128,256]{1,0:T(8,128)(2,1)}) custom-call(bf16[1024,128]{1,0:T(8,128)(2,1)} %nl_v.1, bf16[1024,128]{1,0:T(8,128)(2,1)} %nt_v.1, s32[1,4,128]{2,1,0:T(4,128)} %lists.1), custom_call_target="tpu_custom_call" | custom-call | flops 4294967296 | bytes 524288 | tf_op jit(solution)/shard_map/halo_rows/pallas_call | solution.py:281
  3.0 0.1 collective-permute-start
  3.1 4.5 %collective-permute-start.1 = (bf16[128,256]{1,0:T(8,128)(2,1)}, bf16[128,256]{1,0:T(8,128)(2,1)S(1)}, u32[]{:S(2)}, u32[]{:S(2)}) collective-permute-start(bf16[128,256]{1,0:T(8,128)(2,1)} %get-tuple-element.15), channel_id=1, source_target_pairs={{4,8},{8,4},{12,16},{16,12},{20,24},{24,20},{5,9},{9,5},{13,17},{1... | collective-permute-start | bytes 196616 | tf_op jit(solution)/shard_map/ppermute | solution.py:255
  7.7 1.3 %collective-permute-start.2 = (bf16[128,256]{1,0:T(8,128)(2,1)}, bf16[128,256]{1,0:T(8,128)(2,1)S(1)}, u32[]{:S(2)}, u32[]{:S(2)}) collective-permute-start(bf16[128,256]{1,0:T(8,128)(2,1)} %get-tuple-element.16), channel_id=1, source_target_pairs={{0,1},{1,0},{2,3},{3,2},{4,5},{5,4},{6,7},{7,6},{8,9},{9,8},{10,11... | collective-permute-start | bytes 196616 | tf_op jit(solution)/shard_map/ppermute | solution.py:255
  9.0 0.0 copy-start.15
  9.0 0.0 copy-start.16
  9.0 0.8 %collective-permute-start.3 = (bf16[128,256]{1,0:T(8,128)(2,1)}, bf16[128,256]{1,0:T(8,128)(2,1)S(1)}, u32[]{:S(2)}, u32[]{:S(2)}) collective-permute-start(bf16[128,256]{1,0:T(8,128)(2,1)} %get-tuple-element.17), channel_id=1, source_target_pairs={{1,2},{2,1},{5,6},{6,5},{9,10},{10,9},{13,14},{14,13},{17,18},{18,... | collective-permute-start | bytes 196616 | tf_op jit(solution)/shard_map/ppermute | solution.py:255
  9.8 0.0 copy-done.2
  9.8 0.0 copy-done.1
  9.8 0.0 copy-done.3
  9.8 0.0 copy-done.14
  9.8 0.0 copy-done.13
  9.8 4.8 %local.1.pre = f32[4096,256]{1,0:T(8,128)S(1)} custom-call(bf16[1024,128]{1,0:T(8,128)(2,1)S(1)} %copy-done.1, bf16[1024,128]{1,0:T(8,128)(2,1)S(1)} %copy-done.2, s32[1,4096]{1,0:T(1,128)S(1)} %copy-done.13, s32[1,4096]{1,0:T(1,128)S(1)} %copy-done.14, bf16[384,128]{1,0:T(8,128)(2,1)S(1)} %copy-done.3), custom_call_target="tpu_custom_call" | custom-call | flops 4294967296 | bytes 4194304 | tf_op jit(solution)/shard_map/local/pallas_call | solution.py:292
  14.6 0.0 copy-start.4
  14.6 0.0 copy-start.5
  14.6 0.0 copy-start.6
  14.6 0.0 copy-start.10
  14.6 0.0 copy-start.11
  14.7 0.0 copy-start.12
  16.0 0.0 collective-permute-done.h0
  16.0 0.0 collective-permute-done.1.h1
  16.1 0.0 collective-permute-done.2.h2
  16.1 0.0 collective-permute-done.3.h3
  16.1 0.0 copy-done
  16.1 0.0 copy-done.7
  16.1 0.0 copy-done.8
  16.1 0.0 copy-done.9
  16.1 0.0 copy-done.15
  16.1 0.0 copy-done.16
  16.1 6.5 %edges.1 = (bf16[1024,256]{1,0:T(8,128)(2,1)S(1)}, bf16[144,256]{1,0:T(8,128)(2,1)S(1)}) custom-call(bf16[1024,128]{1,0:T(8,128)(2,1)S(1)} %copy-done.1, bf16[1024,128]{1,0:T(8,128)(2,1)S(1)} %copy-done.2, bf16[4096,128]{1,0:T(8,128)(2,1)S(1)} %copy-done, s32[1,4096]{1,0:T(1,128)S(1)} %copy-done.13, s32[1,4096]{1,0:T(1,128)S(1)} %copy-done.14, ...), custom_call_target="tpu_custom_call" | custom-call | tf_op jit(solution)/shard_map/edges/pallas_call | solution.py:304
  22.7 1.3 %collective-permute-start.6 = (bf16[144,256]{1,0:T(8,128)(2,1)S(1)}, bf16[144,256]{1,0:T(8,128)(2,1)S(1)}, u32[]{:S(2)}, u32[]{:S(2)}) collective-permute-start(bf16[144,256]{1,0:T(8,128)(2,1)S(1)} %get-tuple-element.18), channel_id=1, source_target_pairs={{0,3},{1,2},{2,1},{3,0},{4,7},{5,6},{6,5},{7,4},{8,11},{9,10},{10,... | collective-permute-start | bytes 221192 | tf_op jit(solution)/shard_map/ppermute | solution.py:266
  23.9 3.6 %collective-permute-start.5 = (bf16[144,256]{1,0:T(8,128)(2,1)S(1)}, bf16[144,256]{1,0:T(8,128)(2,1)S(1)}, u32[]{:S(2)}, u32[]{:S(2)}) collective-permute-start(bf16[144,256]{1,0:T(8,128)(2,1)S(1)} %get-tuple-element.18), channel_id=1, source_target_pairs={{0,2},{1,3},{2,0},{3,1},{4,6},{5,7},{6,4},{7,5},{8,10},{9,11},{10,... | collective-permute-start | bytes 221192 | tf_op jit(solution)/shard_map/ppermute | solution.py:266
  27.6 0.0 collective-permute-start.4
  27.6 0.0 collective-permute-done.6
  27.6 2.0 %collective-permute-done.5 = bf16[144,256]{1,0:T(8,128)(2,1)S(1)} collective-permute-done((bf16[144,256]{1,0:T(8,128)(2,1)S(1)}, bf16[144,256]{1,0:T(8,128)(2,1)S(1)}, u32[]{:S(2)}, u32[]{:S(2)}) %collective-permute-start.5) | collective-permute-done | bytes 73760 | tf_op jit(solution)/shard_map/ppermute | solution.py:266
  29.6 1.2 %collective-permute-done.4 = bf16[144,256]{1,0:T(8,128)(2,1)S(1)} collective-permute-done((bf16[144,256]{1,0:T(8,128)(2,1)S(1)}, bf16[144,256]{1,0:T(8,128)(2,1)S(1)}, u32[]{:S(2)}, u32[]{:S(2)}) %collective-permute-start.4) | collective-permute-done | bytes 73760 | tf_op jit(solution)/shard_map/ppermute | solution.py:266
  30.8 4.7 %collective-permute-start.8 = (bf16[144,256]{1,0:T(8,128)(2,1)S(1)}, bf16[144,256]{1,0:T(8,128)(2,1)S(1)}, u32[]{:S(2)}, u32[]{:S(2)}) collective-permute-start(bf16[144,256]{1,0:T(8,128)(2,1)S(1)} %add_convert_fusion.summed), channel_id=1, source_target_pairs={{4,8},{8,4},{12,16},{16,12},{20,24},{24,20},{5,9},{9,5},{13,17},{1... | collective-permute-start | bytes 221192 | tf_op jit(solution)/shard_map/ppermute | solution.py:255
  35.6 0.1 collective-permute-start.7
  35.7 0.3 prepare.1
  36.0 0.5 %own_row.1 = (f32[1024,256]{1,0:T(8,128)S(1)}, bf16[1024,256]{1,0:T(8,128)(2,1)S(1)}, f32[128,256]{1,0:T(8,128)S(1)}) custom-call(bf16[144,256]{1,0:T(8,128)(2,1)S(1)} %add_convert_fusion.summed, bf16[2048,256]{1,0:T(8,128)(2,1)S(1)} %get-tuple-element.20.weights), custom_call_target="tpu_custom_call" | custom-call | flops 67108864 | bytes 4194304 | tf_op jit(solution)/shard_map/own_row/pallas_call | solution.py:334
  36.5 1.0 %collective-permute-done.8.v1 = bf16[144,256]{1,0:T(8,128)(2,1)S(1)} collective-permute-done((bf16[144,256]{1,0:T(8,128)(2,1)S(1)}, bf16[144,256]{1,0:T(8,128)(2,1)S(1)}, u32[]{:S(2)}, u32[]{:S(2)}) %collective-permute-start.8) | collective-permute-done | bytes 73760 | tf_op jit(solution)/shard_map/ppermute | solution.py:255
  37.6 0.0 collective-permute-done.7.v0
  37.6 2.8 %coarse.1 = (bf16[1024,128]{1,0:T(8,128)(2,1)}, bf16[1024,128]{1,0:T(8,128)(2,1)}) custom-call(bf16[144,256]{1,0:T(8,128)(2,1)S(1)} %collective-permute-done.7.v0, bf16[144,256]{1,0:T(8,128)(2,1)S(1)} %collective-permute-done.8.v1, f32[1024,256]{1,0:T(8,128)S(1)} %get-tuple-element.21.given, bf16[1024,256]{1,0:T(8,128)(2,1)S(1)} %get-tuple-element.22.outer, ...), custom_call_target="tpu_custom_call" | custom-call | tf_op jit(solution)/shard_map/coarse/pallas_call | solution.py:351
  (11 shorter events, 0.1 us)
Async XLA Ops:
  0.6 9.2 %copy-start.2 = (bf16[1024,128]{1,0:T(8,128)(2,1)S(1)}, bf16[1024,128]{1,0:T(8,128)(2,1)}, u32[]{:S(2)}) copy-start(bf16[1024,128]{1,0:T(8,128)(2,1)} %nt_v.1) | copy-start | bytes 786436
  0.6 9.2 %copy-start.1 = (bf16[1024,128]{1,0:T(8,128)(2,1)S(1)}, bf16[1024,128]{1,0:T(8,128)(2,1)}, u32[]{:S(2)}) copy-start(bf16[1024,128]{1,0:T(8,128)(2,1)} %nl_v.1) | copy-start | bytes 786436
  0.7 9.2 %copy-start.3 = (bf16[384,128]{1,0:T(8,128)(2,1)S(1)}, bf16[384,128]{1,0:T(8,128)(2,1)}, u32[]{:S(2)}) copy-start(bf16[384,128]{1,0:T(8,128)(2,1)} %ef_v.1) | copy-start | bytes 294916
  0.7 9.2 %copy-start.14 = (s32[1,4096]{1,0:T(1,128)S(1)}, s32[1,4096]{1,0:T(1,128)}, u32[]{:S(2)}) copy-start(s32[1,4096]{1,0:T(1,128)} %tgt_v.1) | copy-start | bytes 49156
  0.7 9.2 %copy-start.13 = (s32[1,4096]{1,0:T(1,128)S(1)}, s32[1,4096]{1,0:T(1,128)}, u32[]{:S(2)}) copy-start(s32[1,4096]{1,0:T(1,128)} %src_v.1) | copy-start | bytes 49156
  3.0 13.0 %collective-permute-start = (bf16[128,256]{1,0:T(8,128)(2,1)}, bf16[128,256]{1,0:T(8,128)(2,1)S(1)}, u32[]{:S(2)}, u32[]{:S(2)}) collective-permute-start(bf16[128,256]{1,0:T(8,128)(2,1)} %get-tuple-element.14), channel_id=1, source_target_pairs={{0,4},{4,0},{8,12},{12,8},{16,20},{20,16},{24,28},{28,24},{1,5},{5... | collective-permute-start | bytes 196616 | tf_op jit(solution)/shard_map/ppermute | solution.py:255
  3.1 12.9 %collective-permute-start.1 = (bf16[128,256]{1,0:T(8,128)(2,1)}, bf16[128,256]{1,0:T(8,128)(2,1)S(1)}, u32[]{:S(2)}, u32[]{:S(2)}) collective-permute-start(bf16[128,256]{1,0:T(8,128)(2,1)} %get-tuple-element.15), channel_id=1, source_target_pairs={{4,8},{8,4},{12,16},{16,12},{20,24},{24,20},{5,9},{9,5},{13,17},{1... | collective-permute-start | bytes 196616 | tf_op jit(solution)/shard_map/ppermute | solution.py:255
  7.7 8.4 %collective-permute-start.2 = (bf16[128,256]{1,0:T(8,128)(2,1)}, bf16[128,256]{1,0:T(8,128)(2,1)S(1)}, u32[]{:S(2)}, u32[]{:S(2)}) collective-permute-start(bf16[128,256]{1,0:T(8,128)(2,1)} %get-tuple-element.16), channel_id=1, source_target_pairs={{0,1},{1,0},{2,3},{3,2},{4,5},{5,4},{6,7},{7,6},{8,9},{9,8},{10,11... | collective-permute-start | bytes 196616 | tf_op jit(solution)/shard_map/ppermute | solution.py:255
  8.9 7.1 %copy-start = (bf16[4096,128]{1,0:T(8,128)(2,1)S(1)}, bf16[4096,128]{1,0:T(8,128)(2,1)}, u32[]{:S(2)}) copy-start(bf16[4096,128]{1,0:T(8,128)(2,1)} %ed_v.1) | copy-start | bytes 3145732
  9.0 7.1 %copy-start.7 = (bf16[256,128]{1,0:T(8,128)(2,1)S(1)}, bf16[256,128]{1,0:T(8,128)(2,1)}, u32[]{:S(2)}) copy-start(bf16[256,128]{1,0:T(8,128)(2,1)} %nf_v.1) | copy-start | bytes 196612
  9.0 7.1 %copy-start.8 = (bf16[128,128]{1,0:T(8,128)(2,1)S(1)}, bf16[128,128]{1,0:T(8,128)(2,1)}, u32[]{:S(2)}) copy-start(bf16[128,128]{1,0:T(8,128)(2,1)} %es_v.1) | copy-start | bytes 98308
  9.0 7.2 %copy-start.9 = (bf16[128,128]{1,0:T(8,128)(2,1)S(1)}, bf16[128,128]{1,0:T(8,128)(2,1)}, u32[]{:S(2)}) copy-start(bf16[128,128]{1,0:T(8,128)(2,1)} %ns_v.1) | copy-start | bytes 98308
  9.0 7.2 %copy-start.15 = (s32[1,1024]{1,0:T(1,128)S(1)}, s32[1,1024]{1,0:T(1,128)}, u32[]{:S(2)}) copy-start(s32[1,1024]{1,0:T(1,128)} %own.1) | copy-start | bytes 12292
  9.0 7.2 %copy-start.16 = (s32[32,8]{0,1:T(8,128)S(1)}, s32[32,8]{0,1:T(8,128)}, u32[]{:S(2)}) copy-start(s32[32,8]{0,1:T(8,128)} %param.29) | copy-start | bytes 3076
  9.0 7.1 %collective-permute-start.3 = (bf16[128,256]{1,0:T(8,128)(2,1)}, bf16[128,256]{1,0:T(8,128)(2,1)S(1)}, u32[]{:S(2)}, u32[]{:S(2)}) collective-permute-start(bf16[128,256]{1,0:T(8,128)(2,1)} %get-tuple-element.17), channel_id=1, source_target_pairs={{1,2},{2,1},{5,6},{6,5},{9,10},{10,9},{13,14},{14,13},{17,18},{18,... | collective-permute-start | bytes 196616 | tf_op jit(solution)/shard_map/ppermute | solution.py:255
  14.6 21.0 %copy-start.4 = (bf16[256,128]{1,0:T(8,128)(2,1)S(1)}, bf16[256,128]{1,0:T(8,128)(2,1)}, u32[]{:S(2)}) copy-start(bf16[256,128]{1,0:T(8,128)(2,1)} %mf.1) | copy-start | bytes 196612
  14.6 21.0 %copy-start.5 = (bf16[256,128]{1,0:T(8,128)(2,1)S(1)}, bf16[256,128]{1,0:T(8,128)(2,1)}, u32[]{:S(2)}) copy-start(bf16[256,128]{1,0:T(8,128)(2,1)} %cf.1) | copy-start | bytes 196612
  14.6 21.0 %copy-start.6 = (bf16[256,128]{1,0:T(8,128)(2,1)S(1)}, bf16[256,128]{1,0:T(8,128)(2,1)}, u32[]{:S(2)}) copy-start(bf16[256,128]{1,0:T(8,128)(2,1)} %pf.1) | copy-start | bytes 196612
  14.6 21.0 %copy-start.10 = (bf16[128,128]{1,0:T(8,128)(2,1)S(1)}, bf16[128,128]{1,0:T(8,128)(2,1)}, u32[]{:S(2)}) copy-start(bf16[128,128]{1,0:T(8,128)(2,1)} %ms.1) | copy-start | bytes 98308
  14.6 21.0 %copy-start.11 = (bf16[128,128]{1,0:T(8,128)(2,1)S(1)}, bf16[128,128]{1,0:T(8,128)(2,1)}, u32[]{:S(2)}) copy-start(bf16[128,128]{1,0:T(8,128)(2,1)} %cs.1) | copy-start | bytes 98308
  14.7 21.0 %copy-start.12 = (bf16[128,128]{1,0:T(8,128)(2,1)S(1)}, bf16[128,128]{1,0:T(8,128)(2,1)}, u32[]{:S(2)}) copy-start(bf16[128,128]{1,0:T(8,128)(2,1)} %ps.1) | copy-start | bytes 98308
  22.7 4.9 %collective-permute-start.6 = (bf16[144,256]{1,0:T(8,128)(2,1)S(1)}, bf16[144,256]{1,0:T(8,128)(2,1)S(1)}, u32[]{:S(2)}, u32[]{:S(2)}) collective-permute-start(bf16[144,256]{1,0:T(8,128)(2,1)S(1)} %get-tuple-element.18), channel_id=1, source_target_pairs={{0,3},{1,2},{2,1},{3,0},{4,7},{5,6},{6,5},{7,4},{8,11},{9,10},{10,... | collective-permute-start | bytes 221192 | tf_op jit(solution)/shard_map/ppermute | solution.py:266
  23.9 5.7 %collective-permute-start.5 = (bf16[144,256]{1,0:T(8,128)(2,1)S(1)}, bf16[144,256]{1,0:T(8,128)(2,1)S(1)}, u32[]{:S(2)}, u32[]{:S(2)}) collective-permute-start(bf16[144,256]{1,0:T(8,128)(2,1)S(1)} %get-tuple-element.18), channel_id=1, source_target_pairs={{0,2},{1,3},{2,0},{3,1},{4,6},{5,7},{6,4},{7,5},{8,10},{9,11},{10,... | collective-permute-start | bytes 221192 | tf_op jit(solution)/shard_map/ppermute | solution.py:266
  27.6 3.2 %collective-permute-start.4 = (bf16[144,256]{1,0:T(8,128)(2,1)S(1)}, bf16[144,256]{1,0:T(8,128)(2,1)S(1)}, u32[]{:S(2)}, u32[]{:S(2)}) collective-permute-start(bf16[144,256]{1,0:T(8,128)(2,1)S(1)} %get-tuple-element.18), channel_id=1, source_target_pairs={{0,1},{1,0},{2,3},{3,2},{4,5},{5,4},{6,7},{7,6},{8,9},{9,8},{10,11... | collective-permute-start | bytes 221192 | tf_op jit(solution)/shard_map/ppermute | solution.py:266
  30.8 6.7 %collective-permute-start.8 = (bf16[144,256]{1,0:T(8,128)(2,1)S(1)}, bf16[144,256]{1,0:T(8,128)(2,1)S(1)}, u32[]{:S(2)}, u32[]{:S(2)}) collective-permute-start(bf16[144,256]{1,0:T(8,128)(2,1)S(1)} %add_convert_fusion.summed), channel_id=1, source_target_pairs={{4,8},{8,4},{12,16},{16,12},{20,24},{24,20},{5,9},{9,5},{13,17},{1... | collective-permute-start | bytes 221192 | tf_op jit(solution)/shard_map/ppermute | solution.py:255
  35.6 2.0 %collective-permute-start.7 = (bf16[144,256]{1,0:T(8,128)(2,1)S(1)}, bf16[144,256]{1,0:T(8,128)(2,1)S(1)}, u32[]{:S(2)}, u32[]{:S(2)}) collective-permute-start(bf16[144,256]{1,0:T(8,128)(2,1)S(1)} %add_convert_fusion.summed), channel_id=1, source_target_pairs={{0,4},{4,0},{8,12},{12,8},{16,20},{20,16},{24,28},{28,24},{1,5},{5... | collective-permute-start | bytes 221192 | tf_op jit(solution)/shard_map/ppermute | solution.py:255

commit v5 on v4

--- a/solution.py
+++ b/solution.py
@@ -89,26 +89,18 @@
     return copies
 
 
-def halo_kernel(nl, nt, lists, o0, o1, o2, o3, nl_v, nt_v, lists_v, sent_v, sems, out_sems):
+def halo_kernel(nl, nt, lists, o0, o1, o2, o3, nl_v, nt_v, lists_v, sems):
     for copy in fetch([(lists, lists_v), (nl, nl_v), (nt, nt_v)], sems):
         copy.wait()
     slots = nl.shape[0]
-    rim = o0.shape[0]
     paired = jnp.concatenate([nl_v[...], nt_v[...]], 1)
     even = (lax.rem(lax.axis_index("dom"), 2) == 0, lax.rem(lax.axis_index("grp"), 2) == 0)
-    stores = []
     for k, out in enumerate((o0, o1, o2, o3)):
         base = k // 2 * 2
         up = even[k // 2] if k % 2 == 0 else jnp.logical_not(even[k // 2])
         row = jnp.where(up, lists_v[0, base : base + 1, :], lists_v[0, base + 1 : base + 2, :])
         selector = jnp.concatenate(picks(column(row), slots), 1)
-        at = slice(k * rim, (k + 1) * rim)
-        sent_v[at, :] = mm(selector, paired).astype(BF)
-        copy = pltpu.make_async_copy(sent_v.at[at], out, out_sems.at[k])
-        copy.start()
-        stores.append(copy)
-    for copy in stores:
-        copy.wait()
+        out[...] = mm(selector, paired).astype(BF)
 
 
 def local_kernel(nl, nt, src, tgt, ef, pre_o, table, *, block):
@@ -176,9 +168,8 @@
     stack = (
         twice(mf[0:width, :]),
         twice(mf[width:, :]),
-        twice(ms[...]),
+        twice(mm(ms[...], cf[width:, :]).astype(BF)),
         twice(cf[0:width, :]),
-        twice(cf[width:, :]),
         twice(centred(cs[...])),
         twice(pf[width:, :]),
         twice(centred(ps[...])),
@@ -213,7 +204,7 @@
                   node_o, tangent_o, table, node_v, tangent_v, out_sems, *, fan):
     slots, width = node_o.shape
     row_nodes, size = mine.shape
-    held = [weights[k * size : (k + 1) * size, :] for k in range(8)]
+    held = [weights[k * size : (k + 1) * size, :] for k in range(7)]
     ones = averaging(width)
     odd = lax.rem(lax.axis_index("dom"), 2)
     for k, got in enumerate((v0, v1)):
@@ -227,11 +218,11 @@
         sums.append(sum(part))
     hidden = jnp.concatenate(sums, 0)
     large = hidden.astype(BF)
-    message = mm(large, held[2]) + mm((hidden - large.astype(F32)).astype(BF), held[2])
-    value, tangent = normed(mine[...] + mm(message.astype(BF), held[4]), held[5], ones)
+    small = (hidden - large.astype(F32)).astype(BF)
+    value, tangent = normed(mine[...] + mm(large, held[2]) + mm(small, held[2]), held[4], ones)
     updated = jnp.concatenate([value, tangent], 1).astype(BF)
-    brought = mm(updated, held[6]).astype(BF)
-    value, tangent = normed(fixed[...] + mm(owner[...], brought), held[7], ones)
+    brought = mm(updated, held[5]).astype(BF)
+    value, tangent = normed(fixed[...] + mm(owner[...], brought), held[6], ones)
     base = first[...].astype(F32)
     valid = lax.broadcasted_iota(I32, (slots, 1), 0) < nc[0]
     node_v[...] = jnp.where(valid, base[:, :width] + value, 0.0).astype(BF)
@@ -255,16 +246,17 @@
     return lax.ppermute(x, axis, pairs)
 
 
-def row_sum(x):
+def row_sum(x, ready):
     size = lax.axis_size("grp")
-    total = x.astype(F32)
+    got = []
     for by in range(1, size):
         if size & (size - 1) == 0:
             pairs = [(i, i ^ by) for i in range(size)]
         else:
             pairs = [(i, (i + by) % size) for i in range(size)]
-        total = total + lax.ppermute(x, "grp", pairs).astype(F32)
-    return total.astype(BF)
+        got.append(lax.ppermute(x, "grp", pairs))
+    got, ready = lax.optimization_barrier((got, ready))
+    return sum([y.astype(F32) for y in got], x.astype(F32)).astype(BF), ready
 
 
 def per_device(nl, nt, ed, nc, ec, lists, src, tgt, own, sources, ef, es, nf, ns, mf, ms, cf, cs, pf, ps):
@@ -278,16 +270,16 @@
     rows, block, cut = min(slots, 512), min(edges, 1024), min(edges, 512)
     shape = jax.ShapeDtypeStruct
     dma = pltpu.SemaphoreType.DMA
-    sent = pl.pallas_call(
+    *sent, nl, nt = pl.pallas_call(
         halo_kernel,
-        out_shape=[shape((rim, 2 * width), BF)] * 4,
+        out_shape=[pltpu.VMEM((rim, 2 * width), BF)] * 4 + like(nl, nt),
         in_specs=[HBM] * 3,
-        out_specs=[HBM] * 4,
-        scratch_shapes=like(nl, nt, lists) + [pltpu.VMEM((4 * rim, 2 * width), BF), dma((3,)), dma((4,))],
-        compiler_params=params(60),
+        out_specs=[VMEM] * 6,
+        scratch_shapes=like(lists) + [dma((3,))],
+        compiler_params=params(),
         cost_estimate=pl.CostEstimate(flops=8 * edges * slots * width, bytes_accessed=4 * slots * width, transcendentals=0),
         name="halo_rows",
-    )(nl, nt, lists)
+    )(*(pltpu.with_memory_space_constraint(x, pltpu.HBM) for x in (nl, nt, lists)))
     got = [swap(sent[k], ("dom", "grp")[k // 2], k % 2) for k in range(4)]
     pre = pl.pallas_call(
         functools.partial(local_kernel, block=cut),
@@ -302,7 +294,7 @@
         name="local",
     )(nl, nt, src, tgt, ef)
     first, part = pl.pallas_call(
-        functools.partial(edge_kernel, block=block, rows=rows),
+        functools.partial(edge_kernel, block=min(edges, 2048), rows=256),
         out_shape=[shape((slots, 2 * width), BF), shape((row_nodes + extra, 2 * width), BF)],
         in_specs=[VMEM] * 11 + [SMEM] * 2 + [VMEM] * 5,
         out_specs=[VMEM] * 2,
@@ -317,7 +309,7 @@
     weights, fixed, owner = pl.pallas_call(
         prepare_kernel,
         out_shape=[
-            shape((16 * width, 2 * width), BF),
+            shape((14 * width, 2 * width), BF),
             shape((slots, 2 * width), F32),
             shape((slots, row_nodes), BF),
         ],
@@ -329,7 +321,7 @@
         ),
         name="prepare",
     )(first, own, mf, ms, cf, cs, pf, ps)
-    summed = row_sum(part)
+    summed, (weights, fixed, owner) = row_sum(part, (weights, fixed, owner))
     v1, v0 = swap(summed, "dom", 1), swap(summed, "dom", 0)
     given, outer, mine = pl.pallas_call(
         functools.partial(own_row_kernel, fan=fan),

time: 40.6 us -> 39.5 us (0.973)
  Pallas kernels: 17.2 us -> 16.2 us
    pallas_call x3, Pallas kernels: 9.16 us -> 8.29 us  [the longest x1 6.35 us: per_device(): pl.pallas_call(functools.partial(edge_kernel, block=min(edges, 2048), row...]
where the time goes in v5:
time: 39.5 us; the launch traced here: 39.3 us
  starting transfers between devices  16.3 us (41%)
  Pallas kernels  16.2 us (41%)
  waiting for transfers between devices  4.28 us (11%)
  between operations  2.33 us (6%)
    ppermute x6, starting transfers between devices, swap(): return lax.ppermute(x, axis, pairs)  11.4 us
    pallas_call x1, Pallas kernels, per_device(): pl.pallas_call(functools.partial(edge_kernel, block=min(edges, 2048), row...  6.35 us
    ppermute x3, starting transfers between devices, row_sum(): got.append(lax.ppermute(x, 'grp', pairs))  4.92 us
    pallas_call x1, Pallas kernels, per_device(): pl.pallas_call(functools.partial(local_kernel, block=cut), out_shape=shap...  4.76 us
    ppermute x3, waiting for transfers between devices, row_sum(): got.append(lax.ppermute(x, 'grp', pairs))  2.82 us
    pallas_call x1, Pallas kernels, per_device(): pl.pallas_call(functools.partial(coarse_kernel, fan=fan), out_shape=[shap...  2.71 us
    pallas_call x1, Pallas kernels, per_device(): pl.pallas_call(halo_kernel, out_shape=[pltpu.VMEM((rim, 2 * width), BF)]...  1.62 us
    ppermute x6, waiting for transfers between devices, swap(): return lax.ppermute(x, axis, pairs)  1.46 us
  transfers between devices with their start and end apart: 9, of which 3 were waited for; matrix products, arithmetic and copies ran while one was open for 0% of the time, Pallas kernels for 14%

profile of v5, /device:TPU:1, one launch (start us, length us, event | category | flops | bytes accessed | tf_op | source)
XLA Modules:
  0.0 39.3 jit_solution(7093750588144469573)
XLA Ops:
  0.6 0.0 copy-start.1
  0.6 0.0 copy-start.12
  0.7 1.6 %halo_rows.1 = (bf16[128,256]{1,0:T(8,128)(2,1)S(1)}, bf16[128,256]{1,0:T(8,128)(2,1)S(1)}, bf16[128,256]{1,0:T(8,128)(2,1)S(1)}, bf16[128,256]{1,0:T(8,128)(2,1...) custom-call(bf16[1024,128]{1,0:T(8,128)(2,1)} %nl.1, bf16[1024,128]{1,0:T(8,128)(2,1)} %nt.1, ...), custom_call_target="tpu_custom_call" | custom-call | flops 4294967296 | bytes 524288 | tf_op jit(solution)/shard_map/halo_rows/pallas_call | solution.py:273
  2.3 0.1 collective-permute-start
  2.4 4.6 %collective-permute-start.1 = (bf16[128,256]{1,0:T(8,128)(2,1)S(1)}, bf16[128,256]{1,0:T(8,128)(2,1)S(1)}, u32[]{:S(2)}, u32[]{:S(2)}) collective-permute-start(bf16[128,256]{1,0:T(8,128)(2,1)S(1)} %get-tuple-element.25), channel_id=1, source_target_pairs={{4,8},{8,4},{12,16},{16,12},{20,24},{24,20},{5,9},{9,5},{13,17},{1... | collective-permute-start | bytes 196616 | tf_op jit(solution)/shard_map/ppermute | solution.py:246
  7.0 1.3 %collective-permute-start.2 = (bf16[128,256]{1,0:T(8,128)(2,1)S(1)}, bf16[128,256]{1,0:T(8,128)(2,1)S(1)}, u32[]{:S(2)}, u32[]{:S(2)}) collective-permute-start(bf16[128,256]{1,0:T(8,128)(2,1)S(1)} %get-tuple-element.26), channel_id=1, source_target_pairs={{0,1},{1,0},{2,3},{3,2},{4,5},{5,4},{6,7},{7,6},{8,9},{9,8},{10,11... | collective-permute-start | bytes 196616 | tf_op jit(solution)/shard_map/ppermute | solution.py:246
  8.2 0.7 %collective-permute-start.3 = (bf16[128,256]{1,0:T(8,128)(2,1)S(1)}, bf16[128,256]{1,0:T(8,128)(2,1)S(1)}, u32[]{:S(2)}, u32[]{:S(2)}) collective-permute-start(bf16[128,256]{1,0:T(8,128)(2,1)S(1)} %get-tuple-element.27), channel_id=1, source_target_pairs={{1,2},{2,1},{5,6},{6,5},{9,10},{10,9},{13,14},{14,13},{17,18},{18,... | collective-permute-start | bytes 196616 | tf_op jit(solution)/shard_map/ppermute | solution.py:246
  8.9 0.0 copy-start
  8.9 0.0 copy-start.5
  9.0 0.0 copy-start.6
  9.0 0.0 copy-start.7
  9.0 0.0 copy-start.13
  9.0 0.0 copy-start.14
  9.0 4.8 %local.1.pre = f32[4096,256]{1,0:T(8,128)S(1)} custom-call(bf16[1024,128]{1,0:T(8,128)(2,1)S(1)} %get-tuple-element.22.nl.nl_v, bf16[1024,128]{1,0:T(8,128)(2,1)S(1)} %get-tuple-element.23.nt.nt_v, s32[1,4096]{1,0:T(1,128)S(1)} %copy-done.11, s32[1,4096]{1,0:T(1,128)S(1)} %copy-done.12, bf16[384,128]{1,0:T(8,128)(2,1)S(1)} %copy-done.1), custom_call_target="tpu_custom_call" | custom-call | flops 4294967296 | bytes 4194304 | tf_op jit(solution)/shard_map/local/pallas_call | solution.py:284
  13.8 0.0 copy-start.2
  13.8 0.0 copy-start.3
  13.8 0.0 copy-start.4
  13.8 0.0 copy-start.8
  13.8 0.0 copy-start.9
  13.8 0.0 copy-start.10
  15.2 0.0 collective-permute-done.h0
  15.2 0.0 collective-permute-done.1.h1
  15.2 0.0 collective-permute-done.2.h2
  15.2 0.0 collective-permute-done.3.h3
  15.2 0.0 copy-done
  15.3 0.0 copy-done.5
  15.3 0.0 copy-done.6
  15.3 0.0 copy-done.7
  15.3 0.0 copy-done.13
  15.3 0.0 copy-done.14
  15.3 6.4 %edges.1 = (bf16[1024,256]{1,0:T(8,128)(2,1)S(1)}, bf16[144,256]{1,0:T(8,128)(2,1)S(1)}) custom-call(bf16[1024,128]{1,0:T(8,128)(2,1)S(1)} %get-tuple-element.22.nl.nl_v, bf16[1024,128]{1,0:T(8,128)(2,1)S(1)} %get-tuple-element.23.nt.nt_v, bf16[4096,128]{1,0:T(8,128)(2,1)S(1)} %copy-done, s32[1,4096]{1,0:T(1,128)S(1)} %copy-done.11, ...), custom_call_target="tpu_custom_call" | custom-call | tf_op jit(solution)/shard_map/edges/pallas_call | solution.py:296
  21.7 1.3 %collective-permute-start.6 = (bf16[144,256]{1,0:T(8,128)(2,1)S(1)}, bf16[144,256]{1,0:T(8,128)(2,1)S(1)}, u32[]{:S(2)}, u32[]{:S(2)}) collective-permute-start(bf16[144,256]{1,0:T(8,128)(2,1)S(1)} %get-tuple-element.28), channel_id=1, source_target_pairs={{0,3},{1,2},{2,1},{3,0},{4,7},{5,6},{6,5},{7,4},{8,11},{9,10},{10,... | collective-permute-start | bytes 221192 | tf_op jit(solution)/shard_map/ppermute | solution.py:257
  22.9 3.6 %collective-permute-start.5 = (bf16[144,256]{1,0:T(8,128)(2,1)S(1)}, bf16[144,256]{1,0:T(8,128)(2,1)S(1)}, u32[]{:S(2)}, u32[]{:S(2)}) collective-permute-start(bf16[144,256]{1,0:T(8,128)(2,1)S(1)} %get-tuple-element.28), channel_id=1, source_target_pairs={{0,2},{1,3},{2,0},{3,1},{4,6},{5,7},{6,4},{7,5},{8,10},{9,11},{10,... | collective-permute-start | bytes 221192 | tf_op jit(solution)/shard_map/ppermute | solution.py:257
  26.6 0.0 collective-permute-start.4
  26.6 0.0 copy-done.4
  26.6 0.0 copy-done.8
  26.6 0.0 copy-done.9
  26.6 0.0 copy-done.10
  26.6 0.3 prepare.1
  27.0 0.0 collective-permute-done.6
  27.0 1.6 %collective-permute-done.5 = bf16[144,256]{1,0:T(8,128)(2,1)S(1)} collective-permute-done((bf16[144,256]{1,0:T(8,128)(2,1)S(1)}, bf16[144,256]{1,0:T(8,128)(2,1)S(1)}, u32[]{:S(2)}, u32[]{:S(2)}) %collective-permute-start.5) | collective-permute-done | bytes 73760 | tf_op jit(solution)/shard_map/ppermute | solution.py:257
  28.6 1.2 %collective-permute-done.4 = bf16[144,256]{1,0:T(8,128)(2,1)S(1)} collective-permute-done((bf16[144,256]{1,0:T(8,128)(2,1)S(1)}, bf16[144,256]{1,0:T(8,128)(2,1)S(1)}, u32[]{:S(2)}, u32[]{:S(2)}) %collective-permute-start.4) | collective-permute-done | bytes 73760 | tf_op jit(solution)/shard_map/ppermute | solution.py:257
  29.8 4.7 %collective-permute-start.8 = (bf16[144,256]{1,0:T(8,128)(2,1)S(1)}, bf16[144,256]{1,0:T(8,128)(2,1)S(1)}, u32[]{:S(2)}, u32[]{:S(2)}) collective-permute-start(bf16[144,256]{1,0:T(8,128)(2,1)S(1)} %add_convert_fusion.summed), channel_id=1, source_target_pairs={{4,8},{8,4},{12,16},{16,12},{20,24},{24,20},{5,9},{9,5},{13,17},{1... | collective-permute-start | bytes 221192 | tf_op jit(solution)/shard_map/ppermute | solution.py:246
  34.6 0.1 collective-permute-start.7
  34.6 0.5 %own_row.1 = (f32[1024,256]{1,0:T(8,128)S(1)}, bf16[1024,256]{1,0:T(8,128)(2,1)S(1)}, f32[128,256]{1,0:T(8,128)S(1)}) custom-call(bf16[144,256]{1,0:T(8,128)(2,1)S(1)} %add_convert_fusion.summed, bf16[1792,256]{1,0:T(8,128)(2,1)S(1)} %get-tuple-element.36.weights), custom_call_target="tpu_custom_call" | custom-call | flops 67108864 | bytes 4194304 | tf_op jit(solution)/shard_map/own_row/pallas_call | solution.py:326
  35.1 1.5 %collective-permute-done.8.v1 = bf16[144,256]{1,0:T(8,128)(2,1)S(1)} collective-permute-done((bf16[144,256]{1,0:T(8,128)(2,1)S(1)}, bf16[144,256]{1,0:T(8,128)(2,1)S(1)}, u32[]{:S(2)}, u32[]{:S(2)}) %collective-permute-start.8) | collective-permute-done | bytes 73760 | tf_op jit(solution)/shard_map/ppermute | solution.py:246
  36.6 0.0 collective-permute-done.7.v0
  36.6 2.7 %coarse.1 = (bf16[1024,128]{1,0:T(8,128)(2,1)}, bf16[1024,128]{1,0:T(8,128)(2,1)}) custom-call(bf16[144,256]{1,0:T(8,128)(2,1)S(1)} %collective-permute-done.7.v0, bf16[144,256]{1,0:T(8,128)(2,1)S(1)} %collective-permute-done.8.v1, f32[1024,256]{1,0:T(8,128)S(1)} %get-tuple-element.37.given, bf16[1024,256]{1,0:T(8,128)(2,1)S(1)} %get-tuple-element.38.outer, ...), custom_call_target="tpu_custom_call" | custom-call | tf_op jit(solution)/shard_map/coarse/pallas_call | solution.py:343
  (7 shorter events, 0.1 us)
Async XLA Ops:
  0.6 8.3 %copy-start.1 = (bf16[384,128]{1,0:T(8,128)(2,1)S(1)}, bf16[384,128]{1,0:T(8,128)(2,1)}, u32[]{:S(2)}) copy-start(bf16[384,128]{1,0:T(8,128)(2,1)} %ef_v.1) | copy-start | bytes 294916
  0.6 8.3 %copy-start.12 = (s32[1,4096]{1,0:T(1,128)S(1)}, s32[1,4096]{1,0:T(1,128)}, u32[]{:S(2)}) copy-start(s32[1,4096]{1,0:T(1,128)} %tgt_v.1) | copy-start | bytes 49156
  0.7 8.3 %copy-start.11 = (s32[1,4096]{1,0:T(1,128)S(1)}, s32[1,4096]{1,0:T(1,128)}, u32[]{:S(2)}) copy-start(s32[1,4096]{1,0:T(1,128)} %src_v.1) | copy-start | bytes 49156
  2.3 12.9 %collective-permute-start = (bf16[128,256]{1,0:T(8,128)(2,1)S(1)}, bf16[128,256]{1,0:T(8,128)(2,1)S(1)}, u32[]{:S(2)}, u32[]{:S(2)}) collective-permute-start(bf16[128,256]{1,0:T(8,128)(2,1)S(1)} %get-tuple-element.24), channel_id=1, source_target_pairs={{0,4},{4,0},{8,12},{12,8},{16,20},{20,16},{24,28},{28,24},{1,5},{5... | collective-permute-start | bytes 196616 | tf_op jit(solution)/shard_map/ppermute | solution.py:246
  2.4 12.8 %collective-permute-start.1 = (bf16[128,256]{1,0:T(8,128)(2,1)S(1)}, bf16[128,256]{1,0:T(8,128)(2,1)S(1)}, u32[]{:S(2)}, u32[]{:S(2)}) collective-permute-start(bf16[128,256]{1,0:T(8,128)(2,1)S(1)} %get-tuple-element.25), channel_id=1, source_target_pairs={{4,8},{8,4},{12,16},{16,12},{20,24},{24,20},{5,9},{9,5},{13,17},{1... | collective-permute-start | bytes 196616 | tf_op jit(solution)/shard_map/ppermute | solution.py:246
  7.0 8.3 %collective-permute-start.2 = (bf16[128,256]{1,0:T(8,128)(2,1)S(1)}, bf16[128,256]{1,0:T(8,128)(2,1)S(1)}, u32[]{:S(2)}, u32[]{:S(2)}) collective-permute-start(bf16[128,256]{1,0:T(8,128)(2,1)S(1)} %get-tuple-element.26), channel_id=1, source_target_pairs={{0,1},{1,0},{2,3},{3,2},{4,5},{5,4},{6,7},{7,6},{8,9},{9,8},{10,11... | collective-permute-start | bytes 196616 | tf_op jit(solution)/shard_map/ppermute | solution.py:246
  8.2 7.0 %collective-permute-start.3 = (bf16[128,256]{1,0:T(8,128)(2,1)S(1)}, bf16[128,256]{1,0:T(8,128)(2,1)S(1)}, u32[]{:S(2)}, u32[]{:S(2)}) collective-permute-start(bf16[128,256]{1,0:T(8,128)(2,1)S(1)} %get-tuple-element.27), channel_id=1, source_target_pairs={{1,2},{2,1},{5,6},{6,5},{9,10},{10,9},{13,14},{14,13},{17,18},{18,... | collective-permute-start | bytes 196616 | tf_op jit(solution)/shard_map/ppermute | solution.py:246
  8.9 6.3 %copy-start = (bf16[4096,128]{1,0:T(8,128)(2,1)S(1)}, bf16[4096,128]{1,0:T(8,128)(2,1)}, u32[]{:S(2)}) copy-start(bf16[4096,128]{1,0:T(8,128)(2,1)} %ed_v.1) | copy-start | bytes 3145732
  8.9 6.3 %copy-start.5 = (bf16[256,128]{1,0:T(8,128)(2,1)S(1)}, bf16[256,128]{1,0:T(8,128)(2,1)}, u32[]{:S(2)}) copy-start(bf16[256,128]{1,0:T(8,128)(2,1)} %nf_v.1) | copy-start | bytes 196612
  9.0 6.3 %copy-start.6 = (bf16[128,128]{1,0:T(8,128)(2,1)S(1)}, bf16[128,128]{1,0:T(8,128)(2,1)}, u32[]{:S(2)}) copy-start(bf16[128,128]{1,0:T(8,128)(2,1)} %es_v.1) | copy-start | bytes 98308
  9.0 6.3 %copy-start.7 = (bf16[128,128]{1,0:T(8,128)(2,1)S(1)}, bf16[128,128]{1,0:T(8,128)(2,1)}, u32[]{:S(2)}) copy-start(bf16[128,128]{1,0:T(8,128)(2,1)} %ns_v.1) | copy-start | bytes 98308
  9.0 6.3 %copy-start.13 = (s32[1,1024]{1,0:T(1,128)S(1)}, s32[1,1024]{1,0:T(1,128)}, u32[]{:S(2)}) copy-start(s32[1,1024]{1,0:T(1,128)} %own.1) | copy-start | bytes 12292
  9.0 6.3 %copy-start.14 = (s32[32,8]{0,1:T(8,128)S(1)}, s32[32,8]{0,1:T(8,128)}, u32[]{:S(2)}) copy-start(s32[32,8]{0,1:T(8,128)} %param.29) | copy-start | bytes 3076
  13.8 12.8 %copy-start.2 = (bf16[256,128]{1,0:T(8,128)(2,1)S(1)}, bf16[256,128]{1,0:T(8,128)(2,1)}, u32[]{:S(2)}) copy-start(bf16[256,128]{1,0:T(8,128)(2,1)} %mf.1) | copy-start | bytes 196612
  13.8 12.8 %copy-start.3 = (bf16[256,128]{1,0:T(8,128)(2,1)S(1)}, bf16[256,128]{1,0:T(8,128)(2,1)}, u32[]{:S(2)}) copy-start(bf16[256,128]{1,0:T(8,128)(2,1)} %cf.1) | copy-start | bytes 196612
  13.8 12.8 %copy-start.4 = (bf16[256,128]{1,0:T(8,128)(2,1)S(1)}, bf16[256,128]{1,0:T(8,128)(2,1)}, u32[]{:S(2)}) copy-start(bf16[256,128]{1,0:T(8,128)(2,1)} %pf.1) | copy-start | bytes 196612
  13.8 12.8 %copy-start.8 = (bf16[128,128]{1,0:T(8,128)(2,1)S(1)}, bf16[128,128]{1,0:T(8,128)(2,1)}, u32[]{:S(2)}) copy-start(bf16[128,128]{1,0:T(8,128)(2,1)} %ms.1) | copy-start | bytes 98308
  13.8 12.8 %copy-start.9 = (bf16[128,128]{1,0:T(8,128)(2,1)S(1)}, bf16[128,128]{1,0:T(8,128)(2,1)}, u32[]{:S(2)}) copy-start(bf16[128,128]{1,0:T(8,128)(2,1)} %cs.1) | copy-start | bytes 98308
  13.8 12.8 %copy-start.10 = (bf16[128,128]{1,0:T(8,128)(2,1)S(1)}, bf16[128,128]{1,0:T(8,128)(2,1)}, u32[]{:S(2)}) copy-start(bf16[128,128]{1,0:T(8,128)(2,1)} %ps.1) | copy-start | bytes 98308
  21.7 5.3 %collective-permute-start.6 = (bf16[144,256]{1,0:T(8,128)(2,1)S(1)}, bf16[144,256]{1,0:T(8,128)(2,1)S(1)}, u32[]{:S(2)}, u32[]{:S(2)}) collective-permute-start(bf16[144,256]{1,0:T(8,128)(2,1)S(1)} %get-tuple-element.28), channel_id=1, source_target_pairs={{0,3},{1,2},{2,1},{3,0},{4,7},{5,6},{6,5},{7,4},{8,11},{9,10},{10,... | collective-permute-start | bytes 221192 | tf_op jit(solution)/shard_map/ppermute | solution.py:257
  22.9 5.7 %collective-permute-start.5 = (bf16[144,256]{1,0:T(8,128)(2,1)S(1)}, bf16[144,256]{1,0:T(8,128)(2,1)S(1)}, u32[]{:S(2)}, u32[]{:S(2)}) collective-permute-start(bf16[144,256]{1,0:T(8,128)(2,1)S(1)} %get-tuple-element.28), channel_id=1, source_target_pairs={{0,2},{1,3},{2,0},{3,1},{4,6},{5,7},{6,4},{7,5},{8,10},{9,11},{10,... | collective-permute-start | bytes 221192 | tf_op jit(solution)/shard_map/ppermute | solution.py:257
  26.6 3.2 %collective-permute-start.4 = (bf16[144,256]{1,0:T(8,128)(2,1)S(1)}, bf16[144,256]{1,0:T(8,128)(2,1)S(1)}, u32[]{:S(2)}, u32[]{:S(2)}) collective-permute-start(bf16[144,256]{1,0:T(8,128)(2,1)S(1)} %get-tuple-element.28), channel_id=1, source_target_pairs={{0,1},{1,0},{2,3},{3,2},{4,5},{5,4},{6,7},{7,6},{8,9},{9,8},{10,11... | collective-permute-start | bytes 221192 | tf_op jit(solution)/shard_map/ppermute | solution.py:257
  29.8 6.7 %collective-permute-start.8 = (bf16[144,256]{1,0:T(8,128)(2,1)S(1)}, bf16[144,256]{1,0:T(8,128)(2,1)S(1)}, u32[]{:S(2)}, u32[]{:S(2)}) collective-permute-start(bf16[144,256]{1,0:T(8,128)(2,1)S(1)} %add_convert_fusion.summed), channel_id=1, source_target_pairs={{4,8},{8,4},{12,16},{16,12},{20,24},{24,20},{5,9},{9,5},{13,17},{1... | collective-permute-start | bytes 221192 | tf_op jit(solution)/shard_map/ppermute | solution.py:246
  34.6 2.0 %collective-permute-start.7 = (bf16[144,256]{1,0:T(8,128)(2,1)S(1)}, bf16[144,256]{1,0:T(8,128)(2,1)S(1)}, u32[]{:S(2)}, u32[]{:S(2)}) collective-permute-start(bf16[144,256]{1,0:T(8,128)(2,1)S(1)} %add_convert_fusion.summed), channel_id=1, source_target_pairs={{0,4},{4,0},{8,12},{12,8},{16,20},{20,16},{24,28},{28,24},{1,5},{5... | collective-permute-start | bytes 221192 | tf_op jit(solution)/shard_map/ppermute | solution.py:246

commit v6 on v5

--- a/solution.py
+++ b/solution.py
@@ -15,6 +15,8 @@
 SMEM = pl.BlockSpec(memory_space=pltpu.SMEM)
 VMEM = pl.BlockSpec(memory_space=pltpu.VMEM)
 LANES = 128
+ORDER = (0, 1, 2, 3)
+PEERS = (2, 1, 3)
 
 
 def mm(a, b):
@@ -89,13 +91,13 @@
     return copies
 
 
-def halo_kernel(nl, nt, lists, o0, o1, o2, o3, nl_v, nt_v, lists_v, sems):
+def halo_kernel(nl, nt, lists, o0, o1, o2, o3, nl_v, nt_v, lists_v, sems, *, order):
     for copy in fetch([(lists, lists_v), (nl, nl_v), (nt, nt_v)], sems):
         copy.wait()
     slots = nl.shape[0]
     paired = jnp.concatenate([nl_v[...], nt_v[...]], 1)
     even = (lax.rem(lax.axis_index("dom"), 2) == 0, lax.rem(lax.axis_index("grp"), 2) == 0)
-    for k, out in enumerate((o0, o1, o2, o3)):
+    for k, out in zip(order, (o0, o1, o2, o3)):
         base = k // 2 * 2
         up = even[k // 2] if k % 2 == 0 else jnp.logical_not(even[k // 2])
         row = jnp.where(up, lists_v[0, base : base + 1, :], lists_v[0, base + 1 : base + 2, :])
@@ -117,13 +119,13 @@
 
 
 def edge_kernel(nl_v, nt_v, ed_v, src_v, tgt_v, own_v, sources_v, ef_v, es_v, nf_v, ns_v, nc, ec,
-                h0, h1, h2, h3, pre, first_o, part_o, table, pairs, sums, *, block, rows):
+                h0, h1, h2, h3, pre, first_o, part_o, table, pairs, sums, *, block, rows, order):
     slots, width = nl_v.shape
     edges = ed_v.shape[0]
     rim = h0.shape[0]
     weight = twice(ef_v[width : 2 * width, :])
     odd = (lax.rem(lax.axis_index("dom"), 2), lax.rem(lax.axis_index("grp"), 2))
-    for k, got in enumerate((h0, h1, h2, h3)):
+    for k, got in zip(order, (h0, h1, h2, h3)):
         place = k // 2 * 2 + (odd[k // 2] if k % 2 else 1 - odd[k // 2])
         at = pl.ds(pl.multiple_of(place * rim, rim), rim)
         table[at, :] = mm(got[...], weight).astype(BF)
@@ -249,7 +251,7 @@
 def row_sum(x, ready):
     size = lax.axis_size("grp")
     got = []
-    for by in range(1, size):
+    for by in PEERS if size == len(PEERS) + 1 else range(1, size):
         if size & (size - 1) == 0:
             pairs = [(i, i ^ by) for i in range(size)]
         else:
@@ -271,7 +273,7 @@
     shape = jax.ShapeDtypeStruct
     dma = pltpu.SemaphoreType.DMA
     *sent, nl, nt = pl.pallas_call(
-        halo_kernel,
+        functools.partial(halo_kernel, order=ORDER),
         out_shape=[pltpu.VMEM((rim, 2 * width), BF)] * 4 + like(nl, nt),
         in_specs=[HBM] * 3,
         out_specs=[VMEM] * 6,
@@ -280,7 +282,7 @@
         cost_estimate=pl.CostEstimate(flops=8 * edges * slots * width, bytes_accessed=4 * slots * width, transcendentals=0),
         name="halo_rows",
     )(*(pltpu.with_memory_space_constraint(x, pltpu.HBM) for x in (nl, nt, lists)))
-    got = [swap(sent[k], ("dom", "grp")[k // 2], k % 2) for k in range(4)]
+    got = [swap(x, ("dom", "grp")[k // 2], k % 2) for k, x in zip(ORDER, sent)]
     pre = pl.pallas_call(
         functools.partial(local_kernel, block=cut),
         out_shape=shape((edges, 2 * width), F32),
@@ -294,7 +296,7 @@
         name="local",
     )(nl, nt, src, tgt, ef)
     first, part = pl.pallas_call(
-        functools.partial(edge_kernel, block=min(edges, 2048), rows=256),
+        functools.partial(edge_kernel, block=min(edges, 2048), rows=256, order=ORDER),
         out_shape=[shape((slots, 2 * width), BF), shape((row_nodes + extra, 2 * width), BF)],
         in_specs=[VMEM] * 11 + [SMEM] * 2 + [VMEM] * 5,
         out_specs=[VMEM] * 2,

time: 39.5 us -> 38.8 us (0.982); the launches traced: 39.3 us -> 38.2 us
  waiting for transfers between devices: 4.28 us -> 3.31 us
    ppermute x3, waiting for transfers between devices: 2.82 us -> 1.85 us  [row_sum(): got.append(lax.ppermute(x, 'grp', pairs))]
  transfers between devices with their start and end apart: 9 -> 9, of which waited for: 3 -> 3; matrix products, arithmetic and copies ran while one was open for 0% -> 0% of each run, Pallas kernels for 14% -> 15%
where the time goes in v6:
time: 38.8 us; the launch traced here: 38.2 us
  Pallas kernels  16.3 us (42%)
  starting transfers between devices  16.2 us (42%)
  waiting for transfers between devices  3.31 us (9%)
  between operations  2.32 us (6%)
    ppermute x6, starting transfers between devices, swap(): return lax.ppermute(x, axis, pairs)  11.2 us
    pallas_call x1, Pallas kernels, per_device(): pl.pallas_call(functools.partial(edge_kernel, block=min(edges, 2048), row...  6.35 us
    ppermute x3, starting transfers between devices, row_sum(): got.append(lax.ppermute(x, 'grp', pairs))  4.92 us
    pallas_call x1, Pallas kernels, per_device(): pl.pallas_call(functools.partial(local_kernel, block=cut), out_shape=shap...  4.76 us
    pallas_call x1, Pallas kernels, per_device(): pl.pallas_call(functools.partial(coarse_kernel, fan=fan), out_shape=[shap...  2.72 us
    ppermute x3, waiting for transfers between devices, row_sum(): got.append(lax.ppermute(x, 'grp', pairs))  1.85 us
    pallas_call x1, Pallas kernels, per_device(): pl.pallas_call(functools.partial(halo_kernel, order=ORDER), out_shape=[pl...  1.62 us
    ppermute x6, waiting for transfers between devices, swap(): return lax.ppermute(x, axis, pairs)  1.46 us
  transfers between devices with their start and end apart: 9, of which 3 were waited for; matrix products, arithmetic and copies ran while one was open for 0% of the time, Pallas kernels for 15%

profile of v6, /device:TPU:1, one launch (start us, length us, event | category | flops | bytes accessed | tf_op | source)
XLA Modules:
  0.0 38.2 jit_solution(2133582120431030294)
XLA Ops:
  0.6 0.0 copy-start.1
  0.6 0.0 copy-start.12
  0.7 0.0 copy-start.11
  0.7 1.6 %halo_rows.1 = (bf16[128,256]{1,0:T(8,128)(2,1)S(1)}, bf16[128,256]{1,0:T(8,128)(2,1)S(1)}, bf16[128,256]{1,0:T(8,128)(2,1)S(1)}, bf16[128,256]{1,0:T(8,128)(2,1...) custom-call(bf16[1024,128]{1,0:T(8,128)(2,1)} %nl.1, bf16[1024,128]{1,0:T(8,128)(2,1)} %nt.1, ...), custom_call_target="tpu_custom_call" | custom-call | flops 4294967296 | bytes 524288 | tf_op jit(solution)/shard_map/halo_rows/pallas_call | solution.py:275
  2.3 0.1 collective-permute-start
  2.4 4.6 %collective-permute-start.1 = (bf16[128,256]{1,0:T(8,128)(2,1)S(1)}, bf16[128,256]{1,0:T(8,128)(2,1)S(1)}, u32[]{:S(2)}, u32[]{:S(2)}) collective-permute-start(bf16[128,256]{1,0:T(8,128)(2,1)S(1)} %get-tuple-element.25), channel_id=1, source_target_pairs={{4,8},{8,4},{12,16},{16,12},{20,24},{24,20},{5,9},{9,5},{13,17},{1... | collective-permute-start | bytes 196616 | tf_op jit(solution)/shard_map/ppermute | solution.py:248
  7.0 1.3 %collective-permute-start.2 = (bf16[128,256]{1,0:T(8,128)(2,1)S(1)}, bf16[128,256]{1,0:T(8,128)(2,1)S(1)}, u32[]{:S(2)}, u32[]{:S(2)}) collective-permute-start(bf16[128,256]{1,0:T(8,128)(2,1)S(1)} %get-tuple-element.26), channel_id=1, source_target_pairs={{0,1},{1,0},{2,3},{3,2},{4,5},{5,4},{6,7},{7,6},{8,9},{9,8},{10,11... | collective-permute-start | bytes 196616 | tf_op jit(solution)/shard_map/ppermute | solution.py:248
  8.2 0.7 %collective-permute-start.3 = (bf16[128,256]{1,0:T(8,128)(2,1)S(1)}, bf16[128,256]{1,0:T(8,128)(2,1)S(1)}, u32[]{:S(2)}, u32[]{:S(2)}) collective-permute-start(bf16[128,256]{1,0:T(8,128)(2,1)S(1)} %get-tuple-element.27), channel_id=1, source_target_pairs={{1,2},{2,1},{5,6},{6,5},{9,10},{10,9},{13,14},{14,13},{17,18},{18,... | collective-permute-start | bytes 196616 | tf_op jit(solution)/shard_map/ppermute | solution.py:248
  8.9 0.0 copy-done.1
  8.9 0.0 copy-done.12
  8.9 0.0 copy-done.11
  8.9 0.0 copy-start
  8.9 0.0 copy-start.5
  9.0 0.0 copy-start.6
  9.0 0.0 copy-start.7
  9.0 0.0 copy-start.13
  9.0 0.0 copy-start.14
  9.0 4.8 %local.1.pre = f32[4096,256]{1,0:T(8,128)S(1)} custom-call(bf16[1024,128]{1,0:T(8,128)(2,1)S(1)} %get-tuple-element.22.nl.nl_v, bf16[1024,128]{1,0:T(8,128)(2,1)S(1)} %get-tuple-element.23.nt.nt_v, s32[1,4096]{1,0:T(1,128)S(1)} %copy-done.11, s32[1,4096]{1,0:T(1,128)S(1)} %copy-done.12, bf16[384,128]{1,0:T(8,128)(2,1)S(1)} %copy-done.1), custom_call_target="tpu_custom_call" | custom-call | flops 4294967296 | bytes 4194304 | tf_op jit(solution)/shard_map/local/pallas_call | solution.py:286
  13.8 0.0 copy-start.2
  13.8 0.0 copy-start.3
  13.8 0.0 copy-start.4
  13.8 0.0 copy-start.8
  13.8 0.0 copy-start.9
  13.8 0.0 copy-start.10
  15.2 0.0 collective-permute-done.h0
  15.2 0.0 collective-permute-done.1.h1
  15.2 0.0 collective-permute-done.2.h2
  15.2 0.0 collective-permute-done.3.h3
  15.2 0.0 copy-done
  15.3 0.0 copy-done.5
  15.3 0.0 copy-done.6
  15.3 0.0 copy-done.7
  15.3 0.0 copy-done.13
  15.3 0.0 copy-done.14
  15.3 6.4 %edges.1 = (bf16[1024,256]{1,0:T(8,128)(2,1)S(1)}, bf16[144,256]{1,0:T(8,128)(2,1)S(1)}) custom-call(bf16[1024,128]{1,0:T(8,128)(2,1)S(1)} %get-tuple-element.22.nl.nl_v, bf16[1024,128]{1,0:T(8,128)(2,1)S(1)} %get-tuple-element.23.nt.nt_v, bf16[4096,128]{1,0:T(8,128)(2,1)S(1)} %copy-done, s32[1,4096]{1,0:T(1,128)S(1)} %copy-done.11, ...), custom_call_target="tpu_custom_call" | custom-call | tf_op jit(solution)/shard_map/edges/pallas_call | solution.py:298
  21.7 1.3 %collective-permute-start.6 = (bf16[144,256]{1,0:T(8,128)(2,1)S(1)}, bf16[144,256]{1,0:T(8,128)(2,1)S(1)}, u32[]{:S(2)}, u32[]{:S(2)}) collective-permute-start(bf16[144,256]{1,0:T(8,128)(2,1)S(1)} %get-tuple-element.28), channel_id=1, source_target_pairs={{0,3},{1,2},{2,1},{3,0},{4,7},{5,6},{6,5},{7,4},{8,11},{9,10},{10,... | collective-permute-start | bytes 221192 | tf_op jit(solution)/shard_map/ppermute | solution.py:259
  22.9 2.7 %collective-permute-start.5 = (bf16[144,256]{1,0:T(8,128)(2,1)S(1)}, bf16[144,256]{1,0:T(8,128)(2,1)S(1)}, u32[]{:S(2)}, u32[]{:S(2)}) collective-permute-start(bf16[144,256]{1,0:T(8,128)(2,1)S(1)} %get-tuple-element.28), channel_id=1, source_target_pairs={{0,1},{1,0},{2,3},{3,2},{4,5},{5,4},{6,7},{7,6},{8,9},{9,8},{10,11... | collective-permute-start | bytes 221192 | tf_op jit(solution)/shard_map/ppermute | solution.py:259
  25.6 1.0 %collective-permute-start.4 = (bf16[144,256]{1,0:T(8,128)(2,1)S(1)}, bf16[144,256]{1,0:T(8,128)(2,1)S(1)}, u32[]{:S(2)}, u32[]{:S(2)}) collective-permute-start(bf16[144,256]{1,0:T(8,128)(2,1)S(1)} %get-tuple-element.28), channel_id=1, source_target_pairs={{0,2},{1,3},{2,0},{3,1},{4,6},{5,7},{6,4},{7,5},{8,10},{9,11},{10,... | collective-permute-start | bytes 221192 | tf_op jit(solution)/shard_map/ppermute | solution.py:259
  26.6 0.3 prepare.1
  27.0 0.0 collective-permute-done.6
  27.0 1.2 %collective-permute-done.5 = bf16[144,256]{1,0:T(8,128)(2,1)S(1)} collective-permute-done((bf16[144,256]{1,0:T(8,128)(2,1)S(1)}, bf16[144,256]{1,0:T(8,128)(2,1)S(1)}, u32[]{:S(2)}, u32[]{:S(2)}) %collective-permute-start.5) | collective-permute-done | bytes 73760 | tf_op jit(solution)/shard_map/ppermute | solution.py:259
  28.1 0.7 %collective-permute-done.4 = bf16[144,256]{1,0:T(8,128)(2,1)S(1)} collective-permute-done((bf16[144,256]{1,0:T(8,128)(2,1)S(1)}, bf16[144,256]{1,0:T(8,128)(2,1)S(1)}, u32[]{:S(2)}, u32[]{:S(2)}) %collective-permute-start.4) | collective-permute-done | bytes 73760 | tf_op jit(solution)/shard_map/ppermute | solution.py:259
  28.9 4.6 %collective-permute-start.8 = (bf16[144,256]{1,0:T(8,128)(2,1)S(1)}, bf16[144,256]{1,0:T(8,128)(2,1)S(1)}, u32[]{:S(2)}, u32[]{:S(2)}) collective-permute-start(bf16[144,256]{1,0:T(8,128)(2,1)S(1)} %add_convert_fusion.summed), channel_id=1, source_target_pairs={{4,8},{8,4},{12,16},{16,12},{20,24},{24,20},{5,9},{9,5},{13,17},{1... | collective-permute-start | bytes 221192 | tf_op jit(solution)/shard_map/ppermute | solution.py:248
  33.4 0.1 collective-permute-start.7
  33.5 0.5 %own_row.1 = (f32[1024,256]{1,0:T(8,128)S(1)}, bf16[1024,256]{1,0:T(8,128)(2,1)S(1)}, f32[128,256]{1,0:T(8,128)S(1)}) custom-call(bf16[144,256]{1,0:T(8,128)(2,1)S(1)} %add_convert_fusion.summed, bf16[1792,256]{1,0:T(8,128)(2,1)S(1)} %get-tuple-element.36.weights), custom_call_target="tpu_custom_call" | custom-call | flops 67108864 | bytes 4194304 | tf_op jit(solution)/shard_map/own_row/pallas_call | solution.py:328
  34.0 1.4 %collective-permute-done.8.v1 = bf16[144,256]{1,0:T(8,128)(2,1)S(1)} collective-permute-done((bf16[144,256]{1,0:T(8,128)(2,1)S(1)}, bf16[144,256]{1,0:T(8,128)(2,1)S(1)}, u32[]{:S(2)}, u32[]{:S(2)}) %collective-permute-start.8) | collective-permute-done | bytes 73760 | tf_op jit(solution)/shard_map/ppermute | solution.py:248
  35.5 0.0 collective-permute-done.7.v0
  35.5 2.7 %coarse.1 = (bf16[1024,128]{1,0:T(8,128)(2,1)}, bf16[1024,128]{1,0:T(8,128)(2,1)}) custom-call(bf16[144,256]{1,0:T(8,128)(2,1)S(1)} %collective-permute-done.7.v0, bf16[144,256]{1,0:T(8,128)(2,1)S(1)} %collective-permute-done.8.v1, f32[1024,256]{1,0:T(8,128)S(1)} %get-tuple-element.37.given, bf16[1024,256]{1,0:T(8,128)(2,1)S(1)} %get-tuple-element.38.outer, ...), custom_call_target="tpu_custom_call" | custom-call | tf_op jit(solution)/shard_map/coarse/pallas_call | solution.py:345
  (7 shorter events, 0.1 us)
Async XLA Ops:
  0.6 8.3 %copy-start.1 = (bf16[384,128]{1,0:T(8,128)(2,1)S(1)}, bf16[384,128]{1,0:T(8,128)(2,1)}, u32[]{:S(2)}) copy-start(bf16[384,128]{1,0:T(8,128)(2,1)} %ef_v.1) | copy-start | bytes 294916
  0.6 8.3 %copy-start.12 = (s32[1,4096]{1,0:T(1,128)S(1)}, s32[1,4096]{1,0:T(1,128)}, u32[]{:S(2)}) copy-start(s32[1,4096]{1,0:T(1,128)} %tgt_v.1) | copy-start | bytes 49156
  0.7 8.3 %copy-start.11 = (s32[1,4096]{1,0:T(1,128)S(1)}, s32[1,4096]{1,0:T(1,128)}, u32[]{:S(2)}) copy-start(s32[1,4096]{1,0:T(1,128)} %src_v.1) | copy-start | bytes 49156
  2.3 12.9 %collective-permute-start = (bf16[128,256]{1,0:T(8,128)(2,1)S(1)}, bf16[128,256]{1,0:T(8,128)(2,1)S(1)}, u32[]{:S(2)}, u32[]{:S(2)}) collective-permute-start(bf16[128,256]{1,0:T(8,128)(2,1)S(1)} %get-tuple-element.24), channel_id=1, source_target_pairs={{0,4},{4,0},{8,12},{12,8},{16,20},{20,16},{24,28},{28,24},{1,5},{5... | collective-permute-start | bytes 196616 | tf_op jit(solution)/shard_map/ppermute | solution.py:248
  2.4 12.8 %collective-permute-start.1 = (bf16[128,256]{1,0:T(8,128)(2,1)S(1)}, bf16[128,256]{1,0:T(8,128)(2,1)S(1)}, u32[]{:S(2)}, u32[]{:S(2)}) collective-permute-start(bf16[128,256]{1,0:T(8,128)(2,1)S(1)} %get-tuple-element.25), channel_id=1, source_target_pairs={{4,8},{8,4},{12,16},{16,12},{20,24},{24,20},{5,9},{9,5},{13,17},{1... | collective-permute-start | bytes 196616 | tf_op jit(solution)/shard_map/ppermute | solution.py:248
  7.0 8.3 %collective-permute-start.2 = (bf16[128,256]{1,0:T(8,128)(2,1)S(1)}, bf16[128,256]{1,0:T(8,128)(2,1)S(1)}, u32[]{:S(2)}, u32[]{:S(2)}) collective-permute-start(bf16[128,256]{1,0:T(8,128)(2,1)S(1)} %get-tuple-element.26), channel_id=1, source_target_pairs={{0,1},{1,0},{2,3},{3,2},{4,5},{5,4},{6,7},{7,6},{8,9},{9,8},{10,11... | collective-permute-start | bytes 196616 | tf_op jit(solution)/shard_map/ppermute | solution.py:248
  8.2 7.0 %collective-permute-start.3 = (bf16[128,256]{1,0:T(8,128)(2,1)S(1)}, bf16[128,256]{1,0:T(8,128)(2,1)S(1)}, u32[]{:S(2)}, u32[]{:S(2)}) collective-permute-start(bf16[128,256]{1,0:T(8,128)(2,1)S(1)} %get-tuple-element.27), channel_id=1, source_target_pairs={{1,2},{2,1},{5,6},{6,5},{9,10},{10,9},{13,14},{14,13},{17,18},{18,... | collective-permute-start | bytes 196616 | tf_op jit(solution)/shard_map/ppermute | solution.py:248
  8.9 6.3 %copy-start = (bf16[4096,128]{1,0:T(8,128)(2,1)S(1)}, bf16[4096,128]{1,0:T(8,128)(2,1)}, u32[]{:S(2)}) copy-start(bf16[4096,128]{1,0:T(8,128)(2,1)} %ed_v.1) | copy-start | bytes 3145732
  8.9 6.3 %copy-start.5 = (bf16[256,128]{1,0:T(8,128)(2,1)S(1)}, bf16[256,128]{1,0:T(8,128)(2,1)}, u32[]{:S(2)}) copy-start(bf16[256,128]{1,0:T(8,128)(2,1)} %nf_v.1) | copy-start | bytes 196612
  9.0 6.3 %copy-start.6 = (bf16[128,128]{1,0:T(8,128)(2,1)S(1)}, bf16[128,128]{1,0:T(8,128)(2,1)}, u32[]{:S(2)}) copy-start(bf16[128,128]{1,0:T(8,128)(2,1)} %es_v.1) | copy-start | bytes 98308
  9.0 6.3 %copy-start.7 = (bf16[128,128]{1,0:T(8,128)(2,1)S(1)}, bf16[128,128]{1,0:T(8,128)(2,1)}, u32[]{:S(2)}) copy-start(bf16[128,128]{1,0:T(8,128)(2,1)} %ns_v.1) | copy-start | bytes 98308
  9.0 6.3 %copy-start.13 = (s32[1,1024]{1,0:T(1,128)S(1)}, s32[1,1024]{1,0:T(1,128)}, u32[]{:S(2)}) copy-start(s32[1,1024]{1,0:T(1,128)} %own.1) | copy-start | bytes 12292
  9.0 6.3 %copy-start.14 = (s32[32,8]{0,1:T(8,128)S(1)}, s32[32,8]{0,1:T(8,128)}, u32[]{:S(2)}) copy-start(s32[32,8]{0,1:T(8,128)} %param.29) | copy-start | bytes 3076
  13.8 12.8 %copy-start.2 = (bf16[256,128]{1,0:T(8,128)(2,1)S(1)}, bf16[256,128]{1,0:T(8,128)(2,1)}, u32[]{:S(2)}) copy-start(bf16[256,128]{1,0:T(8,128)(2,1)} %mf.1) | copy-start | bytes 196612
  13.8 12.8 %copy-start.3 = (bf16[256,128]{1,0:T(8,128)(2,1)S(1)}, bf16[256,128]{1,0:T(8,128)(2,1)}, u32[]{:S(2)}) copy-start(bf16[256,128]{1,0:T(8,128)(2,1)} %cf.1) | copy-start | bytes 196612
  13.8 12.8 %copy-start.4 = (bf16[256,128]{1,0:T(8,128)(2,1)S(1)}, bf16[256,128]{1,0:T(8,128)(2,1)}, u32[]{:S(2)}) copy-start(bf16[256,128]{1,0:T(8,128)(2,1)} %pf.1) | copy-start | bytes 196612
  13.8 12.8 %copy-start.8 = (bf16[128,128]{1,0:T(8,128)(2,1)S(1)}, bf16[128,128]{1,0:T(8,128)(2,1)}, u32[]{:S(2)}) copy-start(bf16[128,128]{1,0:T(8,128)(2,1)} %ms.1) | copy-start | bytes 98308
  13.8 12.8 %copy-start.9 = (bf16[128,128]{1,0:T(8,128)(2,1)S(1)}, bf16[128,128]{1,0:T(8,128)(2,1)}, u32[]{:S(2)}) copy-start(bf16[128,128]{1,0:T(8,128)(2,1)} %cs.1) | copy-start | bytes 98308
  13.8 12.8 %copy-start.10 = (bf16[128,128]{1,0:T(8,128)(2,1)S(1)}, bf16[128,128]{1,0:T(8,128)(2,1)}, u32[]{:S(2)}) copy-start(bf16[128,128]{1,0:T(8,128)(2,1)} %ps.1) | copy-start | bytes 98308
  21.7 5.3 %collective-permute-start.6 = (bf16[144,256]{1,0:T(8,128)(2,1)S(1)}, bf16[144,256]{1,0:T(8,128)(2,1)S(1)}, u32[]{:S(2)}, u32[]{:S(2)}) collective-permute-start(bf16[144,256]{1,0:T(8,128)(2,1)S(1)} %get-tuple-element.28), channel_id=1, source_target_pairs={{0,3},{1,2},{2,1},{3,0},{4,7},{5,6},{6,5},{7,4},{8,11},{9,10},{10,... | collective-permute-start | bytes 221192 | tf_op jit(solution)/shard_map/ppermute | solution.py:259
  22.9 5.2 %collective-permute-start.5 = (bf16[144,256]{1,0:T(8,128)(2,1)S(1)}, bf16[144,256]{1,0:T(8,128)(2,1)S(1)}, u32[]{:S(2)}, u32[]{:S(2)}) collective-permute-start(bf16[144,256]{1,0:T(8,128)(2,1)S(1)} %get-tuple-element.28), channel_id=1, source_target_pairs={{0,1},{1,0},{2,3},{3,2},{4,5},{5,4},{6,7},{7,6},{8,9},{9,8},{10,11... | collective-permute-start | bytes 221192 | tf_op jit(solution)/shard_map/ppermute | solution.py:259
  25.6 3.2 %collective-permute-start.4 = (bf16[144,256]{1,0:T(8,128)(2,1)S(1)}, bf16[144,256]{1,0:T(8,128)(2,1)S(1)}, u32[]{:S(2)}, u32[]{:S(2)}) collective-permute-start(bf16[144,256]{1,0:T(8,128)(2,1)S(1)} %get-tuple-element.28), channel_id=1, source_target_pairs={{0,2},{1,3},{2,0},{3,1},{4,6},{5,7},{6,4},{7,5},{8,10},{9,11},{10,... | collective-permute-start | bytes 221192 | tf_op jit(solution)/shard_map/ppermute | solution.py:259
  28.9 6.6 %collective-permute-start.8 = (bf16[144,256]{1,0:T(8,128)(2,1)S(1)}, bf16[144,256]{1,0:T(8,128)(2,1)S(1)}, u32[]{:S(2)}, u32[]{:S(2)}) collective-permute-start(bf16[144,256]{1,0:T(8,128)(2,1)S(1)} %add_convert_fusion.summed), channel_id=1, source_target_pairs={{4,8},{8,4},{12,16},{16,12},{20,24},{24,20},{5,9},{9,5},{13,17},{1... | collective-permute-start | bytes 221192 | tf_op jit(solution)/shard_map/ppermute | solution.py:248
  33.4 2.0 %collective-permute-start.7 = (bf16[144,256]{1,0:T(8,128)(2,1)S(1)}, bf16[144,256]{1,0:T(8,128)(2,1)S(1)}, u32[]{:S(2)}, u32[]{:S(2)}) collective-permute-start(bf16[144,256]{1,0:T(8,128)(2,1)S(1)} %add_convert_fusion.summed), channel_id=1, source_target_pairs={{0,4},{4,0},{8,12},{12,8},{16,20},{20,16},{24,28},{28,24},{1,5},{5... | collective-permute-start | bytes 221192 | tf_op jit(solution)/shard_map/ppermute | solution.py:248

commit v7 on v6

--- a/solution.py
+++ b/solution.py
@@ -16,7 +16,7 @@
 VMEM = pl.BlockSpec(memory_space=pltpu.VMEM)
 LANES = 128
 ORDER = (0, 1, 2, 3)
-PEERS = (2, 1, 3)
+PEERS = (1, 2, 3)
 
 
 def mm(a, b):
@@ -91,31 +91,39 @@
     return copies
 
 
-def halo_kernel(nl, nt, lists, o0, o1, o2, o3, nl_v, nt_v, lists_v, sems, *, order):
+def halo_kernel(nl, nt, lists, o0, o1, o2, nl_v, nt_v, lists_v, sems):
     for copy in fetch([(lists, lists_v), (nl, nl_v), (nt, nt_v)], sems):
         copy.wait()
     slots = nl.shape[0]
     paired = jnp.concatenate([nl_v[...], nt_v[...]], 1)
     even = (lax.rem(lax.axis_index("dom"), 2) == 0, lax.rem(lax.axis_index("grp"), 2) == 0)
-    for k, out in zip(order, (o0, o1, o2, o3)):
+    rim = o0.shape[0]
+    for k, (out, at) in enumerate(((o0, 0), (o1, 0), (o2, 0), (o2, rim))):
         base = k // 2 * 2
         up = even[k // 2] if k % 2 == 0 else jnp.logical_not(even[k // 2])
         row = jnp.where(up, lists_v[0, base : base + 1, :], lists_v[0, base + 1 : base + 2, :])
         selector = jnp.concatenate(picks(column(row), slots), 1)
-        out[...] = mm(selector, paired).astype(BF)
-
-
-def local_kernel(nl, nt, src, tgt, ef, pre_o, table, *, block):
+        out[at : at + rim, :] = mm(selector, paired).astype(BF)
+
+
+def receiver_kernel(nl, nt, tgt, ef, pre_o, table, *, block):
     slots, width = nl.shape
     paired = jnp.concatenate([nl[...], nt[...]], 1)
-    table[0:slots, :] = mm(paired, twice(ef[width : 2 * width, :])).astype(BF)
-    table[slots:, :] = mm(paired, twice(ef[2 * width :, :])).astype(BF)
+    table[...] = mm(paired, twice(ef[2 * width :, :])).astype(BF)
     for begin in range(0, pre_o.shape[0], block):
         at = slice(begin, begin + block)
-        selector = jnp.concatenate(
-            picks(column(src[0:1, at]), slots) + picks(column(tgt[0:1, at]), slots), 1
-        )
+        selector = jnp.concatenate(picks(column(tgt[0:1, at]), slots), 1)
         pre_o[at, :] = mm(selector, table[...])
+
+
+def sender_kernel(nl, nt, src, ef, pre, pre_o, table, *, block):
+    slots, width = nl.shape
+    paired = jnp.concatenate([nl[...], nt[...]], 1)
+    table[...] = mm(paired, twice(ef[width : 2 * width, :])).astype(BF)
+    for begin in range(0, pre_o.shape[0], block):
+        at = slice(begin, begin + block)
+        selector = jnp.concatenate(picks(column(src[0:1, at]), slots), 1)
+        pre_o[at, :] = pre[at, :] + mm(selector, table[...])
 
 
 def edge_kernel(nl_v, nt_v, ed_v, src_v, tgt_v, own_v, sources_v, ef_v, es_v, nf_v, ns_v, nc, ec,
@@ -128,7 +136,11 @@
     for k, got in zip(order, (h0, h1, h2, h3)):
         place = k // 2 * 2 + (odd[k // 2] if k % 2 else 1 - odd[k // 2])
         at = pl.ds(pl.multiple_of(place * rim, rim), rim)
-        table[at, :] = mm(got[...], weight).astype(BF)
+        rows_in = got[0:rim, :]
+        if k == 3:
+            g = lax.axis_index("grp")
+            rows_in = jnp.where((g == 0) | (g == lax.axis_size("grp") - 1), jnp.zeros_like(rows_in), rows_in)
+        table[at, :] = mm(rows_in, weight).astype(BF)
     second = twice(centred(es_v[...]))
     ones = averaging(width)
     own_weight = ef_v[0:width, :]
@@ -273,28 +285,48 @@
     shape = jax.ShapeDtypeStruct
     dma = pltpu.SemaphoreType.DMA
     *sent, nl, nt = pl.pallas_call(
-        functools.partial(halo_kernel, order=ORDER),
-        out_shape=[pltpu.VMEM((rim, 2 * width), BF)] * 4 + like(nl, nt),
+        halo_kernel,
+        out_shape=[pltpu.VMEM((k * rim, 2 * width), BF) for k in (1, 1, 2)] + like(nl, nt),
         in_specs=[HBM] * 3,
-        out_specs=[VMEM] * 6,
+        out_specs=[VMEM] * 5,
         scratch_shapes=like(lists) + [dma((3,))],
         compiler_params=params(),
         cost_estimate=pl.CostEstimate(flops=8 * edges * slots * width, bytes_accessed=4 * slots * width, transcendentals=0),
         name="halo_rows",
     )(*(pltpu.with_memory_space_constraint(x, pltpu.HBM) for x in (nl, nt, lists)))
-    got = [swap(x, ("dom", "grp")[k // 2], k % 2) for k, x in zip(ORDER, sent)]
+    got = [swap(sent[0], "dom", 0), swap(sent[1], "dom", 1)]
+    half_cost = pl.CostEstimate(
+        flops=4 * edges * slots * width, bytes_accessed=8 * edges * width, transcendentals=0
+    )
     pre = pl.pallas_call(
-        functools.partial(local_kernel, block=cut),
+        functools.partial(receiver_kernel, block=cut),
+        out_shape=shape((edges, 2 * width), F32),
+        in_specs=[VMEM] * 4,
+        out_specs=VMEM,
+        scratch_shapes=[pltpu.VMEM((slots, 2 * width), BF)],
+        compiler_params=params(),
+        cost_estimate=half_cost,
+        name="receivers",
+    )(nl, nt, tgt, ef)
+    if lax.axis_size("grp") == 4:
+        near = swap(sent[2], "grp", 0)
+        (*got, near), pre = lax.optimization_barrier(((*got, near), pre))
+        far = lax.ppermute(near[rim:], "grp", [(i, i ^ 2) for i in range(4)])
+    else:
+        near, far = swap(sent[2][:rim], "grp", 0), swap(sent[2][rim:], "grp", 1)
+    got += [near, far]
+    pre = pl.pallas_call(
+        functools.partial(sender_kernel, block=cut),
         out_shape=shape((edges, 2 * width), F32),
         in_specs=[VMEM] * 5,
         out_specs=VMEM,
-        scratch_shapes=[pltpu.VMEM((2 * slots, 2 * width), BF)],
-        compiler_params=params(),
-        cost_estimate=pl.CostEstimate(
-            flops=8 * edges * slots * width, bytes_accessed=8 * edges * width, transcendentals=0
-        ),
-        name="local",
-    )(nl, nt, src, tgt, ef)
+        scratch_shapes=[pltpu.VMEM((slots, 2 * width), BF)],
+        input_output_aliases={4: 0},
+        compiler_params=params(),
+        cost_estimate=half_cost,
+        name="senders",
+    )(nl, nt, src, ef, pre)
+    (nc, ec), pre = lax.optimization_barrier(((nc, ec), pre))
     first, part = pl.pallas_call(
         functools.partial(edge_kernel, block=min(edges, 2048), rows=256, order=ORDER),
         out_shape=[shape((slots, 2 * width), BF), shape((row_nodes + extra, 2 * width), BF)],

time: 38.8 us -> 38.6 us (level); the launches traced: 38.2 us -> 38.4 us
  starting transfers between devices: 16.2 us -> 15.3 us
  Pallas kernels: 16.3 us -> 16.9 us
  waiting for transfers between devices: 3.31 us -> 3.84 us
    ppermute x3, starting transfers between devices: 4.92 us -> 2.71 us  [row_sum(): got.append(lax.ppermute(x, 'grp', pairs))]
    ppermute x0 -> x1, starting transfers between devices: none -> 1.3 us  [per_device(): far = lax.ppermute(near[rim:], 'grp', [(i, i ^ 2) for i in range(4)])]
    pallas_call x2 -> x3, Pallas kernels: 6.37 us -> 6.97 us  [the longest x1 2.81 us: per_device(): pl.pallas_call(functools.partial(sender_kernel, block=cut), out_shape=sha...]
    ppermute x3, waiting for transfers between devices: 1.85 us -> 2.31 us  [row_sum(): got.append(lax.ppermute(x, 'grp', pairs))]
    ppermute x6 -> x5, starting transfers between devices: 11.2 us -> 11.3 us  [swap(): return lax.ppermute(x, axis, pairs)]
    ppermute x6 -> x5, waiting for transfers between devices: 1.46 us -> 1.53 us  [swap(): return lax.ppermute(x, axis, pairs)]
  transfers between devices with their start and end apart: 9 -> 9, of which waited for: 3 -> 3; matrix products, arithmetic and copies ran while one was open for 0% -> 0% of each run, Pallas kernels for 15% -> 16%
where the time goes in v7:
time: 38.6 us; the launch traced here: 38.4 us
  Pallas kernels  16.9 us (44%)
  starting transfers between devices  15.3 us (40%)
  waiting for transfers between devices  3.84 us (10%)
  between operations  2.25 us (6%)
    ppermute x5, starting transfers between devices, swap(): return lax.ppermute(x, axis, pairs)  11.3 us
    pallas_call x1, Pallas kernels, per_device(): pl.pallas_call(functools.partial(edge_kernel, block=min(edges, 2048), row...  6.35 us
    pallas_call x1, Pallas kernels, per_device(): pl.pallas_call(functools.partial(sender_kernel, block=cut), out_shape=sha...  2.81 us
    ppermute x3, starting transfers between devices, row_sum(): got.append(lax.ppermute(x, 'grp', pairs))  2.71 us
    pallas_call x1, Pallas kernels, per_device(): pl.pallas_call(functools.partial(coarse_kernel, fan=fan), out_shape=[shap...  2.71 us
    pallas_call x1, Pallas kernels, per_device(): pl.pallas_call(functools.partial(receiver_kernel, block=cut), out_shape=s...  2.55 us
    ppermute x3, waiting for transfers between devices, row_sum(): got.append(lax.ppermute(x, 'grp', pairs))  2.31 us
    pallas_call x1, Pallas kernels, per_device(): pl.pallas_call(halo_kernel, out_shape=[pltpu.VMEM((k * rim, 2 * width), B...  1.61 us
  transfers between devices with their start and end apart: 9, of which 3 were waited for; matrix products, arithmetic and copies ran while one was open for 0% of the time, Pallas kernels for 16%

profile of v7, /device:TPU:1, one launch (start us, length us, event | category | flops | bytes accessed | tf_op | source)
XLA Modules:
  0.0 38.4 jit_solution(4282504951379643916)
XLA Ops:
  0.6 0.0 copy-start.12
  0.6 0.0 copy-start.1
  0.7 1.6 %halo_rows.1 = (bf16[128,256]{1,0:T(8,128)(2,1)S(1)}, bf16[128,256]{1,0:T(8,128)(2,1)S(1)}, bf16[256,256]{1,0:T(8,128)(2,1)S(1)}, bf16[1024,128]{1,0:T(8,128)(2,1)S(1)}, bf16[1024,128]{1,0:T(8,128)(2,1)S(1)}) custom-call(bf16[1024,128]{1,0:T(8,128)(2,1)} %nl.1, bf16[1024,128]{1,0:T(8,128)(2,1)} %nt.1, s32[1,4,128]{2,1,0:T(4,128)} %lists.1), custom_call_target="tpu_custom_call" | custom-call | flops 4294967296 | bytes 524288 | tf_op jit(solution)/shard_map/halo_rows/pallas_call | solution.py:287
  2.3 0.0 copy-start.3
  2.3 2.1 %collective-permute-start.2 = (bf16[256,256]{1,0:T(8,128)(2,1)S(1)}, bf16[256,256]{1,0:T(8,128)(2,1)S(1)}, u32[]{:S(2)}, u32[]{:S(2)}) collective-permute-start(bf16[256,256]{1,0:T(8,128)(2,1)S(1)} %get-tuple-element.32), channel_id=1, source_target_pairs={{0,1},{1,0},{2,3},{3,2},{4,5},{5,4},{6,7},{7,6},{8,9},{9,8},{10,11... | collective-permute-start | bytes 393224 | tf_op jit(solution)/shard_map/ppermute | solution.py:260
  4.4 1.0 %collective-permute-start = (bf16[128,256]{1,0:T(8,128)(2,1)S(1)}, bf16[128,256]{1,0:T(8,128)(2,1)S(1)}, u32[]{:S(2)}, u32[]{:S(2)}) collective-permute-start(bf16[128,256]{1,0:T(8,128)(2,1)S(1)} %get-tuple-element.30), channel_id=1, source_target_pairs={{0,4},{4,0},{8,12},{12,8},{16,20},{20,16},{24,28},{28,24},{1,5},{5... | collective-permute-start | bytes 196616 | tf_op jit(solution)/shard_map/ppermute | solution.py:260
  5.3 3.1 %collective-permute-start.1 = (bf16[128,256]{1,0:T(8,128)(2,1)S(1)}, bf16[128,256]{1,0:T(8,128)(2,1)S(1)}, u32[]{:S(2)}, u32[]{:S(2)}) collective-permute-start(bf16[128,256]{1,0:T(8,128)(2,1)S(1)} %get-tuple-element.31), channel_id=1, source_target_pairs={{4,8},{8,4},{12,16},{16,12},{20,24},{24,20},{5,9},{9,5},{13,17},{1... | collective-permute-start | bytes 196616 | tf_op jit(solution)/shard_map/ppermute | solution.py:260
  8.4 0.0 copy-done.12
  8.4 0.0 copy-done.1
  8.4 2.6 %receivers.1.pre = f32[4096,256]{1,0:T(8,128)S(1)} custom-call(bf16[1024,128]{1,0:T(8,128)(2,1)S(1)} %get-tuple-element.28.nl.nl_v, bf16[1024,128]{1,0:T(8,128)(2,1)S(1)} %get-tuple-element.29.nt.nt_v, s32[1,4096]{1,0:T(1,128)S(1)} %copy-done.12, bf16[384,128]{1,0:T(8,128)(2,1)S(1)} %copy-done.1), custom_call_target="tpu_custom_call" | custom-call | flops 2147483648 | bytes 4194304 | tf_op jit(solution)/shard_map/receivers/pallas_call | solution.py:301
  12.3 0.0 collective-permute-done.h0
  12.3 0.0 collective-permute-done.1.h1
  12.3 0.0 collective-permute-done.2.h2
  12.4 0.0 copy-start
  12.4 0.0 copy-start.2
  12.4 0.0 copy-start.7
  12.4 0.0 copy-start.8
  12.4 0.0 copy-start.13
  12.4 0.0 copy-start.14
  12.4 1.3 %collective-permute-start.3 = (bf16[128,256]{1,0:T(8,128)(2,1)S(1)}, bf16[128,256]{1,0:T(8,128)(2,1)S(1)}, u32[]{:S(2)}, u32[]{:S(2)}) collective-permute-start(bf16[128,256]{1,0:T(8,128)(2,1)S(1)} %slice.3), channel_id=1, source_target_pairs={{0,2},{1,3},{2,0},{3,1},{4,6},{5,7},{6,4},{7,5},{8,10},{9,11},{10,... | collective-permute-start | bytes 196616 | tf_op jit(solution)/shard_map/ppermute | solution.py:314
  13.7 0.0 copy-done.3
  13.7 2.8 %senders.1.pre = f32[4096,256]{1,0:T(8,128)S(1)} custom-call(bf16[1024,128]{1,0:T(8,128)(2,1)S(1)} %get-tuple-element.28.nl.nl_v, bf16[1024,128]{1,0:T(8,128)(2,1)S(1)} %get-tuple-element.29.nt.nt_v, s32[1,4096]{1,0:T(1,128)S(1)} %copy-done.3, bf16[384,128]{1,0:T(8,128)(2,1)S(1)} %copy-done.1, ...), custom_call_target="tpu_custom_call", output_to_operand_aliasing={{}: (4, {})} | custom-call | flops 2147483648 | bytes 4194304 | tf_op jit(solution)/shard_map/senders/pallas_call | solution.py:318
  16.5 0.0 copy-start.4
  16.6 0.0 copy-start.5
  16.6 0.0 copy-start.6
  16.6 0.0 copy-start.9
  16.6 0.0 copy-start.10
  16.6 0.0 copy-start.11
  16.6 0.0 collective-permute-done.3.h3
  16.6 0.0 copy-done
  16.6 0.0 copy-done.2
  16.6 0.0 copy-done.7
  16.7 0.0 copy-done.8
  16.7 0.0 copy-done.13
  16.7 6.4 %edges.1 = (bf16[1024,256]{1,0:T(8,128)(2,1)S(1)}, bf16[144,256]{1,0:T(8,128)(2,1)S(1)}) custom-call(bf16[1024,128]{1,0:T(8,128)(2,1)S(1)} %get-tuple-element.28.nl.nl_v, bf16[1024,128]{1,0:T(8,128)(2,1)S(1)} %get-tuple-element.29.nt.nt_v, bf16[4096,128]{1,0:T(8,128)(2,1)S(1)} %copy-done, s32[1,4096]{1,0:T(1,128)S(1)} %copy-done.3, ...), custom_call_target="tpu_custom_call" | custom-call | tf_op jit(solution)/shard_map/edges/pallas_call | solution.py:330
  23.1 0.3 collective-permute-start.4
  23.4 0.2 collective-permute-start.5
  23.6 2.2 %collective-permute-start.6 = (bf16[144,256]{1,0:T(8,128)(2,1)S(1)}, bf16[144,256]{1,0:T(8,128)(2,1)S(1)}, u32[]{:S(2)}, u32[]{:S(2)}) collective-permute-start(bf16[144,256]{1,0:T(8,128)(2,1)S(1)} %get-tuple-element.40), channel_id=1, source_target_pairs={{0,3},{1,2},{2,1},{3,0},{4,7},{5,6},{6,5},{7,4},{8,11},{9,10},{10,... | collective-permute-start | bytes 221192 | tf_op jit(solution)/shard_map/ppermute | solution.py:271
  25.8 0.3 prepare.1
  26.1 0.9 %collective-permute-done.4 = bf16[144,256]{1,0:T(8,128)(2,1)S(1)} collective-permute-done((bf16[144,256]{1,0:T(8,128)(2,1)S(1)}, bf16[144,256]{1,0:T(8,128)(2,1)S(1)}, u32[]{:S(2)}, u32[]{:S(2)}) %collective-permute-start.4) | collective-permute-done | bytes 73760 | tf_op jit(solution)/shard_map/ppermute | solution.py:271
  27.1 0.0 collective-permute-done.5
  27.1 1.4 %collective-permute-done.6 = bf16[144,256]{1,0:T(8,128)(2,1)S(1)} collective-permute-done((bf16[144,256]{1,0:T(8,128)(2,1)S(1)}, bf16[144,256]{1,0:T(8,128)(2,1)S(1)}, u32[]{:S(2)}, u32[]{:S(2)}) %collective-permute-start.6) | collective-permute-done | bytes 73760 | tf_op jit(solution)/shard_map/ppermute | solution.py:271
  28.5 0.5 %collective-permute-start.7 = (bf16[144,256]{1,0:T(8,128)(2,1)S(1)}, bf16[144,256]{1,0:T(8,128)(2,1)S(1)}, u32[]{:S(2)}, u32[]{:S(2)}) collective-permute-start(bf16[144,256]{1,0:T(8,128)(2,1)S(1)} %add_convert_fusion.summed), channel_id=1, source_target_pairs={{0,4},{4,0},{8,12},{12,8},{16,20},{20,16},{24,28},{28,24},{1,5},{5... | collective-permute-start | bytes 221192 | tf_op jit(solution)/shard_map/ppermute | solution.py:260
  28.9 4.7 %collective-permute-start.8 = (bf16[144,256]{1,0:T(8,128)(2,1)S(1)}, bf16[144,256]{1,0:T(8,128)(2,1)S(1)}, u32[]{:S(2)}, u32[]{:S(2)}) collective-permute-start(bf16[144,256]{1,0:T(8,128)(2,1)S(1)} %add_convert_fusion.summed), channel_id=1, source_target_pairs={{4,8},{8,4},{12,16},{16,12},{20,24},{24,20},{5,9},{9,5},{13,17},{1... | collective-permute-start | bytes 221192 | tf_op jit(solution)/shard_map/ppermute | solution.py:260
  33.7 0.5 %own_row.1 = (f32[1024,256]{1,0:T(8,128)S(1)}, bf16[1024,256]{1,0:T(8,128)(2,1)S(1)}, f32[128,256]{1,0:T(8,128)S(1)}) custom-call(bf16[144,256]{1,0:T(8,128)(2,1)S(1)} %add_convert_fusion.summed, bf16[1792,256]{1,0:T(8,128)(2,1)S(1)} %get-tuple-element.48.weights), custom_call_target="tpu_custom_call" | custom-call | flops 67108864 | bytes 4194304 | tf_op jit(solution)/shard_map/own_row/pallas_call | solution.py:360
  34.2 0.0 collective-permute-done.7.v0
  34.2 1.5 %collective-permute-done.8.v1 = bf16[144,256]{1,0:T(8,128)(2,1)S(1)} collective-permute-done((bf16[144,256]{1,0:T(8,128)(2,1)S(1)}, bf16[144,256]{1,0:T(8,128)(2,1)S(1)}, u32[]{:S(2)}, u32[]{:S(2)}) %collective-permute-start.8) | collective-permute-done | bytes 73760 | tf_op jit(solution)/shard_map/ppermute | solution.py:260
  35.7 2.7 %coarse.1 = (bf16[1024,128]{1,0:T(8,128)(2,1)}, bf16[1024,128]{1,0:T(8,128)(2,1)}) custom-call(bf16[144,256]{1,0:T(8,128)(2,1)S(1)} %collective-permute-done.7.v0, bf16[144,256]{1,0:T(8,128)(2,1)S(1)} %collective-permute-done.8.v1, f32[1024,256]{1,0:T(8,128)S(1)} %get-tuple-element.49.given, bf16[1024,256]{1,0:T(8,128)(2,1)S(1)} %get-tuple-element.50.outer, ...), custom_call_target="tpu_custom_call" | custom-call | tf_op jit(solution)/shard_map/coarse/pallas_call | solution.py:377
  (9 shorter events, 0.1 us)
Async XLA Ops:
  0.6 7.8 %copy-start.12 = (s32[1,4096]{1,0:T(1,128)S(1)}, s32[1,4096]{1,0:T(1,128)}, u32[]{:S(2)}) copy-start(s32[1,4096]{1,0:T(1,128)} %tgt_v.1) | copy-start | bytes 49156
  0.6 7.8 %copy-start.1 = (bf16[384,128]{1,0:T(8,128)(2,1)S(1)}, bf16[384,128]{1,0:T(8,128)(2,1)}, u32[]{:S(2)}) copy-start(bf16[384,128]{1,0:T(8,128)(2,1)} %ef_v.1) | copy-start | bytes 294916
  2.3 11.5 %copy-start.3 = (s32[1,4096]{1,0:T(1,128)S(1)}, s32[1,4096]{1,0:T(1,128)}, u32[]{:S(2)}) copy-start(s32[1,4096]{1,0:T(1,128)} %src_v.1) | copy-start | bytes 49156
  2.3 10.0 %collective-permute-start.2 = (bf16[256,256]{1,0:T(8,128)(2,1)S(1)}, bf16[256,256]{1,0:T(8,128)(2,1)S(1)}, u32[]{:S(2)}, u32[]{:S(2)}) collective-permute-start(bf16[256,256]{1,0:T(8,128)(2,1)S(1)} %get-tuple-element.32), channel_id=1, source_target_pairs={{0,1},{1,0},{2,3},{3,2},{4,5},{5,4},{6,7},{7,6},{8,9},{9,8},{10,11... | collective-permute-start | bytes 393224 | tf_op jit(solution)/shard_map/ppermute | solution.py:260
  4.4 7.9 %collective-permute-start = (bf16[128,256]{1,0:T(8,128)(2,1)S(1)}, bf16[128,256]{1,0:T(8,128)(2,1)S(1)}, u32[]{:S(2)}, u32[]{:S(2)}) collective-permute-start(bf16[128,256]{1,0:T(8,128)(2,1)S(1)} %get-tuple-element.30), channel_id=1, source_target_pairs={{0,4},{4,0},{8,12},{12,8},{16,20},{20,16},{24,28},{28,24},{1,5},{5... | collective-permute-start | bytes 196616 | tf_op jit(solution)/shard_map/ppermute | solution.py:260
  5.3 7.0 %collective-permute-start.1 = (bf16[128,256]{1,0:T(8,128)(2,1)S(1)}, bf16[128,256]{1,0:T(8,128)(2,1)S(1)}, u32[]{:S(2)}, u32[]{:S(2)}) collective-permute-start(bf16[128,256]{1,0:T(8,128)(2,1)S(1)} %get-tuple-element.31), channel_id=1, source_target_pairs={{4,8},{8,4},{12,16},{16,12},{20,24},{24,20},{5,9},{9,5},{13,17},{1... | collective-permute-start | bytes 196616 | tf_op jit(solution)/shard_map/ppermute | solution.py:260
  12.4 4.3 %copy-start = (bf16[4096,128]{1,0:T(8,128)(2,1)S(1)}, bf16[4096,128]{1,0:T(8,128)(2,1)}, u32[]{:S(2)}) copy-start(bf16[4096,128]{1,0:T(8,128)(2,1)} %ed_v.1) | copy-start | bytes 3145732
  12.4 4.3 %copy-start.2 = (bf16[256,128]{1,0:T(8,128)(2,1)S(1)}, bf16[256,128]{1,0:T(8,128)(2,1)}, u32[]{:S(2)}) copy-start(bf16[256,128]{1,0:T(8,128)(2,1)} %nf_v.1) | copy-start | bytes 196612
  12.4 4.3 %copy-start.7 = (bf16[128,128]{1,0:T(8,128)(2,1)S(1)}, bf16[128,128]{1,0:T(8,128)(2,1)}, u32[]{:S(2)}) copy-start(bf16[128,128]{1,0:T(8,128)(2,1)} %es_v.1) | copy-start | bytes 98308
  12.4 4.3 %copy-start.8 = (bf16[128,128]{1,0:T(8,128)(2,1)S(1)}, bf16[128,128]{1,0:T(8,128)(2,1)}, u32[]{:S(2)}) copy-start(bf16[128,128]{1,0:T(8,128)(2,1)} %ns_v.1) | copy-start | bytes 98308
  12.4 4.3 %copy-start.13 = (s32[1,1024]{1,0:T(1,128)S(1)}, s32[1,1024]{1,0:T(1,128)}, u32[]{:S(2)}) copy-start(s32[1,1024]{1,0:T(1,128)} %own.1) | copy-start | bytes 12292
  12.4 4.3 %copy-start.14 = (s32[32,8]{0,1:T(8,128)S(1)}, s32[32,8]{0,1:T(8,128)}, u32[]{:S(2)}) copy-start(s32[32,8]{0,1:T(8,128)} %param.29) | copy-start | bytes 3076
  12.4 4.2 %collective-permute-start.3 = (bf16[128,256]{1,0:T(8,128)(2,1)S(1)}, bf16[128,256]{1,0:T(8,128)(2,1)S(1)}, u32[]{:S(2)}, u32[]{:S(2)}) collective-permute-start(bf16[128,256]{1,0:T(8,128)(2,1)S(1)} %slice.3), channel_id=1, source_target_pairs={{0,2},{1,3},{2,0},{3,1},{4,6},{5,7},{6,4},{7,5},{8,10},{9,11},{10,... | collective-permute-start | bytes 196616 | tf_op jit(solution)/shard_map/ppermute | solution.py:314
  16.5 9.2 %copy-start.4 = (bf16[256,128]{1,0:T(8,128)(2,1)S(1)}, bf16[256,128]{1,0:T(8,128)(2,1)}, u32[]{:S(2)}) copy-start(bf16[256,128]{1,0:T(8,128)(2,1)} %mf.1) | copy-start | bytes 196612
  16.6 9.2 %copy-start.5 = (bf16[256,128]{1,0:T(8,128)(2,1)S(1)}, bf16[256,128]{1,0:T(8,128)(2,1)}, u32[]{:S(2)}) copy-start(bf16[256,128]{1,0:T(8,128)(2,1)} %cf.1) | copy-start | bytes 196612
  16.6 9.2 %copy-start.6 = (bf16[256,128]{1,0:T(8,128)(2,1)S(1)}, bf16[256,128]{1,0:T(8,128)(2,1)}, u32[]{:S(2)}) copy-start(bf16[256,128]{1,0:T(8,128)(2,1)} %pf.1) | copy-start | bytes 196612
  16.6 9.2 %copy-start.9 = (bf16[128,128]{1,0:T(8,128)(2,1)S(1)}, bf16[128,128]{1,0:T(8,128)(2,1)}, u32[]{:S(2)}) copy-start(bf16[128,128]{1,0:T(8,128)(2,1)} %ms.1) | copy-start | bytes 98308
  16.6 9.2 %copy-start.10 = (bf16[128,128]{1,0:T(8,128)(2,1)S(1)}, bf16[128,128]{1,0:T(8,128)(2,1)}, u32[]{:S(2)}) copy-start(bf16[128,128]{1,0:T(8,128)(2,1)} %cs.1) | copy-start | bytes 98308
  16.6 9.2 %copy-start.11 = (bf16[128,128]{1,0:T(8,128)(2,1)S(1)}, bf16[128,128]{1,0:T(8,128)(2,1)}, u32[]{:S(2)}) copy-start(bf16[128,128]{1,0:T(8,128)(2,1)} %ps.1) | copy-start | bytes 98308
  23.1 4.0 %collective-permute-start.4 = (bf16[144,256]{1,0:T(8,128)(2,1)S(1)}, bf16[144,256]{1,0:T(8,128)(2,1)S(1)}, u32[]{:S(2)}, u32[]{:S(2)}) collective-permute-start(bf16[144,256]{1,0:T(8,128)(2,1)S(1)} %get-tuple-element.40), channel_id=1, source_target_pairs={{0,1},{1,0},{2,3},{3,2},{4,5},{5,4},{6,7},{7,6},{8,9},{9,8},{10,11... | collective-permute-start | bytes 221192 | tf_op jit(solution)/shard_map/ppermute | solution.py:271
  23.4 3.7 %collective-permute-start.5 = (bf16[144,256]{1,0:T(8,128)(2,1)S(1)}, bf16[144,256]{1,0:T(8,128)(2,1)S(1)}, u32[]{:S(2)}, u32[]{:S(2)}) collective-permute-start(bf16[144,256]{1,0:T(8,128)(2,1)S(1)} %get-tuple-element.40), channel_id=1, source_target_pairs={{0,2},{1,3},{2,0},{3,1},{4,6},{5,7},{6,4},{7,5},{8,10},{9,11},{10,... | collective-permute-start | bytes 221192 | tf_op jit(solution)/shard_map/ppermute | solution.py:271
  23.6 4.8 %collective-permute-start.6 = (bf16[144,256]{1,0:T(8,128)(2,1)S(1)}, bf16[144,256]{1,0:T(8,128)(2,1)S(1)}, u32[]{:S(2)}, u32[]{:S(2)}) collective-permute-start(bf16[144,256]{1,0:T(8,128)(2,1)S(1)} %get-tuple-element.40), channel_id=1, source_target_pairs={{0,3},{1,2},{2,1},{3,0},{4,7},{5,6},{6,5},{7,4},{8,11},{9,10},{10,... | collective-permute-start | bytes 221192 | tf_op jit(solution)/shard_map/ppermute | solution.py:271
  28.5 5.7 %collective-permute-start.7 = (bf16[144,256]{1,0:T(8,128)(2,1)S(1)}, bf16[144,256]{1,0:T(8,128)(2,1)S(1)}, u32[]{:S(2)}, u32[]{:S(2)}) collective-permute-start(bf16[144,256]{1,0:T(8,128)(2,1)S(1)} %add_convert_fusion.summed), channel_id=1, source_target_pairs={{0,4},{4,0},{8,12},{12,8},{16,20},{20,16},{24,28},{28,24},{1,5},{5... | collective-permute-start | bytes 221192 | tf_op jit(solution)/shard_map/ppermute | solution.py:260
  28.9 6.7 %collective-permute-start.8 = (bf16[144,256]{1,0:T(8,128)(2,1)S(1)}, bf16[144,256]{1,0:T(8,128)(2,1)S(1)}, u32[]{:S(2)}, u32[]{:S(2)}) collective-permute-start(bf16[144,256]{1,0:T(8,128)(2,1)S(1)} %add_convert_fusion.summed), channel_id=1, source_target_pairs={{4,8},{8,4},{12,16},{16,12},{20,24},{24,20},{5,9},{9,5},{13,17},{1... | collective-permute-start | bytes 221192 | tf_op jit(solution)/shard_map/ppermute | solution.py:260

commit v8 on v7

--- a/solution.py
+++ b/solution.py
@@ -356,7 +356,8 @@
         name="prepare",
     )(first, own, mf, ms, cf, cs, pf, ps)
     summed, (weights, fixed, owner) = row_sum(part, (weights, fixed, owner))
-    v1, v0 = swap(summed, "dom", 1), swap(summed, "dom", 0)
+    rows_sum = summed[:row_nodes]
+    v1, v0 = swap(rows_sum, "dom", 1), swap(rows_sum, "dom", 0)
     given, outer, mine = pl.pallas_call(
         functools.partial(own_row_kernel, fan=fan),
         out_shape=[

time: 38.6 us -> 38.5 us (level)
  no operation moved by 1% of the time
where the time goes in v8:
time: 38.5 us; the launch traced here: 38.3 us
  Pallas kernels  16.8 us (44%)
  starting transfers between devices  15.3 us (40%)
  waiting for transfers between devices  3.76 us (10%)
  between operations  2.26 us (6%)
    ppermute x5, starting transfers between devices, swap(): return lax.ppermute(x, axis, pairs)  11.3 us
    pallas_call x1, Pallas kernels, per_device(): pl.pallas_call(functools.partial(edge_kernel, block=min(edges, 2048), row...  6.35 us
    pallas_call x1, Pallas kernels, per_device(): pl.pallas_call(functools.partial(sender_kernel, block=cut), out_shape=sha...  2.81 us
    ppermute x3, starting transfers between devices, row_sum(): got.append(lax.ppermute(x, 'grp', pairs))  2.71 us
    pallas_call x1, Pallas kernels, per_device(): pl.pallas_call(functools.partial(coarse_kernel, fan=fan), out_shape=[shap...  2.71 us
    pallas_call x1, Pallas kernels, per_device(): pl.pallas_call(functools.partial(receiver_kernel, block=cut), out_shape=s...  2.55 us
    ppermute x3, waiting for transfers between devices, row_sum(): got.append(lax.ppermute(x, 'grp', pairs))  2.31 us
    pallas_call x1, Pallas kernels, per_device(): pl.pallas_call(halo_kernel, out_shape=[pltpu.VMEM((k * rim, 2 * width), B...  1.61 us
  transfers between devices with their start and end apart: 9, of which 3 were waited for; matrix products, arithmetic and copies ran while one was open for 0% of the time, Pallas kernels for 16%

profile of v8, /device:TPU:1, one launch (start us, length us, event | category | flops | bytes accessed | tf_op | source)
XLA Modules:
  0.0 38.3 jit_solution(8943193687749873499)
XLA Ops:
  0.6 0.0 copy-start.12
  0.6 0.0 copy-start.1
  0.7 1.6 %halo_rows.1 = (bf16[128,256]{1,0:T(8,128)(2,1)S(1)}, bf16[128,256]{1,0:T(8,128)(2,1)S(1)}, bf16[256,256]{1,0:T(8,128)(2,1)S(1)}, bf16[1024,128]{1,0:T(8,128)(2,1)S(1)}, bf16[1024,128]{1,0:T(8,128)(2,1)S(1)}) custom-call(bf16[1024,128]{1,0:T(8,128)(2,1)} %nl.1, bf16[1024,128]{1,0:T(8,128)(2,1)} %nt.1, s32[1,4,128]{2,1,0:T(4,128)} %lists.1), custom_call_target="tpu_custom_call" | custom-call | flops 4294967296 | bytes 524288 | tf_op jit(solution)/shard_map/halo_rows/pallas_call | solution.py:287
  2.3 0.0 copy-start.3
  2.3 2.1 %collective-permute-start.2 = (bf16[256,256]{1,0:T(8,128)(2,1)S(1)}, bf16[256,256]{1,0:T(8,128)(2,1)S(1)}, u32[]{:S(2)}, u32[]{:S(2)}) collective-permute-start(bf16[256,256]{1,0:T(8,128)(2,1)S(1)} %get-tuple-element.32), channel_id=1, source_target_pairs={{0,1},{1,0},{2,3},{3,2},{4,5},{5,4},{6,7},{7,6},{8,9},{9,8},{10,11... | collective-permute-start | bytes 393224 | tf_op jit(solution)/shard_map/ppermute | solution.py:260
  4.4 1.0 %collective-permute-start = (bf16[128,256]{1,0:T(8,128)(2,1)S(1)}, bf16[128,256]{1,0:T(8,128)(2,1)S(1)}, u32[]{:S(2)}, u32[]{:S(2)}) collective-permute-start(bf16[128,256]{1,0:T(8,128)(2,1)S(1)} %get-tuple-element.30), channel_id=1, source_target_pairs={{0,4},{4,0},{8,12},{12,8},{16,20},{20,16},{24,28},{28,24},{1,5},{5... | collective-permute-start | bytes 196616 | tf_op jit(solution)/shard_map/ppermute | solution.py:260
  5.3 3.1 %collective-permute-start.1 = (bf16[128,256]{1,0:T(8,128)(2,1)S(1)}, bf16[128,256]{1,0:T(8,128)(2,1)S(1)}, u32[]{:S(2)}, u32[]{:S(2)}) collective-permute-start(bf16[128,256]{1,0:T(8,128)(2,1)S(1)} %get-tuple-element.31), channel_id=1, source_target_pairs={{4,8},{8,4},{12,16},{16,12},{20,24},{24,20},{5,9},{9,5},{13,17},{1... | collective-permute-start | bytes 196616 | tf_op jit(solution)/shard_map/ppermute | solution.py:260
  8.4 0.0 copy-done.12
  8.4 0.0 copy-done.1
  8.4 2.6 %receivers.1.pre = f32[4096,256]{1,0:T(8,128)S(1)} custom-call(bf16[1024,128]{1,0:T(8,128)(2,1)S(1)} %get-tuple-element.28.nl.nl_v, bf16[1024,128]{1,0:T(8,128)(2,1)S(1)} %get-tuple-element.29.nt.nt_v, s32[1,4096]{1,0:T(1,128)S(1)} %copy-done.12, bf16[384,128]{1,0:T(8,128)(2,1)S(1)} %copy-done.1), custom_call_target="tpu_custom_call" | custom-call | flops 2147483648 | bytes 4194304 | tf_op jit(solution)/shard_map/receivers/pallas_call | solution.py:301
  12.3 0.0 collective-permute-done.h0
  12.3 0.0 collective-permute-done.1.h1
  12.3 0.0 collective-permute-done.2.h2
  12.4 0.0 copy-start
  12.4 0.0 copy-start.2
  12.4 0.0 copy-start.7
  12.4 0.0 copy-start.8
  12.4 0.0 copy-start.13
  12.4 0.0 copy-start.14
  12.4 1.3 %collective-permute-start.3 = (bf16[128,256]{1,0:T(8,128)(2,1)S(1)}, bf16[128,256]{1,0:T(8,128)(2,1)S(1)}, u32[]{:S(2)}, u32[]{:S(2)}) collective-permute-start(bf16[128,256]{1,0:T(8,128)(2,1)S(1)} %slice.6), channel_id=1, source_target_pairs={{0,2},{1,3},{2,0},{3,1},{4,6},{5,7},{6,4},{7,5},{8,10},{9,11},{10,... | collective-permute-start | bytes 196616 | tf_op jit(solution)/shard_map/ppermute | solution.py:314
  13.7 0.0 copy-done.3
  13.7 2.8 %senders.1.pre = f32[4096,256]{1,0:T(8,128)S(1)} custom-call(bf16[1024,128]{1,0:T(8,128)(2,1)S(1)} %get-tuple-element.28.nl.nl_v, bf16[1024,128]{1,0:T(8,128)(2,1)S(1)} %get-tuple-element.29.nt.nt_v, s32[1,4096]{1,0:T(1,128)S(1)} %copy-done.3, bf16[384,128]{1,0:T(8,128)(2,1)S(1)} %copy-done.1, ...), custom_call_target="tpu_custom_call", output_to_operand_aliasing={{}: (4, {})} | custom-call | flops 2147483648 | bytes 4194304 | tf_op jit(solution)/shard_map/senders/pallas_call | solution.py:318
  16.5 0.0 copy-start.4
  16.6 0.0 copy-start.5
  16.6 0.0 copy-start.6
  16.6 0.0 copy-start.9
  16.6 0.0 copy-start.10
  16.6 0.0 copy-start.11
  16.6 0.0 collective-permute-done.3.h3
  16.6 0.0 copy-done
  16.6 0.0 copy-done.2
  16.6 0.0 copy-done.7
  16.7 0.0 copy-done.8
  16.7 6.4 %edges.1 = (bf16[1024,256]{1,0:T(8,128)(2,1)S(1)}, bf16[144,256]{1,0:T(8,128)(2,1)S(1)}) custom-call(bf16[1024,128]{1,0:T(8,128)(2,1)S(1)} %get-tuple-element.28.nl.nl_v, bf16[1024,128]{1,0:T(8,128)(2,1)S(1)} %get-tuple-element.29.nt.nt_v, bf16[4096,128]{1,0:T(8,128)(2,1)S(1)} %copy-done, s32[1,4096]{1,0:T(1,128)S(1)} %copy-done.3, ...), custom_call_target="tpu_custom_call" | custom-call | tf_op jit(solution)/shard_map/edges/pallas_call | solution.py:330
  23.1 0.3 collective-permute-start.4
  23.4 0.2 collective-permute-start.5
  23.6 2.2 %collective-permute-start.6 = (bf16[144,256]{1,0:T(8,128)(2,1)S(1)}, bf16[144,256]{1,0:T(8,128)(2,1)S(1)}, u32[]{:S(2)}, u32[]{:S(2)}) collective-permute-start(bf16[144,256]{1,0:T(8,128)(2,1)S(1)} %get-tuple-element.40), channel_id=1, source_target_pairs={{0,3},{1,2},{2,1},{3,0},{4,7},{5,6},{6,5},{7,4},{8,11},{9,10},{10,... | collective-permute-start | bytes 221192 | tf_op jit(solution)/shard_map/ppermute | solution.py:271
  25.8 0.0 copy-done.5
  25.8 0.3 prepare.1
  26.1 0.9 %collective-permute-done.4 = bf16[144,256]{1,0:T(8,128)(2,1)S(1)} collective-permute-done((bf16[144,256]{1,0:T(8,128)(2,1)S(1)}, bf16[144,256]{1,0:T(8,128)(2,1)S(1)}, u32[]{:S(2)}, u32[]{:S(2)}) %collective-permute-start.4) | collective-permute-done | bytes 73760 | tf_op jit(solution)/shard_map/ppermute | solution.py:271
  27.1 0.0 collective-permute-done.5
  27.1 1.4 %collective-permute-done.6 = bf16[144,256]{1,0:T(8,128)(2,1)S(1)} collective-permute-done((bf16[144,256]{1,0:T(8,128)(2,1)S(1)}, bf16[144,256]{1,0:T(8,128)(2,1)S(1)}, u32[]{:S(2)}, u32[]{:S(2)}) %collective-permute-start.6) | collective-permute-done | bytes 73760 | tf_op jit(solution)/shard_map/ppermute | solution.py:271
  28.5 0.5 %collective-permute-start.7 = (bf16[128,256]{1,0:T(8,128)(2,1)S(1)}, bf16[128,256]{1,0:T(8,128)(2,1)S(1)}, u32[]{:S(2)}, u32[]{:S(2)}) collective-permute-start(bf16[128,256]{1,0:T(8,128)(2,1)S(1)} %slice.8), channel_id=1, source_target_pairs={{0,4},{4,0},{8,12},{12,8},{16,20},{20,16},{24,28},{28,24},{1,5},{5... | collective-permute-start | bytes 196616 | tf_op jit(solution)/shard_map/ppermute | solution.py:260
  29.0 4.7 %collective-permute-start.8 = (bf16[128,256]{1,0:T(8,128)(2,1)S(1)}, bf16[128,256]{1,0:T(8,128)(2,1)S(1)}, u32[]{:S(2)}, u32[]{:S(2)}) collective-permute-start(bf16[128,256]{1,0:T(8,128)(2,1)S(1)} %slice.8), channel_id=1, source_target_pairs={{4,8},{8,4},{12,16},{16,12},{20,24},{24,20},{5,9},{9,5},{13,17},{1... | collective-permute-start | bytes 196616 | tf_op jit(solution)/shard_map/ppermute | solution.py:260
  33.7 0.5 %own_row.1 = (f32[1024,256]{1,0:T(8,128)S(1)}, bf16[1024,256]{1,0:T(8,128)(2,1)S(1)}, f32[128,256]{1,0:T(8,128)S(1)}) custom-call(bf16[144,256]{1,0:T(8,128)(2,1)S(1)} %add_convert_fusion.summed, bf16[1792,256]{1,0:T(8,128)(2,1)S(1)} %get-tuple-element.48.weights), custom_call_target="tpu_custom_call" | custom-call | flops 67108864 | bytes 4194304 | tf_op jit(solution)/shard_map/own_row/pallas_call | solution.py:361
  34.2 0.0 collective-permute-done.7.v0
  34.2 1.4 %collective-permute-done.8.v1 = bf16[128,256]{1,0:T(8,128)(2,1)S(1)} collective-permute-done((bf16[128,256]{1,0:T(8,128)(2,1)S(1)}, bf16[128,256]{1,0:T(8,128)(2,1)S(1)}, u32[]{:S(2)}, u32[]{:S(2)}) %collective-permute-start.8) | collective-permute-done | bytes 65568 | tf_op jit(solution)/shard_map/ppermute | solution.py:260
  35.6 2.7 %coarse.1 = (bf16[1024,128]{1,0:T(8,128)(2,1)}, bf16[1024,128]{1,0:T(8,128)(2,1)}) custom-call(bf16[128,256]{1,0:T(8,128)(2,1)S(1)} %collective-permute-done.7.v0, bf16[128,256]{1,0:T(8,128)(2,1)S(1)} %collective-permute-done.8.v1, f32[1024,256]{1,0:T(8,128)S(1)} %get-tuple-element.49.given, bf16[1024,256]{1,0:T(8,128)(2,1)S(1)} %get-tuple-element.50.outer, ...), custom_call_target="tpu_custom_call" | custom-call | tf_op jit(solution)/shard_map/coarse/pallas_call | solution.py:378
  (10 shorter events, 0.1 us)
Async XLA Ops:
  0.6 7.8 %copy-start.12 = (s32[1,4096]{1,0:T(1,128)S(1)}, s32[1,4096]{1,0:T(1,128)}, u32[]{:S(2)}) copy-start(s32[1,4096]{1,0:T(1,128)} %tgt_v.1) | copy-start | bytes 49156
  0.6 7.8 %copy-start.1 = (bf16[384,128]{1,0:T(8,128)(2,1)S(1)}, bf16[384,128]{1,0:T(8,128)(2,1)}, u32[]{:S(2)}) copy-start(bf16[384,128]{1,0:T(8,128)(2,1)} %ef_v.1) | copy-start | bytes 294916
  2.3 11.5 %copy-start.3 = (s32[1,4096]{1,0:T(1,128)S(1)}, s32[1,4096]{1,0:T(1,128)}, u32[]{:S(2)}) copy-start(s32[1,4096]{1,0:T(1,128)} %src_v.1) | copy-start | bytes 49156
  2.3 10.0 %collective-permute-start.2 = (bf16[256,256]{1,0:T(8,128)(2,1)S(1)}, bf16[256,256]{1,0:T(8,128)(2,1)S(1)}, u32[]{:S(2)}, u32[]{:S(2)}) collective-permute-start(bf16[256,256]{1,0:T(8,128)(2,1)S(1)} %get-tuple-element.32), channel_id=1, source_target_pairs={{0,1},{1,0},{2,3},{3,2},{4,5},{5,4},{6,7},{7,6},{8,9},{9,8},{10,11... | collective-permute-start | bytes 393224 | tf_op jit(solution)/shard_map/ppermute | solution.py:260
  4.4 7.9 %collective-permute-start = (bf16[128,256]{1,0:T(8,128)(2,1)S(1)}, bf16[128,256]{1,0:T(8,128)(2,1)S(1)}, u32[]{:S(2)}, u32[]{:S(2)}) collective-permute-start(bf16[128,256]{1,0:T(8,128)(2,1)S(1)} %get-tuple-element.30), channel_id=1, source_target_pairs={{0,4},{4,0},{8,12},{12,8},{16,20},{20,16},{24,28},{28,24},{1,5},{5... | collective-permute-start | bytes 196616 | tf_op jit(solution)/shard_map/ppermute | solution.py:260
  5.3 7.0 %collective-permute-start.1 = (bf16[128,256]{1,0:T(8,128)(2,1)S(1)}, bf16[128,256]{1,0:T(8,128)(2,1)S(1)}, u32[]{:S(2)}, u32[]{:S(2)}) collective-permute-start(bf16[128,256]{1,0:T(8,128)(2,1)S(1)} %get-tuple-element.31), channel_id=1, source_target_pairs={{4,8},{8,4},{12,16},{16,12},{20,24},{24,20},{5,9},{9,5},{13,17},{1... | collective-permute-start | bytes 196616 | tf_op jit(solution)/shard_map/ppermute | solution.py:260
  12.4 4.3 %copy-start = (bf16[4096,128]{1,0:T(8,128)(2,1)S(1)}, bf16[4096,128]{1,0:T(8,128)(2,1)}, u32[]{:S(2)}) copy-start(bf16[4096,128]{1,0:T(8,128)(2,1)} %ed_v.1) | copy-start | bytes 3145732
  12.4 4.3 %copy-start.2 = (bf16[256,128]{1,0:T(8,128)(2,1)S(1)}, bf16[256,128]{1,0:T(8,128)(2,1)}, u32[]{:S(2)}) copy-start(bf16[256,128]{1,0:T(8,128)(2,1)} %nf_v.1) | copy-start | bytes 196612
  12.4 4.3 %copy-start.7 = (bf16[128,128]{1,0:T(8,128)(2,1)S(1)}, bf16[128,128]{1,0:T(8,128)(2,1)}, u32[]{:S(2)}) copy-start(bf16[128,128]{1,0:T(8,128)(2,1)} %es_v.1) | copy-start | bytes 98308
  12.4 4.3 %copy-start.8 = (bf16[128,128]{1,0:T(8,128)(2,1)S(1)}, bf16[128,128]{1,0:T(8,128)(2,1)}, u32[]{:S(2)}) copy-start(bf16[128,128]{1,0:T(8,128)(2,1)} %ns_v.1) | copy-start | bytes 98308
  12.4 4.3 %copy-start.13 = (s32[1,1024]{1,0:T(1,128)S(1)}, s32[1,1024]{1,0:T(1,128)}, u32[]{:S(2)}) copy-start(s32[1,1024]{1,0:T(1,128)} %own.1) | copy-start | bytes 12292
  12.4 4.3 %copy-start.14 = (s32[32,8]{0,1:T(8,128)S(1)}, s32[32,8]{0,1:T(8,128)}, u32[]{:S(2)}) copy-start(s32[32,8]{0,1:T(8,128)} %param.29) | copy-start | bytes 3076
  12.4 4.2 %collective-permute-start.3 = (bf16[128,256]{1,0:T(8,128)(2,1)S(1)}, bf16[128,256]{1,0:T(8,128)(2,1)S(1)}, u32[]{:S(2)}, u32[]{:S(2)}) collective-permute-start(bf16[128,256]{1,0:T(8,128)(2,1)S(1)} %slice.6), channel_id=1, source_target_pairs={{0,2},{1,3},{2,0},{3,1},{4,6},{5,7},{6,4},{7,5},{8,10},{9,11},{10,... | collective-permute-start | bytes 196616 | tf_op jit(solution)/shard_map/ppermute | solution.py:314
  16.5 9.2 %copy-start.4 = (bf16[256,128]{1,0:T(8,128)(2,1)S(1)}, bf16[256,128]{1,0:T(8,128)(2,1)}, u32[]{:S(2)}) copy-start(bf16[256,128]{1,0:T(8,128)(2,1)} %mf.1) | copy-start | bytes 196612
  16.6 9.2 %copy-start.5 = (bf16[256,128]{1,0:T(8,128)(2,1)S(1)}, bf16[256,128]{1,0:T(8,128)(2,1)}, u32[]{:S(2)}) copy-start(bf16[256,128]{1,0:T(8,128)(2,1)} %cf.1) | copy-start | bytes 196612
  16.6 9.2 %copy-start.6 = (bf16[256,128]{1,0:T(8,128)(2,1)S(1)}, bf16[256,128]{1,0:T(8,128)(2,1)}, u32[]{:S(2)}) copy-start(bf16[256,128]{1,0:T(8,128)(2,1)} %pf.1) | copy-start | bytes 196612
  16.6 9.2 %copy-start.9 = (bf16[128,128]{1,0:T(8,128)(2,1)S(1)}, bf16[128,128]{1,0:T(8,128)(2,1)}, u32[]{:S(2)}) copy-start(bf16[128,128]{1,0:T(8,128)(2,1)} %ms.1) | copy-start | bytes 98308
  16.6 9.2 %copy-start.10 = (bf16[128,128]{1,0:T(8,128)(2,1)S(1)}, bf16[128,128]{1,0:T(8,128)(2,1)}, u32[]{:S(2)}) copy-start(bf16[128,128]{1,0:T(8,128)(2,1)} %cs.1) | copy-start | bytes 98308
  16.6 9.2 %copy-start.11 = (bf16[128,128]{1,0:T(8,128)(2,1)S(1)}, bf16[128,128]{1,0:T(8,128)(2,1)}, u32[]{:S(2)}) copy-start(bf16[128,128]{1,0:T(8,128)(2,1)} %ps.1) | copy-start | bytes 98308
  23.1 4.0 %collective-permute-start.4 = (bf16[144,256]{1,0:T(8,128)(2,1)S(1)}, bf16[144,256]{1,0:T(8,128)(2,1)S(1)}, u32[]{:S(2)}, u32[]{:S(2)}) collective-permute-start(bf16[144,256]{1,0:T(8,128)(2,1)S(1)} %get-tuple-element.40), channel_id=1, source_target_pairs={{0,1},{1,0},{2,3},{3,2},{4,5},{5,4},{6,7},{7,6},{8,9},{9,8},{10,11... | collective-permute-start | bytes 221192 | tf_op jit(solution)/shard_map/ppermute | solution.py:271
  23.4 3.7 %collective-permute-start.5 = (bf16[144,256]{1,0:T(8,128)(2,1)S(1)}, bf16[144,256]{1,0:T(8,128)(2,1)S(1)}, u32[]{:S(2)}, u32[]{:S(2)}) collective-permute-start(bf16[144,256]{1,0:T(8,128)(2,1)S(1)} %get-tuple-element.40), channel_id=1, source_target_pairs={{0,2},{1,3},{2,0},{3,1},{4,6},{5,7},{6,4},{7,5},{8,10},{9,11},{10,... | collective-permute-start | bytes 221192 | tf_op jit(solution)/shard_map/ppermute | solution.py:271
  23.6 4.8 %collective-permute-start.6 = (bf16[144,256]{1,0:T(8,128)(2,1)S(1)}, bf16[144,256]{1,0:T(8,128)(2,1)S(1)}, u32[]{:S(2)}, u32[]{:S(2)}) collective-permute-start(bf16[144,256]{1,0:T(8,128)(2,1)S(1)} %get-tuple-element.40), channel_id=1, source_target_pairs={{0,3},{1,2},{2,1},{3,0},{4,7},{5,6},{6,5},{7,4},{8,11},{9,10},{10,... | collective-permute-start | bytes 221192 | tf_op jit(solution)/shard_map/ppermute | solution.py:271
  28.5 5.7 %collective-permute-start.7 = (bf16[128,256]{1,0:T(8,128)(2,1)S(1)}, bf16[128,256]{1,0:T(8,128)(2,1)S(1)}, u32[]{:S(2)}, u32[]{:S(2)}) collective-permute-start(bf16[128,256]{1,0:T(8,128)(2,1)S(1)} %slice.8), channel_id=1, source_target_pairs={{0,4},{4,0},{8,12},{12,8},{16,20},{20,16},{24,28},{28,24},{1,5},{5... | collective-permute-start | bytes 196616 | tf_op jit(solution)/shard_map/ppermute | solution.py:260
  29.0 6.7 %collective-permute-start.8 = (bf16[128,256]{1,0:T(8,128)(2,1)S(1)}, bf16[128,256]{1,0:T(8,128)(2,1)S(1)}, u32[]{:S(2)}, u32[]{:S(2)}) collective-permute-start(bf16[128,256]{1,0:T(8,128)(2,1)S(1)} %slice.8), channel_id=1, source_target_pairs={{4,8},{8,4},{12,16},{16,12},{20,24},{24,20},{5,9},{9,5},{13,17},{1... | collective-permute-start | bytes 196616 | tf_op jit(solution)/shard_map/ppermute | solution.py:260
